TPU v7x, 256 devices: a whole 4x4x8 slice. The times are simulated.
256 devices in a mesh: gx: 4 (over y), gy: 8 (over x, core), gz: 8 (over z).
Axes of the slice: x: 4, y: 4, z: 8, core: 2. Of those that a mesh axis runs over, the one named last changes fastest.
Arguments:
- populations: float32 [19, 128, 128, 512], P(None, 'gz', 'gy', 'gx'), may hold values from 0.25 to 21, as said below
- solute_state: float32 [7, 2048, 4096], P(None, ('gx', 'gy', 'gz')), may hold values from 0.05 to 3.9, as said below
- pore_mask: int32 [128, 128, 512], P('gz', 'gy', 'gx'), may hold values from 0 to 1, as said below
- block_slot: int32 [8, 8, 32], P('gz', 'gy', 'gx'), may hold values from -1 to 63, as said below
- slot_block: int32 [2048], P(('gx', 'gy', 'gz')), may hold values from -1 to 63, as said below
Outputs:
- new_populations: float32 [19, 128, 128, 512], P(None, 'gz', 'gy', 'gx')
- new_solute: float32 [7, 2048, 4096], P(None, ('gx', 'gy', 'gz'))
Inputs may be any that keep to these rules, and one draw needn't show every extreme that they name: pore_mask is 1 only inside blocks listed in block_slot. `block_slot`: in each column of fixed gx and gy, the listed blocks are numbered k = 0, 1, ... in order of the gz index and then of the x block within the device; block k sits in owner k % 8 (index along gz within the same column), slot k // 8. Every device lists 1 to 8 blocks and in every column some device lists all 8, so one device hands 1 block to some owner. `slot_block`: the inverse of block_slot: an owner's filled slots come first, in increasing k. `populations`: Positive. `solute_state`: Positive.
All inputs are finite; a program needn't handle non-finite values.
Results may differ from a plain program's by a relative error of at most 0.0001.
Values sent between devices are 32-bit elements; how exact they have to be, the bound alone decides.
No kernel may reach another device: no remote copies, remote signals or barrier semaphores. Data moves between devices by JAX's collectives and lax.ppermute only.
A program may use at most 192 MiB of HBM per device.

v0:
```python
import functools

import jax
import jax.numpy as jnp
from jax import lax
from jax.experimental import pallas as pl
from jax.experimental.pallas import tpu as pltpu
from jax.sharding import PartitionSpec as P

STEPS = 4
DIRS = [
    (0, 0, 0),
    (1, 0, 0),
    (-1, 0, 0),
    (0, 1, 0),
    (0, -1, 0),
    (0, 0, 1),
    (0, 0, -1),
    (1, 1, 0),
    (-1, -1, 0),
    (1, -1, 0),
    (-1, 1, 0),
    (1, 0, 1),
    (-1, 0, -1),
    (1, 0, -1),
    (-1, 0, 1),
    (0, 1, 1),
    (0, -1, -1),
    (0, 1, -1),
    (0, -1, 1),
]
OPP = [DIRS.index((-a, -b, -c)) for a, b, c in DIRS]
PAIRS = [(i, OPP[i]) for i in range(1, 19, 2)]
WEIGHTS = [1.0 / 3.0] + [1.0 / 18.0] * 6 + [1.0 / 36.0] * 12
OMEGA_FLOW = 1.2
FORCE_GAIN = 0.02
REST_CONC = 8.0
Y_UP = [i for i in range(19) if DIRS[i][1] == 1]
Y_DN = [i for i in range(19) if DIRS[i][1] == -1]
Z_UP = [i for i in range(19) if DIRS[i][2] == 1]
Z_DN = [i for i in range(19) if DIRS[i][2] == -1]
RHO, VEL, PART, NORM, TRANS, FIELDS = 5, 6, 9, 10, 11, 12
SLABS = FIELDS + 2
B = 16
L = 128
W = 8
PLANE = 2 * B
ROWS = B * PLANE
PADDED = 64
PADROWS = (B + 2) * PADDED
BLOCKROWS = 7 * 32 * 8
F32 = jnp.float32
VMEM = pl.BlockSpec(memory_space=pltpu.VMEM)
SMEM = pl.BlockSpec(memory_space=pltpu.SMEM)


def call(kernel, out_shape, in_specs, scratch, flops, nbytes, limit=48):
    return pl.pallas_call(
        kernel,
        out_shape=out_shape,
        in_specs=in_specs,
        out_specs=jax.tree.map(lambda _: VMEM, out_shape),
        scratch_shapes=scratch,
        compiler_params=pltpu.CompilerParams(vmem_limit_bytes=limit * 1024 * 1024),
        cost_estimate=pl.CostEstimate(flops=flops, bytes_accessed=nbytes, transcendentals=0),
    )


def shape(*dims):
    return jax.ShapeDtypeStruct(dims, F32)


def lanes(rows):
    return lax.broadcasted_iota(jnp.int32, (rows, L), 1)


def row_ids(rows):
    return lax.broadcasted_iota(jnp.int32, (rows, L), 0)


def ring(v, step):
    rolled = pltpu.roll(v, step % L, axis=1)
    other = jnp.concatenate([rolled[B:], rolled[:B]], axis=0)
    return jnp.where(lanes(PLANE) == (0 if step > 0 else L - 1), other, rolled)


def halves(main, side):
    return jnp.concatenate([main, side], axis=0)


def spread(main, side):
    return halves(jnp.broadcast_to(main, (B, L)), jnp.broadcast_to(side, (B, L)))


def shift_rows(v, step, fill):
    rolled = pltpu.roll(v, step % PLANE, axis=0)
    return jnp.where(row_ids(PLANE) % B == (0 if step > 0 else B - 1), fill, rolled)


def is_open(bits, which):
    return (bits & (1 << which)) != 0


def along(which, vx, vy, vz):
    total = None
    for sign, part in zip(DIRS[which], (vx, vy, vz)):
        if sign != 0:
            if total is None:
                total = part if sign > 0 else -part
            else:
                total = total + part if sign > 0 else total - part
    return total


def moments(pops, porous):
    rho = pops[0]
    for which in range(1, 19):
        rho = rho + pops[which]
    scale = porous / rho
    parts = []
    for coord in range(3):
        plus = sum(pops[i] for i in range(19) if DIRS[i][coord] == 1)
        minus = sum(pops[i] for i in range(19) if DIRS[i][coord] == -1)
        parts.append((plus - minus) * scale)
    return rho, parts


def solute_collide(solute, velocity):
    conc = sum(solute)
    out = [-0.5 * solute[0] + 0.375 * conc]
    base = 0.1875 * conc
    for coord in range(3):
        turn = 0.75 * conc * velocity[coord]
        out.append((base - 0.5 * solute[1 + 2 * coord]) + turn)
        out.append((base - 0.5 * solute[2 + 2 * coord]) - turn)
    return out


def chosen(bits, moved, post, which):
    return jnp.where(
        is_open(bits, which),
        moved,
        jnp.where(is_open(bits, 0), post[OPP[which]], post[which]),
    )


def turn_blocks(x):
    row = row_ids(8)
    group = lanes(8) // B
    for bit in (1, 2, 4):
        up = pltpu.roll(pltpu.roll(x, 8 - bit, axis=0), B * bit, axis=1)
        down = up
        if bit != 4:
            down = pltpu.roll(pltpu.roll(x, bit, axis=0), L - B * bit, axis=1)
        low = (row & bit) == 0
        same = low == ((group & bit) == 0)
        x = jnp.where(same, x, jnp.where(low, up, down))
    return x


def gather_kernel(slot_ref, state_ref, send_ref):
    for dest in range(8):
        slot = jnp.int32(0)
        for s in range(8):
            home = slot_ref[s]
            slot = jnp.where((home >= 0) & (home // 8 == dest), s, slot)
        send_ref[dest] = state_ref[pl.ds(slot, BLOCKROWS // 8, stride=8), :]


def spread_kernel(slot_ref, recv_ref, dense_ref, low_ref, high_ref, turn_ref):
    for tile in range(8):
        owner = jnp.maximum(slot_ref[0, 0, tile], 0) // 8
        turn_ref[pl.ds(tile, BLOCKROWS // 8, stride=8), :] = recv_ref[owner]

    def body(group, carry):
        pack_columns(
            group,
            lambda at: turn_blocks(turn_ref[pl.ds(at, 8), :]),
            dense_ref,
            low_ref,
            high_ref,
        )
        return carry

    lax.fori_loop(0, BLOCKROWS // 128, body, 0)


def pack_columns(group, load, dense_ref, low_ref, high_ref):
    lane = lanes(8) // W
    low = jnp.zeros((8, L), F32)
    high = jnp.zeros((8, L), F32)
    for i in range(16):
        at = pl.multiple_of(group * 128 + i * 8, 8)
        x = load(at)
        if dense_ref is not None:
            dense_ref[pl.ds(at, 8), :] = x
        low = jnp.where(lane == i, x if i == 0 else pltpu.roll(x, W * i, axis=1), low)
        turn = (W + W * i) % L
        high = jnp.where(lane == i, x if turn == 0 else pltpu.roll(x, turn, axis=1), high)
    at = pl.multiple_of(group * 8, 8)
    low_ref[pl.ds(at, 8), :] = low
    high_ref[pl.ds(at, 8), :] = high


def unpack_columns(right, left, i):
    a = right if i == 0 else pltpu.roll(right, L - W * i, axis=1)
    b = left if i == 15 else pltpu.roll(left, L - W - W * i, axis=1)
    return jnp.where(lanes(8) < L // 2, a, b)


def columns_kernel(pops_ref, low_ref, high_ref):
    def body(group, carry):
        pack_columns(group, lambda at: pops_ref[pl.ds(at, 8), :], None, low_ref, high_ref)
        return carry

    lax.fori_loop(0, 19 * 2, body, 0)


def fill_ring(main_ref, right_ref, left_ref, out_ref, count):
    def body(group, carry):
        at = pl.multiple_of(group * 8, 8)
        right = right_ref[pl.ds(at, 8), :]
        left = left_ref[pl.ds(at, 8), :]
        comp = group // 2
        for i in range(16):
            z = (group % 2) * 8 + i // 2
            row = z * PLANE + (i % 2) * 8
            src = pl.multiple_of(group * 128 + i * 8, 8)
            out_ref[comp, pl.ds(pl.multiple_of(row, 8), 8), :] = main_ref[pl.ds(src, 8), :]
            out_ref[comp, pl.ds(pl.multiple_of(row + B, 8), 8), :] = unpack_columns(right, left, i)
        return carry

    lax.fori_loop(0, count * 2, body, 0)


def plane(ref, z, *lead):
    return ref[(*lead, pl.ds(pl.multiple_of(z * PLANE, PLANE), PLANE), slice(None))]


def padded_plane(ref, zz, shift, *lead):
    at = zz * PADDED + 8
    return halves(
        ref[(*lead, pl.ds(at - shift, B), slice(None))],
        ref[(*lead, pl.ds(at + 32 - shift, B), slice(None))],
    )


def put_padded(ref, comp, zz, v):
    at = zz * PADDED + 8
    if not isinstance(zz, int):
        at = pl.multiple_of(at, 8)
    ref[comp, pl.ds(at, B), :] = v[:B]
    ref[comp, pl.ds(at + 32, B), :] = v[B:]


def face_rows(ref, row, *lead):
    return halves(
        ref[(*lead, pl.ds(row, B, stride=PLANE), slice(None))],
        ref[(*lead, pl.ds(B + row, B, stride=PLANE), slice(None))],
    )


def start_kernel(pops_ref, right_ref, left_ref, mask_ref, out_ref, aux_ref, bits_ref, open_ref):
    fill_ring(pops_ref, right_ref, left_ref, out_ref, 19)

    def body(z, carry):
        here = padded_plane(mask_ref, z + 1, 0)
        bits = jnp.where(here > 0, 1, 0)
        for which in range(1, 19):
            cx, cy, cz = DIRS[which]
            source = padded_plane(mask_ref, z + 1 - cz, cy)
            if cx:
                source = ring(source, cx)
            bits = bits + jnp.where(source * here > 0, 1 << which, 0)
        bits_ref[pl.ds(pl.multiple_of(z * PLANE, PLANE), PLANE), :] = bits
        rho, velocity = moments([plane(out_ref, z, i) for i in range(19)], here)
        for k, v in enumerate([rho] + velocity):
            aux_ref[k, pl.ds(pl.multiple_of(z * PLANE, PLANE), PLANE), :] = v
        return carry

    lax.fori_loop(0, B, body, 0)
    row = row_ids(B)
    for tile in range(2):
        for side in range(2):
            edge = tile * 32 + (7, 24)[side]
            inner = tile * 32 + (8, 23)[side]
            halo = mask_ref[pl.ds(PADDED + edge, B, stride=PADDED), :]
            own = mask_ref[pl.ds(PADDED + inner, B, stride=PADDED), :]
            first = mask_ref[pl.ds(edge, 1), :]
            last = mask_ref[pl.ds(PADROWS - PADDED + edge, 1), :]
            trans = jnp.where(row == 0, halo * first, jnp.where(row == B - 1, halo * last, 0.0))
            put_open(open_ref, 0, side, tile, halo * own)
            put_open(open_ref, 1, side, tile, trans)
            zz = (0, B + 1)[side]
            near = (1, B)[side]
            at = zz * PADDED + tile * 32
            halo = mask_ref[pl.ds(at + 8, B), :]
            own = mask_ref[pl.ds(near * PADDED + tile * 32 + 8, B), :]
            first = mask_ref[pl.ds(at + 7, 1), :]
            last = mask_ref[pl.ds(at + 24, 1), :]
            trans = jnp.where(row == 0, halo * first, jnp.where(row == B - 1, halo * last, 0.0))
            put_open(open_ref, 2, side, tile, halo * own)
            put_open(open_ref, 3, side, tile, trans)


def open_at(kind, side, tile):
    return ((kind * 2 + side) * 2 + tile) * B


def put_open(ref, kind, side, tile, v):
    ref[pl.ds(open_at(kind, side, tile), B), :] = v


def get_open(ref, kind, side):
    return ref[pl.ds(open_at(kind, side, 0), PLANE), :] > 0


def write_message(out_ref, fields):
    lane = lanes(B) // 16
    for slab in range(2):
        packed = jnp.zeros((B, L), F32)
        for k in range(8):
            f = slab * 8 + k
            if f < FIELDS:
                turn = (W + 16 * k) % L
                packed = jnp.where(lane == k, pltpu.roll(fields[f][B:], turn, axis=1), packed)
        out_ref[pl.ds((FIELDS + slab) * B, B), :] = packed
    for f in range(FIELDS):
        out_ref[pl.ds(f * B, B), :] = fields[f][:B]


def read_field(ref, f):
    side = ref[pl.ds((FIELDS + f // 8) * B, B), :]
    return halves(ref[pl.ds(f * B, B), :], pltpu.roll(side, L - W - 16 * (f % 8), axis=1))


def read_row(ref, f, row):
    side = ref[pl.ds((FIELDS + f // 8) * B + row, 1), :]
    side = jnp.broadcast_to(side, (8, L))
    main = jnp.broadcast_to(ref[pl.ds(f * B + row, 1), :], (8, L))
    return main, pltpu.roll(side, L - W - 16 * (f % 8), axis=1)


def read_diag(ref, side, f):
    base = SLABS * B + side * SLABS
    main = jnp.broadcast_to(ref[pl.ds(base + f, 1), :], (8, L))
    packed = jnp.broadcast_to(ref[pl.ds(base + FIELDS + f // 8, 1), :], (8, L))
    return main, pltpu.roll(packed, L - W - 16 * (f % 8), axis=1)


def spread8(pair):
    return halves(
        jnp.concatenate([pair[0], pair[0]], axis=0), jnp.concatenate([pair[1], pair[1]], axis=0)
    )


def partial_sum(f, inner, bits, normal_up, in_rows):
    row = row_ids(PLANE) % B
    total = f[0]
    total = total + jnp.where(is_open(bits, 1), ring(f[1], 1), f[2])
    total = total + jnp.where(is_open(bits, 2), ring(f[2], -1), f[1])
    up, down = in_rows
    moved = jnp.where(row == 0, 0.0, pltpu.roll(f[up], 1, axis=0))
    total = total + jnp.where(is_open(bits, up), moved, f[down])
    moved = jnp.where(row == B - 1, 0.0, pltpu.roll(f[down], PLANE - 1, axis=0))
    total = total + jnp.where(is_open(bits, down), moved, f[up])
    outward, inward = normal_up
    total = total + jnp.where(is_open(bits, outward), inner, f[inward])
    total = total + jnp.where(is_open(bits, inward), 0.0, f[outward])
    return total


def write_messages(pops_ref, post_ref, aux_ref, bits_ref, y_refs, z_refs):
    row = row_ids(PLANE) % B
    for side in range(2):
        names = (Y_DN, Y_UP)[side]
        edge, inner = ((0, 1), (B - 1, B - 2))[side]
        normal = ((4, 3), (3, 4))[side]
        bits = face_rows(bits_ref, edge)
        f = [face_rows(post_ref, edge, i) for i in range(7)]
        part = partial_sum(f, face_rows(post_ref, inner, normal[0]), bits, normal, (5, 6))
        fields = [face_rows(pops_ref, edge, c) for c in names]
        fields += [face_rows(aux_ref, edge, k) for k in range(4)]
        fields += [part, f[normal[0]], jnp.where(row == 0, f[6], f[5])]
        write_message(y_refs[side], fields)
    for side in range(2):
        names = (Z_DN, Z_UP)[side]
        edge, inner = ((0, 1), (B - 1, B - 2))[side]
        normal = ((6, 5), (5, 6))[side]
        bits = plane(bits_ref, edge)
        f = [plane(post_ref, edge, i) for i in range(7)]
        part = partial_sum(f, plane(post_ref, inner, normal[0]), bits, normal, (3, 4))
        fields = [plane(pops_ref, edge, c) for c in names]
        fields += [plane(aux_ref, edge, k) for k in range(4)]
        fields += [part, f[normal[0]], jnp.where(row == 0, f[4], f[3])]
        write_message(z_refs[side], fields)


def relax(f, which, rho, vx, vy, vz, base):
    a = along(which, vx, vy, vz)
    scale = (OMEGA_FLOW * WEIGHTS[which]) * rho
    return (1.0 - OMEGA_FLOW) * f + scale * (base + a * (3.0 + 4.5 * a))


def lifted(conc, vx, vy, vz):
    vz = vz + FORCE_GAIN * (conc - REST_CONC)
    return vz, 1.0 - 1.5 * (vx * vx + vy * vy + vz * vz)


def stream_solute(z, post_ref, bits, ghost_ref, zghost):
    def fill(side):
        return spread(
            ghost_ref[pl.ds(side * PLANE + z, 1), :], ghost_ref[pl.ds(side * PLANE + B + z, 1), :]
        )

    post = [plane(post_ref, z, i) for i in range(7)]
    moved = [
        None,
        ring(post[1], 1),
        ring(post[2], -1),
        shift_rows(post[3], 1, fill(0)),
        shift_rows(post[4], -1, fill(1)),
        jnp.where(z == 0, zghost[0], plane(post_ref, jnp.maximum(z - 1, 0), 5)),
        jnp.where(z == B - 1, zghost[1], plane(post_ref, jnp.minimum(z + 1, B - 1), 6)),
    ]
    return [post[0]] + [chosen(bits, moved[i], post, i) for i in range(1, 7)]


def set_ghosts(ghost_ref, y_refs, z_refs):
    for side in range(2):
        ghost_ref[pl.ds(side * PLANE, PLANE), :] = read_field(y_refs[side], NORM)
        ghost_ref[pl.ds((2 + side) * PLANE, PLANE), :] = read_field(z_refs[side], NORM)


def collide_halos(post_ref, open_ref, y_refs, z_refs, flow_ref):
    row = row_ids(PLANE) % B
    for side in range(2):
        msg = y_refs[side]
        own = face_rows(post_ref, (0, B - 1)[side], (4, 3)[side])
        ends = jnp.where(
            row == 0,
            spread8(read_diag(z_refs[0], side, TRANS)),
            spread8(read_diag(z_refs[1], side, TRANS)),
        )
        conc = read_field(msg, PART)
        conc = conc + jnp.where(get_open(open_ref, 0, side), own, 0.0)
        conc = conc + jnp.where(get_open(open_ref, 1, side), ends, 0.0)
        rho, vx, vy, vz = (read_field(msg, k) for k in range(RHO, RHO + 4))
        vz, base = lifted(conc, vx, vy, vz)
        at = PADDED + (7, 24)[side]
        for k, which in enumerate((Y_UP, Y_DN)[side]):
            v = relax(read_field(msg, k), which, rho, vx, vy, vz, base)
            flow_ref[which, pl.ds(at, B, stride=PADDED), :] = v[:B]
            flow_ref[which, pl.ds(at + 32, B, stride=PADDED), :] = v[B:]
    for side in range(2):
        msg = z_refs[side]
        own = plane(post_ref, (0, B - 1)[side], (6, 5)[side])
        ends = jnp.where(
            row == 0, spread8(read_diag(msg, 0, NORM)), spread8(read_diag(msg, 1, NORM))
        )
        conc = read_field(msg, PART)
        conc = conc + jnp.where(get_open(open_ref, 2, side), own, 0.0)
        conc = conc + jnp.where(get_open(open_ref, 3, side), ends, 0.0)
        rho, vx, vy, vz = (read_field(msg, k) for k in range(RHO, RHO + 4))
        vz, base = lifted(conc, vx, vy, vz)
        for k, which in enumerate((Z_UP, Z_DN)[side]):
            v = relax(read_field(msg, k), which, rho, vx, vy, vz, base)
            put_padded(flow_ref, which, (0, B + 1)[side], v)
    for y_side in range(2):
        for z_side in range(2):
            which = DIRS.index((0, 1 - 2 * y_side, 1 - 2 * z_side))
            names = (Y_UP, Y_DN)[y_side]
            msg = z_refs[z_side]
            z_row = (0, B - 1)[z_side]
            y_row = (0, B - 1)[y_side]
            from_y = read_row(y_refs[y_side], TRANS, z_row)
            from_z = read_row(msg, TRANS, y_row)
            get = [read_diag(msg, y_side, f) for f in range(FIELDS)]
            for tile in range(2):
                open_y = open_ref[pl.ds(open_at(1, y_side, tile) + z_row, 1), :]
                open_z = open_ref[pl.ds(open_at(3, z_side, tile) + y_row, 1), :]
                conc = get[PART][tile]
                conc = conc + jnp.where(open_y > 0, from_y[tile], 0.0)
                conc = conc + jnp.where(open_z > 0, from_z[tile], 0.0)
                rho, vx, vy, vz = (get[k][tile] for k in range(RHO, RHO + 4))
                vz, base = lifted(conc, vx, vy, vz)
                v = relax(get[names.index(which)][tile], which, rho, vx, vy, vz, base)
                at = (0, B + 1)[z_side] * PADDED + tile * 32 + (7, 24)[y_side]
                flow_ref[which, pl.ds(at, 1), :] = v[:1]


def collide_flow(z, pops_ref, aux_ref, bits, conc, flow_ref):
    porous = jnp.where(is_open(bits, 0), 1.0, 0.0)
    rho, vx, vy, vz = (plane(aux_ref, z, k) for k in range(4))
    vz = vz + porous * (FORCE_GAIN * (conc - REST_CONC))
    base = 1.0 - 1.5 * (vx * vx + vy * vy + vz * vz)
    omega = OMEGA_FLOW * porous
    keep = 1.0 - omega
    scaled = omega * rho
    v = keep * plane(pops_ref, z, 0) + (WEIGHTS[0] * scaled) * base
    put_padded(flow_ref, 0, z + 1, v)
    for i, j in PAIRS:
        a = along(i, vx, vy, vz)
        scale = WEIGHTS[i] * scaled
        even = scale * (base + 4.5 * (a * a))
        odd = scale * (3.0 * a)
        put_padded(flow_ref, i, z + 1, keep * plane(pops_ref, z, i) + (even + odd))
        put_padded(flow_ref, j, z + 1, keep * plane(pops_ref, z, j) + (even - odd))


def stream_flow(z, bits, flow_ref):
    post = [padded_plane(flow_ref, z + 1, 0, i) for i in range(19)]
    out = [post[0]]
    for which in range(1, 19):
        cx, cy, cz = DIRS[which]
        moved = post[which]
        if cy or cz:
            moved = padded_plane(flow_ref, z + 1 - cz, cy, which)
        if cx:
            moved = ring(moved, cx)
        out.append(chosen(bits, moved, post, which))
    return out


def first_kernel(
    dense_ref, right_ref, left_ref, pops_ref, aux_ref, bits_ref,
    post_ref, ydn_ref, yup_ref, zdn_ref, zup_ref, solute_ref,
):
    fill_ring(dense_ref, right_ref, left_ref, solute_ref, 7)

    def body(z, carry):
        solute = [plane(solute_ref, z, i) for i in range(7)]
        post = solute_collide(solute, [plane(aux_ref, z, k) for k in range(1, 4)])
        for i in range(7):
            post_ref[i, pl.ds(pl.multiple_of(z * PLANE, PLANE), PLANE), :] = post[i]
        return carry

    lax.fori_loop(0, B, body, 0)
    write_messages(pops_ref, post_ref, aux_ref, bits_ref, (ydn_ref, yup_ref), (zdn_ref, zup_ref))


def step_kernel(
    pops_ref, post_ref, aux_ref, bits_ref, open_ref, ylo_ref, yhi_ref, zlo_ref, zhi_ref,
    pops_out, post_out, aux_out, ydn_ref, yup_ref, zdn_ref, zup_ref,
    flow_ref, solute_ref, ghost_ref,
):
    y_refs, z_refs = (ylo_ref, yhi_ref), (zlo_ref, zhi_ref)
    set_ghosts(ghost_ref, y_refs, z_refs)
    collide_halos(post_ref, open_ref, y_refs, z_refs, flow_ref)

    def first(z, carry):
        at = pl.ds(pl.multiple_of(z * PLANE, PLANE), PLANE)
        bits = bits_ref[at, :]
        zghost = [ghost_ref[pl.ds((2 + s) * PLANE, PLANE), :] for s in range(2)]
        solute = stream_solute(z, post_ref, bits, ghost_ref, zghost)
        for i in range(7):
            solute_ref[i, at, :] = solute[i]
        collide_flow(z, pops_ref, aux_ref, bits, sum(solute), flow_ref)
        return carry

    lax.fori_loop(0, B, first, 0)

    def second(z, carry):
        at = pl.ds(pl.multiple_of(z * PLANE, PLANE), PLANE)
        bits = bits_ref[at, :]
        pops = stream_flow(z, bits, flow_ref)
        for i in range(19):
            pops_out[i, at, :] = pops[i]
        rho, velocity = moments(pops, jnp.where(is_open(bits, 0), 1.0, 0.0))
        for k, v in enumerate([rho] + velocity):
            aux_out[k, at, :] = v
        post = solute_collide([solute_ref[i, at, :] for i in range(7)], velocity)
        for i in range(7):
            post_out[i, at, :] = post[i]
        return carry

    lax.fori_loop(0, B, second, 0)
    write_messages(pops_out, post_out, aux_out, bits_ref, (ydn_ref, yup_ref), (zdn_ref, zup_ref))


def last_solute_kernel(
    slot_ref, post_ref, bits_ref, ylo_ref, yhi_ref, zlo_ref, zhi_ref,
    send_ref, turn_ref, ghost_ref,
):
    set_ghosts(ghost_ref, (ylo_ref, yhi_ref), (zlo_ref, zhi_ref))

    def body(z, carry):
        bits = plane(bits_ref, z)
        zghost = [ghost_ref[pl.ds((2 + s) * PLANE, PLANE), :] for s in range(2)]
        solute = stream_solute(z, post_ref, bits, ghost_ref, zghost)
        for i in range(7):
            for half in range(2):
                at = pl.multiple_of(i * 256 + z * B + half * 8, 8)
                turn_ref[pl.ds(at, 8), :] = turn_blocks(solute[i][half * 8 : half * 8 + 8])
        return carry

    lax.fori_loop(0, B, body, 0)
    for owner in range(8):
        tile = jnp.int32(0)
        for j in range(8):
            slot = slot_ref[0, 0, j]
            tile = jnp.where((slot >= 0) & (slot // 8 == owner), j, tile)
        send_ref[owner] = turn_ref[pl.ds(tile, BLOCKROWS // 8, stride=8), :]


def last_flow_kernel(
    pops_ref, post_ref, aux_ref, bits_ref, open_ref, ylo_ref, yhi_ref, zlo_ref, zhi_ref,
    pops_out, flow_ref, ghost_ref,
):
    y_refs, z_refs = (ylo_ref, yhi_ref), (zlo_ref, zhi_ref)
    set_ghosts(ghost_ref, y_refs, z_refs)
    collide_halos(post_ref, open_ref, y_refs, z_refs, flow_ref)

    def first(z, carry):
        bits = plane(bits_ref, z)
        zghost = [ghost_ref[pl.ds((2 + s) * PLANE, PLANE), :] for s in range(2)]
        solute = stream_solute(z, post_ref, bits, ghost_ref, zghost)
        collide_flow(z, pops_ref, aux_ref, bits, sum(solute), flow_ref)
        return carry

    lax.fori_loop(0, B, first, 0)

    def second(z, carry):
        pops = stream_flow(z, plane(bits_ref, z), flow_ref)
        for i in range(19):
            pops_out[i, pl.ds(pl.multiple_of(z * B, B), B), :] = pops[i][:B]
        return carry

    lax.fori_loop(0, B, second, 0)


def scatter_kernel(slot_ref, recv_ref, out_ref):
    for s in range(8):
        home = slot_ref[s]
        block = recv_ref[jnp.maximum(home, 0) // 8]
        out_ref[pl.ds(s, BLOCKROWS // 8, stride=8), :] = jnp.where(home >= 0, block, 0.0)


def neighbours(low, high, axis):
    count = lax.axis_size(axis)
    up = [(i, (i + 1) % count) for i in range(count)]
    down = [(i, (i - 1) % count) for i in range(count)]
    return lax.ppermute(high, axis, up), lax.ppermute(low, axis, down)


def inside(axis):
    at = lax.axis_index(axis)
    return (at > 0).astype(F32), (at < lax.axis_size(axis) - 1).astype(F32)


def padded_mask(pore_mask):
    mask = pore_mask.astype(F32)
    left, right = neighbours(mask[:, :, :W], mask[:, :, L - W :], "gx")
    has_left, has_right = inside("gx")
    gap = jnp.zeros((B, B, L - 2 * W), F32)
    side = jnp.concatenate([right * has_right, gap, left * has_left], axis=2)
    cells = jnp.stack([mask, side], axis=1)
    low, high = neighbours(cells[:, :, :1], cells[:, :, B - 1 :], "gy")
    has_low, has_high = inside("gy")
    gap = jnp.zeros((B, 2, 7, L), F32)
    cells = jnp.concatenate([gap, low * has_low, cells, high * has_high, gap], axis=2)
    low, high = neighbours(cells[:1], cells[B - 1 :], "gz")
    has_low, has_high = inside("gz")
    cells = jnp.concatenate([low * has_low, cells, high * has_high], axis=0)
    return cells.reshape(PADROWS, L)


def exchange(ydn, yup, zdn, zup):
    ylo, yhi = neighbours(ydn, yup, "gy")

    def with_edges(face, row):
        lo = ylo.reshape(SLABS, B, L)[:, row]
        hi = yhi.reshape(SLABS, B, L)[:, row]
        return jnp.concatenate([face, lo, hi, jnp.zeros((4, L), F32)], axis=0)

    zlo, zhi = neighbours(with_edges(zdn, 0), with_edges(zup, B - 1), "gz")
    return ylo, yhi, zlo, zhi


def shards(populations, solute_state, pore_mask, block_slot, slot_block):
    message = shape(SLABS * B, L)
    state = solute_state.reshape(7, 8, 32, L).transpose(0, 2, 1, 3).reshape(BLOCKROWS, L)
    send = call(gather_kernel, shape(8, 224, L), [SMEM, VMEM], [], 1, 2 * 10**6)(slot_block, state)
    recv = lax.all_to_all(send, "gz", split_axis=0, concat_axis=0, tiled=True)
    flat = populations.reshape(19 * 256, L)
    low, high = call(columns_kernel, (shape(304, L),) * 2, [VMEM], [], 10**7, 3 * 10**6)(flat)
    left, right = neighbours(low, high, "gx")
    mask = padded_mask(pore_mask)
    pops, aux, bits, opens = call(
        start_kernel,
        (
            shape(19, ROWS, L),
            shape(4, ROWS, L),
            jax.ShapeDtypeStruct((ROWS, L), jnp.int32),
            shape(PLANE * 8, L),
        ),
        [VMEM] * 4,
        [],
        10**7,
        10**7,
    )(flat, right, left, mask)
    dense, low, high = call(
        spread_kernel,
        (shape(BLOCKROWS, L), shape(112, L), shape(112, L)),
        [SMEM, VMEM],
        [pltpu.VMEM((BLOCKROWS, L), F32)],
        10**7,
        2 * 10**6,
    )(block_slot, recv)
    left, right = neighbours(low, high, "gx")
    post, *faces = call(
        first_kernel,
        (shape(7, ROWS, L),) + (message,) * 4,
        [VMEM] * 6,
        [pltpu.VMEM((7, ROWS, L), F32)],
        10**7,
        10**7,
    )(dense, right, left, pops, aux, bits)
    scratch = [
        pltpu.VMEM((19, PADROWS, L), F32),
        pltpu.VMEM((7, ROWS, L), F32),
        pltpu.VMEM((4 * PLANE, L), F32),
    ]
    for step in range(STEPS - 1):
        halos = exchange(*faces)
        pops, post, aux, *faces = call(
            step_kernel,
            (shape(19, ROWS, L), shape(7, ROWS, L), shape(4, ROWS, L)) + (message,) * 4,
            [VMEM] * 9,
            scratch,
            10**8,
            2 * 10**7,
        )(pops, post, aux, bits, opens, *halos)
    halos = exchange(*faces)
    send = call(
        last_solute_kernel,
        shape(8, 224, L),
        [SMEM] + [VMEM] * 6,
        [pltpu.VMEM((BLOCKROWS, L), F32), scratch[2]],
        10**7,
        5 * 10**6,
    )(block_slot, post, bits, *halos)
    recv = lax.all_to_all(send, "gz", split_axis=0, concat_axis=0, tiled=True)
    pops = call(
        last_flow_kernel, shape(19, 256, L), [VMEM] * 9, [scratch[0], scratch[2]], 10**8, 2 * 10**7
    )(pops, post, aux, bits, opens, *halos)
    out = call(scatter_kernel, shape(BLOCKROWS, L), [SMEM, VMEM], [], 1, 2 * 10**6)(slot_block, recv)
    new_solute = out.reshape(7, 32, 8, L).transpose(0, 2, 1, 3).reshape(7, 8, 4096)
    return pops.reshape(19, B, B, L), new_solute


def solution(mesh):
    in_specs = (
        P(None, "gz", "gy", "gx"),
        P(None, ("gx", "gy", "gz"), None),
        P("gz", "gy", "gx"),
        P("gz", "gy", "gx"),
        P(("gx", "gy", "gz")),
    )
    out_specs = (P(None, "gz", "gy", "gx"), P(None, ("gx", "gy", "gz"), None))
    return jax.shard_map(shards, mesh=mesh, in_specs=in_specs, out_specs=out_specs, check_vma=False)
```

profile of v0, /device:TPU:7, one launch (start us, length us, event | category | flops | bytes accessed | tf_op | source)
XLA Modules:
  0.0 194.5 jit_solution(5016584214769903868)
XLA Ops:
  0.6 0.9 fusion.4
  1.6 0.8 fusion.3
  2.3 2.7 %collective-permute-start.2 = (f32[16,16,8]{2,1,0:T(8,128)}, f32[16,16,8]{2,1,0:T(8,128)}, u32[]{:S(2)}, u32[]{:S(2)}) collective-permute-start(f32[16,16,8]{2,1,0:T(8,128)} %get-tuple-element.76), channel_id=1, source_target_pairs={{0,192},{64,0},{128,64},{192,128},{1,193},{65,1},{129,65},{193,129... | collective-permute-start | bytes 24584 | tf_op jit(solution)/shard_map/ppermute | solution.py:643
  5.1 1.2 copy-done.8
  6.9 0.9 shard_map.70
  7.8 0.9 copy-done.1
  8.7 8.3 %all-to-all-start = ((f32[8,224,128]{2,1,0:T(8,128)}), f32[8,224,128]{2,1,0:T(8,128)S(1)}, u32[]{:S(2)}, u32[]{:S(2)}) async-start(f32[8,224,128]{2,1,0:T(8,128)} %copy-done.1), calls=%async_computation | async-start | bytes 1835008 | tf_op jit(solution)/shard_map/all_to_all | solution.py:684
  17.1 0.9 broadcast_multiply_fusion.1
  18.0 0.9 broadcast_multiply_fusion
  19.1 1.2 collective-permute-start.5
  20.3 0.7 pad_maximum_fusion.1
  21.1 1.7 collective-permute-start.4
  22.8 0.7 collective-permute-done.5
  24.7 4.5 %concatenate.34 = f32[16,2,32,128]{3,2,0,1:T(8,128)} concatenate(f32[16,2,7,128]{3,2,0,1:T(8,128)S(1)} %broadcast_in_dim.6, f32[16,2,1,128]{3,2,0,1:T(1,128)} %bitcast.88, f32[16,2,16,128]{3,2,0,1:T(8,128)} %pad_maximum_fusion.1, f32[16,2,1,128]{3,2,0,1:T(1,128)} %bitcast.87, f32[16,2,7,128]{3,2,0,1:T(8,128)S(1)} %broadcast_in_dim.6), dimensions={2} | concatenate | bytes 1048576 | tf_op jit(solution)/shard_map/concatenate | solution.py:661
  29.2 0.8 fusion.2
  30.0 1.5 collective-permute-start.6
  31.4 4.5 %shard_map.68 = (f32[304,128]{1,0:T(8,128)}, f32[304,128]{1,0:T(8,128)}) custom-call(f32[4864,128]{1,0:T(8,128)S(1)} %bitcast.73), custom_call_target="tpu_custom_call" | custom-call | flops 10000000 | bytes 3000000 | tf_op jit(solution)/shard_map/pallas_call | solution.py:686
  36.0 2.7 %collective-permute-start = (f32[304,128]{1,0:T(8,128)}, f32[304,128]{1,0:T(8,128)}, u32[]{:S(2)}, u32[]{:S(2)}) collective-permute-start(f32[304,128]{1,0:T(8,128)} %get-tuple-element.37), channel_id=1, source_target_pairs={{0,192},{64,0},{128,64},{192,128},{1,193},{65,1},{129,65},{193,129... | collective-permute-start | bytes 466952 | tf_op jit(solution)/shard_map/ppermute | solution.py:643
  38.6 1.5 collective-permute-start.7
  40.2 1.6 collective-permute-done.7
  41.8 1.3 all-to-all-done.recv_ref
  43.1 5.2 %shard_map.71 = (f32[1792,128]{1,0:T(8,128)S(1)}, f32[112,128]{1,0:T(8,128)S(1)}, f32[112,128]{1,0:T(8,128)S(1)}) custom-call(s32[1,1,8]{2,1,0:T(1,128)S(1)} %copy-done.9, f32[8,224,128]{2,1,0:T(8,128)S(1)} %all-to-all-done.recv_ref), custom_call_target="tpu_custom_call" | custom-call | flops 10000000 | bytes 2000000 | tf_op jit(solution)/shard_map/pallas_call | solution.py:702
  48.2 2.5 %collective-permute-start.8 = (f32[112,128]{1,0:T(8,128)S(1)}, f32[112,128]{1,0:T(8,128)S(1)}, u32[]{:S(2)}, u32[]{:S(2)}) collective-permute-start(f32[112,128]{1,0:T(8,128)S(1)} %get-tuple-element.41), channel_id=1, source_target_pairs={{0,192},{64,0},{128,64},{192,128},{1,193},{65,1},{129,65},{193,129... | collective-permute-start | bytes 172040 | tf_op jit(solution)/shard_map/ppermute | solution.py:643
  50.7 1.1 pad_maximum_fusion
  51.9 8.9 %shard_map.69 = (f32[19,512,128]{2,1,0:T(8,128)}, f32[4,512,128]{2,1,0:T(8,128)S(1)}, s32[512,128]{1,0:T(8,128)S(1)}, f32[256,128]{1,0:T(8,128)S(1)}) custom-call(f32[4864,128]{1,0:T(8,128)S(1)} %bitcast.74, f32[304,128]{1,0:T(8,128)} %collective-permute-done.right_ref, f32[304,128]{1,0:T(8,128)} %collective-permute-done.1.left_ref, f32[1152,128]{1,0:T(8,128)S(1)} %bitcast.75), custom_call_target="tpu_custom_call" | custom-call | flops 10000000 | bytes 10000000 | tf_op jit(solution)/shard_map/pallas_call | solution.py:689
  60.8 4.7 %shard_map.72 = (f32[7,512,128]{2,1,0:T(8,128)S(1)}, f32[224,128]{1,0:T(8,128)S(1)}, f32[224,128]{1,0:T(8,128)S(1)}, f32[224,128]{1,0:T(8,128)S(1)}, f32[224,128]{1,0:T(8,128)S(1)}) custom-call(f32[1792,128]{1,0:T(8,128)S(1)} %get-tuple-element.40.dense_ref, f32[112,128]{1,0:T(8,128)S(1)} %collective-permute-done.8.right_ref, ...), custom_call_target="tpu_custom_call" | custom-call | flops 10000000 | bytes 10000000 | tf_op jit(solution)/shard_map/pallas_call | solution.py:711
  65.5 1.2 copy-done.3
  66.8 4.0 %collective-permute-start.10 = (f32[224,128]{1,0:T(8,128)S(1)}, f32[224,128]{1,0:T(8,128)S(1)}, u32[]{:S(2)}, u32[]{:S(2)}) collective-permute-start(f32[224,128]{1,0:T(8,128)S(1)} %get-tuple-element.47), channel_id=1, source_target_pairs={{0,8},{8,16},{16,24},{24,32},{32,40},{40,48},{48,56},{56,0},{1,9},... | collective-permute-start | bytes 344072 | tf_op jit(solution)/shard_map/ppermute | solution.py:643
  70.8 1.7 collective-permute-done.10.ylo_ref
  72.6 3.7 %collective-permute-done.11.yhi_ref = f32[224,128]{1,0:T(8,128)S(1)} collective-permute-done((f32[224,128]{1,0:T(8,128)S(1)}, f32[224,128]{1,0:T(8,128)S(1)}, u32[]{:S(2)}, u32[]{:S(2)}) %collective-permute-start.11) | collective-permute-done | bytes 114720 | tf_op jit(solution)/shard_map/ppermute | solution.py:643
  76.4 2.5 %collective-permute-start.13 = (f32[256,128]{1,0:T(8,128)S(1)}, f32[256,128]{1,0:T(8,128)S(1)}, u32[]{:S(2)}, u32[]{:S(2)}) collective-permute-start(f32[256,128]{1,0:T(8,128)S(1)} %get-tuple-element.102), channel_id=1, source_target_pairs={{0,7},{1,0},{2,1},{3,2},{4,3},{5,4},{6,5},{7,6},{8,15},{9,8},{10,9... | collective-permute-start | bytes 393224 | tf_op jit(solution)/shard_map/ppermute | solution.py:643
  78.9 1.9 collective-permute-done.13.zhi_ref
  80.9 3.1 %collective-permute-done.12.zlo_ref = f32[256,128]{1,0:T(8,128)S(1)} collective-permute-done((f32[256,128]{1,0:T(8,128)S(1)}, f32[256,128]{1,0:T(8,128)S(1)}, u32[]{:S(2)}, u32[]{:S(2)}) %collective-permute-start.12) | collective-permute-done | bytes 131104 | tf_op jit(solution)/shard_map/ppermute | solution.py:643
  83.9 10.2 %shard_map.73 = (f32[19,512,128]{2,1,0:T(8,128)}, f32[7,512,128]{2,1,0:T(8,128)S(1)}, f32[4,512,128]{2,1,0:T(8,128)S(1)}, f32[224,128]{1,0:T(8,128)S(1)}, f32[22...) custom-call(f32[19,512,128]{2,1,0:T(8,128)} %get-tuple-element.39.pops_ref, ...), custom_call_target="tpu_custom_call" | custom-call | flops 100000000 | bytes 20000000 | tf_op jit(solution)/shard_map/pallas_call | solution.py:726
  94.2 1.2 copy-done.4
  95.4 1.4 collective-permute-start.14
  96.8 1.8 collective-permute-done.14.ylo_ref
  98.6 3.6 %collective-permute-done.15.yhi_ref = f32[224,128]{1,0:T(8,128)S(1)} collective-permute-done((f32[224,128]{1,0:T(8,128)S(1)}, f32[224,128]{1,0:T(8,128)S(1)}, u32[]{:S(2)}, u32[]{:S(2)}) %collective-permute-start.15) | collective-permute-done | bytes 114720 | tf_op jit(solution)/shard_map/ppermute | solution.py:643
  102.6 1.5 collective-permute-start.16
  104.1 2.4 %collective-permute-done.17.zhi_ref = f32[256,128]{1,0:T(8,128)S(1)} collective-permute-done((f32[256,128]{1,0:T(8,128)S(1)}, f32[256,128]{1,0:T(8,128)S(1)}, u32[]{:S(2)}, u32[]{:S(2)}) %collective-permute-start.17) | collective-permute-done | bytes 131104 | tf_op jit(solution)/shard_map/ppermute | solution.py:643
  106.4 1.3 collective-permute-done.16.zlo_ref
  107.7 10.2 %shard_map.74 = (f32[19,512,128]{2,1,0:T(8,128)}, f32[7,512,128]{2,1,0:T(8,128)S(1)}, f32[4,512,128]{2,1,0:T(8,128)S(1)}, f32[224,128]{1,0:T(8,128)S(1)}, f32[22...) custom-call(f32[19,512,128]{2,1,0:T(8,128)} %get-tuple-element.51.pops_ref, ...), custom_call_target="tpu_custom_call" | custom-call | flops 100000000 | bytes 20000000 | tf_op jit(solution)/shard_map/pallas_call | solution.py:726
  117.9 1.2 copy-done.5
  119.2 1.2 collective-permute-start.18
  120.4 1.8 collective-permute-done.18.ylo_ref
  122.2 3.6 %collective-permute-done.19.yhi_ref = f32[224,128]{1,0:T(8,128)S(1)} collective-permute-done((f32[224,128]{1,0:T(8,128)S(1)}, f32[224,128]{1,0:T(8,128)S(1)}, u32[]{:S(2)}, u32[]{:S(2)}) %collective-permute-start.19) | collective-permute-done | bytes 114720 | tf_op jit(solution)/shard_map/ppermute | solution.py:643
  126.5 1.0 collective-permute-start.20
  127.5 2.4 %collective-permute-done.21.zhi_ref = f32[256,128]{1,0:T(8,128)S(1)} collective-permute-done((f32[256,128]{1,0:T(8,128)S(1)}, f32[256,128]{1,0:T(8,128)S(1)}, u32[]{:S(2)}, u32[]{:S(2)}) %collective-permute-start.21) | collective-permute-done | bytes 131104 | tf_op jit(solution)/shard_map/ppermute | solution.py:643
  129.8 2.0 %collective-permute-done.20.zlo_ref = f32[256,128]{1,0:T(8,128)S(1)} collective-permute-done((f32[256,128]{1,0:T(8,128)S(1)}, f32[256,128]{1,0:T(8,128)S(1)}, u32[]{:S(2)}, u32[]{:S(2)}) %collective-permute-start.20) | collective-permute-done | bytes 131104 | tf_op jit(solution)/shard_map/ppermute | solution.py:643
  131.8 10.2 %shard_map.75 = (f32[19,512,128]{2,1,0:T(8,128)}, f32[7,512,128]{2,1,0:T(8,128)S(1)}, f32[4,512,128]{2,1,0:T(8,128)S(1)}, f32[224,128]{1,0:T(8,128)S(1)}, f32[22...) custom-call(f32[19,512,128]{2,1,0:T(8,128)} %get-tuple-element.58.pops_ref, ...), custom_call_target="tpu_custom_call" | custom-call | flops 100000000 | bytes 20000000 | tf_op jit(solution)/shard_map/pallas_call | solution.py:726
  142.1 1.0 copy-done.6
  143.0 1.2 collective-permute-start.22
  144.2 1.8 collective-permute-done.22.ylo_ref
  146.1 3.6 %collective-permute-done.23.yhi_ref = f32[224,128]{1,0:T(8,128)S(1)} collective-permute-done((f32[224,128]{1,0:T(8,128)S(1)}, f32[224,128]{1,0:T(8,128)S(1)}, u32[]{:S(2)}, u32[]{:S(2)}) %collective-permute-start.23) | collective-permute-done | bytes 114720 | tf_op jit(solution)/shard_map/ppermute | solution.py:643
  149.8 1.8 collective-permute-start.25
  151.6 2.3 %collective-permute-done.25.zhi_ref = f32[256,128]{1,0:T(8,128)S(1)} collective-permute-done((f32[256,128]{1,0:T(8,128)S(1)}, f32[256,128]{1,0:T(8,128)S(1)}, u32[]{:S(2)}, u32[]{:S(2)}) %collective-permute-start.25) | collective-permute-done | bytes 131104 | tf_op jit(solution)/shard_map/ppermute | solution.py:643
  153.9 2.7 %collective-permute-done.24.zlo_ref = f32[256,128]{1,0:T(8,128)S(1)} collective-permute-done((f32[256,128]{1,0:T(8,128)S(1)}, f32[256,128]{1,0:T(8,128)S(1)}, u32[]{:S(2)}, u32[]{:S(2)}) %collective-permute-start.24) | collective-permute-done | bytes 131104 | tf_op jit(solution)/shard_map/ppermute | solution.py:643
  156.7 5.5 %shard_map.77 = f32[8,224,128]{2,1,0:T(8,128)S(1)} custom-call(s32[1,1,8]{2,1,0:T(1,128)S(1)} %copy-done.9, f32[7,512,128]{2,1,0:T(8,128)S(1)} %get-tuple-element.66.post_ref, s32[512,128]{1,0:T(8,128)S(1)} %get-tuple-element.44.bits_ref, f32[224,128]{1,0:T(8,128)S(1)} %collective-permute-done.22.ylo_ref, f32[224,128]{1,0:T(8,128)S(1)} %collective-permute-done.23.yhi_ref, ...), custom_call_target="tpu_custom_call" | custom-call | flops 10000000 | bytes 5000000 | tf_op jit(solution)/shard_map/pallas_call | solution.py:735
  162.2 0.9 copy-done.2
  163.1 4.3 %all-to-all-start.1 = ((f32[8,224,128]{2,1,0:T(8,128)}), f32[8,224,128]{2,1,0:T(8,128)}, u32[]{:S(2)}, u32[]{:S(2)}) async-start(f32[8,224,128]{2,1,0:T(8,128)} %copy-done.2), calls=%async_computation.1 | async-start | bytes 1835008 | tf_op jit(solution)/shard_map/all_to_all | solution.py:743
  167.4 1.2 copy-done.7
  168.6 8.5 %shard_map.76 = f32[19,256,128]{2,1,0:T(8,128)} custom-call(f32[19,512,128]{2,1,0:T(8,128)} %get-tuple-element.65.pops_ref, f32[7,512,128]{2,1,0:T(8,128)S(1)} %get-tuple-element.66.post_ref, f32[4,512,128]{2,1,0:T(8,128)S(1)} %copy-done.7, s32[512,128]{1,0:T(8,128)S(1)} %get-tuple-element.44.bits_ref, f32[256,128]{1,0:T(8,128)S(1)} %get-tuple-element.46.open_ref, ...), custom_call_target="tpu_custom_call" | custom-call | flops 100000000 | bytes 20000000 | tf_op jit(solution)/shard_map/pallas_call | solution.py:744
  177.1 15.0 %all-to-all-done.1.recv_ref = f32[8,224,128]{2,1,0:T(8,128)} async-done(((f32[8,224,128]{2,1,0:T(8,128)}), f32[8,224,128]{2,1,0:T(8,128)}, u32[]{:S(2)}, u32[]{:S(2)}) %all-to-all-start.1) | async-done | bytes 917536 | tf_op jit(solution)/shard_map/all_to_all | solution.py:743
  192.2 2.4 %shard_map.78 = f32[1792,128]{1,0:T(8,128)} custom-call(s32[8]{0:T(128)S(1)} %copy-done.11, f32[8,224,128]{2,1,0:T(8,128)} %all-to-all-done.1.recv_ref), custom_call_target="tpu_custom_call" | custom-call | flops 1 | bytes 2000000 | tf_op jit(solution)/shard_map/pallas_call | solution.py:747
  (73 shorter events, 3.7 us)
Async XLA Ops:
  2.3 14.8 %collective-permute-start.2 = (f32[16,16,8]{2,1,0:T(8,128)}, f32[16,16,8]{2,1,0:T(8,128)}, u32[]{:S(2)}, u32[]{:S(2)}) collective-permute-start(f32[16,16,8]{2,1,0:T(8,128)} %get-tuple-element.76), channel_id=1, source_target_pairs={{0,192},{64,0},{128,64},{192,128},{1,193},{65,1},{129,65},{193,129... | collective-permute-start | bytes 24584 | tf_op jit(solution)/shard_map/ppermute | solution.py:643
  5.0 13.0 %collective-permute-start.3 = (f32[16,16,8]{2,1,0:T(8,128)}, f32[16,16,8]{2,1,0:T(8,128)}, u32[]{:S(2)}, u32[]{:S(2)}) collective-permute-start(f32[16,16,8]{2,1,0:T(8,128)} %get-tuple-element.77), channel_id=1, source_target_pairs={{0,64},{64,128},{128,192},{192,0},{1,65},{65,129},{129,193},{193,1... | collective-permute-start | bytes 24584 | tf_op jit(solution)/shard_map/ppermute | solution.py:643
  5.0 1.2 copy-start.8
  6.2 0.7 copy-start.10
  7.8 0.9 copy-start.1
  8.7 22.7 %copy-start = (f32[19,16,16,128]{3,2,1,0:T(8,128)S(1)}, f32[19,16,16,128]{3,2,1,0:T(8,128)}, u32[]{:S(2)}) copy-start(f32[19,16,16,128]{3,2,1,0:T(8,128)} %param.5) | copy-start | bytes 7471108
  8.7 34.4 %all-to-all-start = ((f32[8,224,128]{2,1,0:T(8,128)}), f32[8,224,128]{2,1,0:T(8,128)S(1)}, u32[]{:S(2)}, u32[]{:S(2)}) async-start(f32[8,224,128]{2,1,0:T(8,128)} %copy-done.1), calls=%async_computation | async-start | bytes 1835008 | tf_op jit(solution)/shard_map/all_to_all | solution.py:684
  19.1 24.0 %copy-start.9 = (s32[1,1,8]{2,1,0:T(1,128)S(1)}, s32[1,1,8]{2,1,0:T(1,128)}, u32[]{:S(2)}) copy-start(s32[1,1,8]{2,1,0:T(1,128)} %slot_ref.6) | copy-start | bytes 100
  19.1 4.4 %collective-permute-start.5 = (f32[16,2,1,128]{3,2,0,1:T(1,128)S(1)}, f32[16,2,1,128]{3,2,0,1:T(1,128)S(1)}, u32[]{:S(2)}, u32[]{:S(2)}) collective-permute-start(f32[16,2,1,128]{3,2,0,1:T(1,128)S(1)} %get-tuple-element.74), channel_id=1, source_target_pairs={{0,56},{8,0},{16,8},{24,16},{32,24},{40,32},{48,40},{56,48},{1,57}... | collective-permute-start | bytes 49160 | tf_op jit(solution)/shard_map/ppermute | solution.py:643
  21.1 3.0 %collective-permute-start.4 = (f32[16,2,1,128]{3,2,0,1:T(1,128)S(1)}, f32[16,2,1,128]{3,2,0,1:T(1,128)S(1)}, u32[]{:S(2)}, u32[]{:S(2)}) collective-permute-start(f32[16,2,1,128]{3,2,0,1:T(1,128)S(1)} %get-tuple-element.75), channel_id=1, source_target_pairs={{0,8},{8,16},{16,24},{24,32},{32,40},{40,48},{48,56},{56,0},{1,9},... | collective-permute-start | bytes 49160 | tf_op jit(solution)/shard_map/ppermute | solution.py:643
  30.0 10.2 %collective-permute-start.6 = (f32[1,2,32,128]{3,2,0,1:T(8,128)S(1)}, f32[1,2,32,128]{3,2,0,1:T(8,128)S(1)}, u32[]{:S(2)}, u32[]{:S(2)}) collective-permute-start(f32[1,2,32,128]{3,2,0,1:T(8,128)S(1)} %get-tuple-element.72), channel_id=1, source_target_pairs={{0,1},{1,2},{2,3},{3,4},{4,5},{5,6},{6,7},{7,0},{8,9},{9,10},{10,1... | collective-permute-start | bytes 98312 | tf_op jit(solution)/shard_map/ppermute | solution.py:643
  36.0 15.9 %collective-permute-start = (f32[304,128]{1,0:T(8,128)}, f32[304,128]{1,0:T(8,128)}, u32[]{:S(2)}, u32[]{:S(2)}) collective-permute-start(f32[304,128]{1,0:T(8,128)} %get-tuple-element.37), channel_id=1, source_target_pairs={{0,192},{64,0},{128,64},{192,128},{1,193},{65,1},{129,65},{193,129... | collective-permute-start | bytes 466952 | tf_op jit(solution)/shard_map/ppermute | solution.py:643
  38.6 13.2 %collective-permute-start.1 = (f32[304,128]{1,0:T(8,128)}, f32[304,128]{1,0:T(8,128)}, u32[]{:S(2)}, u32[]{:S(2)}) collective-permute-start(f32[304,128]{1,0:T(8,128)} %get-tuple-element.38), channel_id=1, source_target_pairs={{0,64},{64,128},{128,192},{192,0},{1,65},{65,129},{129,193},{193,1... | collective-permute-start | bytes 466952 | tf_op jit(solution)/shard_map/ppermute | solution.py:643
  38.6 3.2 %collective-permute-start.7 = (f32[1,2,32,128]{3,2,0,1:T(8,128)S(1)}, f32[1,2,32,128]{3,2,0,1:T(8,128)S(1)}, u32[]{:S(2)}, u32[]{:S(2)}) collective-permute-start(f32[1,2,32,128]{3,2,0,1:T(8,128)S(1)} %get-tuple-element.73), channel_id=1, source_target_pairs={{0,7},{1,0},{2,1},{3,2},{4,3},{5,4},{6,5},{7,6},{8,15},{9,8},{10,9... | collective-permute-start | bytes 98312 | tf_op jit(solution)/shard_map/ppermute | solution.py:643
  48.2 12.6 %collective-permute-start.8 = (f32[112,128]{1,0:T(8,128)S(1)}, f32[112,128]{1,0:T(8,128)S(1)}, u32[]{:S(2)}, u32[]{:S(2)}) collective-permute-start(f32[112,128]{1,0:T(8,128)S(1)} %get-tuple-element.41), channel_id=1, source_target_pairs={{0,192},{64,0},{128,64},{192,128},{1,193},{65,1},{129,65},{193,129... | collective-permute-start | bytes 172040 | tf_op jit(solution)/shard_map/ppermute | solution.py:643
  50.7 10.1 %collective-permute-start.9 = (f32[112,128]{1,0:T(8,128)S(1)}, f32[112,128]{1,0:T(8,128)S(1)}, u32[]{:S(2)}, u32[]{:S(2)}) collective-permute-start(f32[112,128]{1,0:T(8,128)S(1)} %get-tuple-element.42), channel_id=1, source_target_pairs={{0,64},{64,128},{128,192},{192,0},{1,65},{65,129},{129,193},{193,1... | collective-permute-start | bytes 172040 | tf_op jit(solution)/shard_map/ppermute | solution.py:643
  65.5 1.2 copy-start.3
  66.8 5.8 %collective-permute-start.10 = (f32[224,128]{1,0:T(8,128)S(1)}, f32[224,128]{1,0:T(8,128)S(1)}, u32[]{:S(2)}, u32[]{:S(2)}) collective-permute-start(f32[224,128]{1,0:T(8,128)S(1)} %get-tuple-element.47), channel_id=1, source_target_pairs={{0,8},{8,16},{16,24},{24,32},{32,40},{40,48},{48,56},{56,0},{1,9},... | collective-permute-start | bytes 344072 | tf_op jit(solution)/shard_map/ppermute | solution.py:643
  70.8 5.4 %collective-permute-start.11 = (f32[224,128]{1,0:T(8,128)S(1)}, f32[224,128]{1,0:T(8,128)S(1)}, u32[]{:S(2)}, u32[]{:S(2)}) collective-permute-start(f32[224,128]{1,0:T(8,128)S(1)} %get-tuple-element.48), channel_id=1, source_target_pairs={{0,56},{8,0},{16,8},{24,16},{32,24},{40,32},{48,40},{56,48},{1,57}... | collective-permute-start | bytes 344072 | tf_op jit(solution)/shard_map/ppermute | solution.py:643
  76.4 4.5 %collective-permute-start.13 = (f32[256,128]{1,0:T(8,128)S(1)}, f32[256,128]{1,0:T(8,128)S(1)}, u32[]{:S(2)}, u32[]{:S(2)}) collective-permute-start(f32[256,128]{1,0:T(8,128)S(1)} %get-tuple-element.102), channel_id=1, source_target_pairs={{0,7},{1,0},{2,1},{3,2},{4,3},{5,4},{6,5},{7,6},{8,15},{9,8},{10,9... | collective-permute-start | bytes 393224 | tf_op jit(solution)/shard_map/ppermute | solution.py:643
  78.9 5.0 %collective-permute-start.12 = (f32[256,128]{1,0:T(8,128)S(1)}, f32[256,128]{1,0:T(8,128)S(1)}, u32[]{:S(2)}, u32[]{:S(2)}) collective-permute-start(f32[256,128]{1,0:T(8,128)S(1)} %get-tuple-element.103), channel_id=1, source_target_pairs={{0,1},{1,2},{2,3},{3,4},{4,5},{5,6},{6,7},{7,0},{8,9},{9,10},{10,1... | collective-permute-start | bytes 393224 | tf_op jit(solution)/shard_map/ppermute | solution.py:643
  94.2 1.2 copy-start.4
  95.4 3.2 %collective-permute-start.14 = (f32[224,128]{1,0:T(8,128)S(1)}, f32[224,128]{1,0:T(8,128)S(1)}, u32[]{:S(2)}, u32[]{:S(2)}) collective-permute-start(f32[224,128]{1,0:T(8,128)S(1)} %get-tuple-element.54), channel_id=1, source_target_pairs={{0,8},{8,16},{16,24},{24,32},{32,40},{40,48},{48,56},{56,0},{1,9},... | collective-permute-start | bytes 344072 | tf_op jit(solution)/shard_map/ppermute | solution.py:643
  96.8 5.4 %collective-permute-start.15 = (f32[224,128]{1,0:T(8,128)S(1)}, f32[224,128]{1,0:T(8,128)S(1)}, u32[]{:S(2)}, u32[]{:S(2)}) collective-permute-start(f32[224,128]{1,0:T(8,128)S(1)} %get-tuple-element.55), channel_id=1, source_target_pairs={{0,56},{8,0},{16,8},{24,16},{32,24},{40,32},{48,40},{56,48},{1,57}... | collective-permute-start | bytes 344072 | tf_op jit(solution)/shard_map/ppermute | solution.py:643
  102.4 4.1 %collective-permute-start.17 = (f32[256,128]{1,0:T(8,128)S(1)}, f32[256,128]{1,0:T(8,128)S(1)}, u32[]{:S(2)}, u32[]{:S(2)}) collective-permute-start(f32[256,128]{1,0:T(8,128)S(1)} %get-tuple-element.100), channel_id=1, source_target_pairs={{0,7},{1,0},{2,1},{3,2},{4,3},{5,4},{6,5},{7,6},{8,15},{9,8},{10,9... | collective-permute-start | bytes 393224 | tf_op jit(solution)/shard_map/ppermute | solution.py:643
  102.6 5.1 %collective-permute-start.16 = (f32[256,128]{1,0:T(8,128)S(1)}, f32[256,128]{1,0:T(8,128)S(1)}, u32[]{:S(2)}, u32[]{:S(2)}) collective-permute-start(f32[256,128]{1,0:T(8,128)S(1)} %get-tuple-element.101), channel_id=1, source_target_pairs={{0,1},{1,2},{2,3},{3,4},{4,5},{5,6},{6,7},{7,0},{8,9},{9,10},{10,1... | collective-permute-start | bytes 393224 | tf_op jit(solution)/shard_map/ppermute | solution.py:643
  117.9 1.2 copy-start.5
  119.2 3.0 %collective-permute-start.18 = (f32[224,128]{1,0:T(8,128)S(1)}, f32[224,128]{1,0:T(8,128)S(1)}, u32[]{:S(2)}, u32[]{:S(2)}) collective-permute-start(f32[224,128]{1,0:T(8,128)S(1)} %get-tuple-element.61), channel_id=1, source_target_pairs={{0,8},{8,16},{16,24},{24,32},{32,40},{40,48},{48,56},{56,0},{1,9},... | collective-permute-start | bytes 344072 | tf_op jit(solution)/shard_map/ppermute | solution.py:643
  120.4 5.4 %collective-permute-start.19 = (f32[224,128]{1,0:T(8,128)S(1)}, f32[224,128]{1,0:T(8,128)S(1)}, u32[]{:S(2)}, u32[]{:S(2)}) collective-permute-start(f32[224,128]{1,0:T(8,128)S(1)} %get-tuple-element.62), channel_id=1, source_target_pairs={{0,56},{8,0},{16,8},{24,16},{32,24},{40,32},{48,40},{56,48},{1,57}... | collective-permute-start | bytes 344072 | tf_op jit(solution)/shard_map/ppermute | solution.py:643
  125.9 3.9 %collective-permute-start.21 = (f32[256,128]{1,0:T(8,128)S(1)}, f32[256,128]{1,0:T(8,128)S(1)}, u32[]{:S(2)}, u32[]{:S(2)}) collective-permute-start(f32[256,128]{1,0:T(8,128)S(1)} %get-tuple-element.98), channel_id=1, source_target_pairs={{0,7},{1,0},{2,1},{3,2},{4,3},{5,4},{6,5},{7,6},{8,15},{9,8},{10,9... | collective-permute-start | bytes 393224 | tf_op jit(solution)/shard_map/ppermute | solution.py:643
  126.5 5.3 %collective-permute-start.20 = (f32[256,128]{1,0:T(8,128)S(1)}, f32[256,128]{1,0:T(8,128)S(1)}, u32[]{:S(2)}, u32[]{:S(2)}) collective-permute-start(f32[256,128]{1,0:T(8,128)S(1)} %get-tuple-element.99), channel_id=1, source_target_pairs={{0,1},{1,2},{2,3},{3,4},{4,5},{5,6},{6,7},{7,0},{8,9},{9,10},{10,1... | collective-permute-start | bytes 393224 | tf_op jit(solution)/shard_map/ppermute | solution.py:643
  142.1 1.0 copy-start.6
  143.0 3.0 %collective-permute-start.22 = (f32[224,128]{1,0:T(8,128)S(1)}, f32[224,128]{1,0:T(8,128)S(1)}, u32[]{:S(2)}, u32[]{:S(2)}) collective-permute-start(f32[224,128]{1,0:T(8,128)S(1)} %get-tuple-element.68), channel_id=1, source_target_pairs={{0,8},{8,16},{16,24},{24,32},{32,40},{40,48},{48,56},{56,0},{1,9},... | collective-permute-start | bytes 344072 | tf_op jit(solution)/shard_map/ppermute | solution.py:643
  144.2 5.4 %collective-permute-start.23 = (f32[224,128]{1,0:T(8,128)S(1)}, f32[224,128]{1,0:T(8,128)S(1)}, u32[]{:S(2)}, u32[]{:S(2)}) collective-permute-start(f32[224,128]{1,0:T(8,128)S(1)} %get-tuple-element.69), channel_id=1, source_target_pairs={{0,56},{8,0},{16,8},{24,16},{32,24},{40,32},{48,40},{56,48},{1,57}... | collective-permute-start | bytes 344072 | tf_op jit(solution)/shard_map/ppermute | solution.py:643
  149.8 4.1 %collective-permute-start.25 = (f32[256,128]{1,0:T(8,128)S(1)}, f32[256,128]{1,0:T(8,128)S(1)}, u32[]{:S(2)}, u32[]{:S(2)}) collective-permute-start(f32[256,128]{1,0:T(8,128)S(1)} %get-tuple-element.96), channel_id=1, source_target_pairs={{0,7},{1,0},{2,1},{3,2},{4,3},{5,4},{6,5},{7,6},{8,15},{9,8},{10,9... | collective-permute-start | bytes 393224 | tf_op jit(solution)/shard_map/ppermute | solution.py:643
  151.6 5.0 %collective-permute-start.24 = (f32[256,128]{1,0:T(8,128)S(1)}, f32[256,128]{1,0:T(8,128)S(1)}, u32[]{:S(2)}, u32[]{:S(2)}) collective-permute-start(f32[256,128]{1,0:T(8,128)S(1)} %get-tuple-element.97), channel_id=1, source_target_pairs={{0,1},{1,2},{2,3},{3,4},{4,5},{5,6},{6,7},{7,0},{8,9},{9,10},{10,1... | collective-permute-start | bytes 393224 | tf_op jit(solution)/shard_map/ppermute | solution.py:643
  162.2 0.9 copy-start.2
  163.1 29.0 %all-to-all-start.1 = ((f32[8,224,128]{2,1,0:T(8,128)}), f32[8,224,128]{2,1,0:T(8,128)}, u32[]{:S(2)}, u32[]{:S(2)}) async-start(f32[8,224,128]{2,1,0:T(8,128)} %copy-done.2), calls=%async_computation.1 | async-start | bytes 1835008 | tf_op jit(solution)/shard_map/all_to_all | solution.py:743
  167.4 1.2 copy-start.7
  168.6 23.5 %copy-start.11 = (s32[8]{0:T(128)S(1)}, s32[8]{0:T(128)}, u32[]{:S(2)}) copy-start(s32[8]{0:T(128)} %slot_ref.7) | copy-start | bytes 100
where the time goes:
time: 196 us; the launch traced here: 195 us
  Pallas kernels  71.2 us (36%)
  waiting for transfers between devices  58.3 us (30%)
  starting transfers between devices  41.8 us (21%)
  local copies, waits for them, and re-layouts  15.9 us (8%)
  other arithmetic  6.31 us (3%)
    ppermute x26, waiting for transfers between devices, neighbours(): return (lax.ppermute(high, axis, up), lax.ppermute(low, axis, down))  42 us
    pallas_call x3, Pallas kernels, shards(): call(step_kernel, (shape(19, ROWS, L), shape(7, ROWS, L), shape(4, ROWS,...  30.7 us
    ppermute x26, starting transfers between devices, neighbours(): return (lax.ppermute(high, axis, up), lax.ppermute(low, axis, down))  29.2 us
    all_to_all x2, waiting for transfers between devices, shards(): recv = lax.all_to_all(send, 'gz', split_axis=0, concat_axis=0, tiled=True)  16.3 us
    all_to_all x2, starting transfers between devices, shards(): recv = lax.all_to_all(send, 'gz', split_axis=0, concat_axis=0, tiled=True)  12.6 us
    unnamed x36, local copies, waits for them, and re-layouts  9.58 us
    pallas_call x1, Pallas kernels, shards(): call(start_kernel, (shape(19, ROWS, L), shape(4, ROWS, L), jax.ShapeDtype...  8.94 us
    pallas_call x1, Pallas kernels, shards(): call(last_flow_kernel, shape(19, 256, L), [VMEM] * 9, [scratch[0], scratc...  8.46 us
  transfers between devices with their start and end apart: 28, of which 20 were waited for; matrix products, arithmetic and copies ran while one was open for 5% of the time, Pallas kernels for 14%

commit v1 on v0

v1 whole, which is shorter than its diff:
```python
import functools

import jax
import jax.numpy as jnp
from jax import lax
from jax.experimental import pallas as pl
from jax.experimental.pallas import tpu as pltpu
from jax.sharding import PartitionSpec as P

STEPS = 4
DIRS = [
    (0, 0, 0),
    (1, 0, 0),
    (-1, 0, 0),
    (0, 1, 0),
    (0, -1, 0),
    (0, 0, 1),
    (0, 0, -1),
    (1, 1, 0),
    (-1, -1, 0),
    (1, -1, 0),
    (-1, 1, 0),
    (1, 0, 1),
    (-1, 0, -1),
    (1, 0, -1),
    (-1, 0, 1),
    (0, 1, 1),
    (0, -1, -1),
    (0, 1, -1),
    (0, -1, 1),
]
OPP = [DIRS.index((-a, -b, -c)) for a, b, c in DIRS]
PAIRS = [(i, OPP[i]) for i in range(1, 19, 2)]
WEIGHTS = [1.0 / 3.0] + [1.0 / 18.0] * 6 + [1.0 / 36.0] * 12
OMEGA_FLOW = 1.2
FORCE_GAIN = 0.02
REST_CONC = 8.0
Y_UP = [i for i in range(19) if DIRS[i][1] == 1]
Y_DN = [i for i in range(19) if DIRS[i][1] == -1]
Z_UP = [i for i in range(19) if DIRS[i][2] == 1]
Z_DN = [i for i in range(19) if DIRS[i][2] == -1]
RHO, VEL, PART, NORM, TRANS, MASK = 5, 6, 9, 10, 11, 12
SIDES = 2
B = 16
L = 128
W = 8
PLANE = 2 * B
ROWS = B * PLANE
PADDED = 64
PADROWS = (B + 2) * PADDED
BLOCKROWS = 7 * 32 * 8
F32 = jnp.float32
VMEM = pl.BlockSpec(memory_space=pltpu.VMEM)
SMEM = pl.BlockSpec(memory_space=pltpu.SMEM)


def call(kernel, out_shape, in_specs, scratch, flops, nbytes, aliases={}, keep=False):
    run = pl.pallas_call(
        kernel,
        out_shape=out_shape,
        in_specs=in_specs,
        out_specs=jax.tree.map(lambda _: VMEM, out_shape),
        scratch_shapes=scratch,
        input_output_aliases=aliases,
        compiler_params=pltpu.CompilerParams(vmem_limit_bytes=20 * 1024 * 1024),
        cost_estimate=pl.CostEstimate(flops=flops, bytes_accessed=nbytes, transcendentals=0),
    )

    if not keep:
        return run

    def placed(*args):
        return run(
            *(
                pltpu.with_memory_space_constraint(x, pltpu.VMEM) if spec is VMEM else x
                for x, spec in zip(args, in_specs)
            )
        )

    return placed


def shape(*dims):
    return jax.ShapeDtypeStruct(dims, F32)


def held(*dims, dtype=F32):
    return pltpu.VMEM(dims, dtype)


def lanes(rows):
    return lax.broadcasted_iota(jnp.int32, (rows, L), 1)


def row_ids(rows):
    return lax.broadcasted_iota(jnp.int32, (rows, L), 0)


def ring(v, step):
    rolled = pltpu.roll(v, step % L, axis=1)
    other = jnp.concatenate([rolled[B:], rolled[:B]], axis=0)
    return jnp.where(lanes(PLANE) == (0 if step > 0 else L - 1), other, rolled)


def halves(main, side):
    return jnp.concatenate([main, side], axis=0)


def spread(main, side):
    return halves(jnp.broadcast_to(main, (B, L)), jnp.broadcast_to(side, (B, L)))


def shift_rows(v, step, fill):
    rolled = pltpu.roll(v, step % PLANE, axis=0)
    return jnp.where(row_ids(PLANE) % B == (0 if step > 0 else B - 1), fill, rolled)


def is_open(bits, which):
    return (bits & (1 << which)) != 0


def along(which, vx, vy, vz):
    total = None
    for sign, part in zip(DIRS[which], (vx, vy, vz)):
        if sign != 0:
            if total is None:
                total = part if sign > 0 else -part
            else:
                total = total + part if sign > 0 else total - part
    return total


def moments(pops, porous):
    rho = pops[0]
    for which in range(1, 19):
        rho = rho + pops[which]
    scale = porous / rho
    parts = []
    for coord in range(3):
        plus = sum(pops[i] for i in range(19) if DIRS[i][coord] == 1)
        minus = sum(pops[i] for i in range(19) if DIRS[i][coord] == -1)
        parts.append((plus - minus) * scale)
    return rho, parts


def solute_collide(solute, velocity):
    conc = sum(solute)
    out = [-0.5 * solute[0] + 0.375 * conc]
    base = 0.1875 * conc
    for coord in range(3):
        turn = 0.75 * conc * velocity[coord]
        out.append((base - 0.5 * solute[1 + 2 * coord]) + turn)
        out.append((base - 0.5 * solute[2 + 2 * coord]) - turn)
    return out


def chosen(bits, moved, post, which):
    return jnp.where(
        is_open(bits, which),
        moved,
        jnp.where(is_open(bits, 0), post[OPP[which]], post[which]),
    )


def turn_blocks(x):
    row, lane = row_ids(8), lanes(8)
    x = take(x, (lane - B * row) & (L - 1), 1)
    x = take(x, (lane // B - row) & 7, 0)
    return take(x, (lane + B * row) & (L - 1), 1)


def take(x, index, axis):
    return jnp.take_along_axis(x, index, axis=axis, mode="promise_in_bounds")


def gather_kernel(slot_ref, state_ref, send_ref):
    for dest in range(8):
        slot = jnp.int32(0)
        for s in range(8):
            home = slot_ref[s]
            slot = jnp.where((home >= 0) & (home // 8 == dest), s, slot)
        send_ref[dest] = state_ref[pl.ds(slot, BLOCKROWS // 8, stride=8), :]


def spread_kernel(slot_ref, recv_ref, dense_ref, turn_ref):
    for tile in range(8):
        owner = jnp.maximum(slot_ref[0, 0, tile], 0) // 8
        turn_ref[pl.ds(tile, BLOCKROWS // 8, stride=8), :] = recv_ref[owner]

    def body(group, carry):
        for i in range(16):
            at = pl.multiple_of(group * 128 + i * 8, 8)
            dense_ref[pl.ds(at, 8), :] = turn_blocks(turn_ref[pl.ds(at, 8), :])
        return carry

    lax.fori_loop(0, BLOCKROWS // 128, body, 0)


def pack_columns(load, low_ref, high_ref, at):
    lane = lanes(8) // W
    low = jnp.zeros((8, L), F32)
    high = jnp.zeros((8, L), F32)
    for i in range(16):
        x = load(i)
        low = jnp.where(lane == i, x if i == 0 else pltpu.roll(x, W * i, axis=1), low)
        turn = (W + W * i) % L
        high = jnp.where(lane == i, x if turn == 0 else pltpu.roll(x, turn, axis=1), high)
    at = pl.multiple_of(at, 8)
    low_ref[pl.ds(at, 8), :] = low
    high_ref[pl.ds(at, 8), :] = high


def columns_kernel(pops_ref, mask_ref, low_ref, high_ref):
    def rows(start, i):
        return pl.ds(pl.multiple_of(start + i * 8, 8), 8)

    def body(group, carry):
        at = (group % 2) * 128
        pack_columns(
            lambda i: pops_ref[group // 2, rows(at, i), :], low_ref, high_ref, group * 8
        )
        return carry

    lax.fori_loop(0, 38, body, 0)
    for group in range(2):
        pack_columns(
            lambda i: mask_ref[rows(group * 128, i), :].astype(F32),
            low_ref,
            high_ref,
            (38 + group) * 8,
        )


def unpack_columns(right, left, i):
    a = right if i == 0 else pltpu.roll(right, L - W * i, axis=1)
    b = left if i == 15 else pltpu.roll(left, L - W - W * i, axis=1)
    return jnp.where(lanes(8) < L // 2, a, b)


def ring_kernel(
    flag_ref, pops_ref, mask_ref, right_ref, left_ref,
    side_ref, ring_ref, aux_ref,
):
    def body(group, carry):
        at = pl.ds(pl.multiple_of(group * 8, 8), 8)
        right, left = right_ref[at, :], left_ref[at, :]
        for i in range(16):
            row = pl.multiple_of((group % 2) * 128 + i * 8, 8)
            side_ref[group // 2, pl.ds(row, 8), :] = unpack_columns(right, left, i)
        return carry

    lax.fori_loop(0, 38, body, 0)
    lane = lanes(8)
    inside = jnp.where(lane < W, flag_ref[1], jnp.where(lane >= L - W, flag_ref[0], 0.0))
    for group in range(2):
        right, left = right_ref[pl.ds(304 + group * 8, 8), :], left_ref[pl.ds(304 + group * 8, 8), :]
        for i in range(16):
            z = group * 8 + i // 2
            row = z * PLANE + (i % 2) * 8
            ring_ref[pl.ds(row, 8), :] = mask_ref[pl.ds(group * 128 + i * 8, 8), :].astype(F32)
            ring_ref[pl.ds(row + B, 8), :] = unpack_columns(right, left, i) * inside
    def flow(z, carry):
        pops = [flow_plane((pops_ref, side_ref), z, i) for i in range(19)]
        rho, velocity = moments(pops, plane(ring_ref, z))
        for k, v in enumerate([rho] + velocity):
            aux_ref[k, pl.ds(pl.multiple_of(z * PLANE, PLANE), PLANE), :] = v
        return carry

    lax.fori_loop(0, B, flow, 0)


def plane(ref, z, *lead):
    return ref[(*lead, pl.ds(pl.multiple_of(z * PLANE, PLANE), PLANE), slice(None))]


def flow_plane(refs, z, which):
    at = pl.ds(pl.multiple_of(z * B, B), B)
    return halves(refs[0][which, at, :], refs[1][which, at, :])


def flow_rows(refs, row, which):
    at = pl.ds(row, B, stride=B)
    return halves(refs[0][which, at, :], refs[1][which, at, :])


def padded_plane(ref, zz, shift, *lead):
    at = zz * PADDED + 8
    return halves(
        ref[(*lead, pl.ds(at - shift, B), slice(None))],
        ref[(*lead, pl.ds(at + 32 - shift, B), slice(None))],
    )


def put_rows(ref, zz, v):
    ref[pl.ds(zz * PADDED + 8, B), :] = v[:B]
    ref[pl.ds(zz * PADDED + 40, B), :] = v[B:]


def put_padded(ref, comp, zz, v):
    at = zz * PADDED + 8
    if not isinstance(zz, int):
        at = pl.multiple_of(at, 8)
    ref[comp, pl.ds(at, B), :] = v[:B]
    ref[comp, pl.ds(at + 32, B), :] = v[B:]


def face_rows(ref, row, *lead):
    return halves(
        ref[(*lead, pl.ds(row, B, stride=PLANE), slice(None))],
        ref[(*lead, pl.ds(B + row, B, stride=PLANE), slice(None))],
    )


def set_bits(mask_ref, bits_ref, z):
    here = padded_plane(mask_ref, z + 1, 0)
    bits = jnp.where(here > 0, 1, 0)
    for which in range(1, 19):
        cx, cy, cz = DIRS[which]
        source = padded_plane(mask_ref, z + 1 - cz, cy)
        if cx:
            source = ring(source, cx)
        bits = bits + jnp.where(source * here > 0, 1 << which, 0)
    bits_ref[pl.ds(pl.multiple_of(z * PLANE, PLANE), PLANE), :] = bits


def inner_open_kernel(flag_ref, ring_ref, ylo_ref, yhi_ref, mask_ref, bits_ref, open_ref):
    mask_ref[...] = jnp.zeros_like(mask_ref)
    for z in range(B):
        put_rows(mask_ref, z + 1, ring_ref[pl.ds(z * PLANE, PLANE), :])
    for side in range(2):
        halo = read_field((ylo_ref, yhi_ref)[side], MASK) * flag_ref[2 + side]
        for tile in range(2):
            part = halo[tile * B : (tile + 1) * B]
            edge = PADDED + tile * 32 + (7, 24)[side]
            inner = PADDED + tile * 32 + (8, 23)[side]
            mask_ref[pl.ds(edge, B, stride=PADDED), :] = part
            own = mask_ref[pl.ds(inner, B, stride=PADDED), :]
            put_open(open_ref, 0, side, tile, part * own)

    def body(z, carry):
        set_bits(mask_ref, bits_ref, z)
        return carry

    lax.fori_loop(1, B - 1, body, 0)


def edge_open_kernel(
    flag_ref, zlo_ref, zhi_ref, mask_in, bits_in, open_in, mask_ref, bits_ref, open_ref
):
    row = row_ids(B)
    for side in range(2):
        z_ref, zz = (zlo_ref, zhi_ref)[side], (0, B + 1)[side]
        put_rows(mask_ref, zz, read_field(z_ref, MASK) * flag_ref[4 + side])
        for y_side in range(2):
            pair = read_diag(z_ref, y_side, MASK)
            for tile in range(2):
                at = zz * PADDED + tile * 32 + (7, 24)[y_side]
                scale = flag_ref[4 + side] * flag_ref[2 + y_side]
                mask_ref[pl.ds(at, 1), :] = pair[tile][:1] * scale

    def body(k, carry):
        set_bits(mask_ref, bits_ref, k * (B - 1))
        return carry

    lax.fori_loop(0, 2, body, 0)
    for tile in range(2):
        for side in range(2):
            edge = tile * 32 + (7, 24)[side]
            halo = mask_ref[pl.ds(PADDED + edge, B, stride=PADDED), :]
            first = mask_ref[pl.ds(edge, 1), :]
            last = mask_ref[pl.ds(PADROWS - PADDED + edge, 1), :]
            ends = jnp.where(row == 0, halo * first, jnp.where(row == B - 1, halo * last, 0.0))
            put_open(open_ref, 1, side, tile, ends)
            at = (0, B + 1)[side] * PADDED + tile * 32
            near = (1, B)[side]
            halo = mask_ref[pl.ds(at + 8, B), :]
            own = mask_ref[pl.ds(near * PADDED + tile * 32 + 8, B), :]
            first = mask_ref[pl.ds(at + 7, 1), :]
            last = mask_ref[pl.ds(at + 24, 1), :]
            ends = jnp.where(row == 0, halo * first, jnp.where(row == B - 1, halo * last, 0.0))
            put_open(open_ref, 2, side, tile, halo * own)
            put_open(open_ref, 3, side, tile, ends)


def open_at(kind, side, tile):
    return ((kind * 2 + side) * 2 + tile) * B


def put_open(ref, kind, side, tile, v):
    ref[pl.ds(open_at(kind, side, tile), B), :] = v


def get_open(ref, kind, side):
    return ref[pl.ds(open_at(kind, side, 0), PLANE), :] > 0


def write_message(out_ref, fields):
    lane = lanes(B) // 16
    for slab in range(SIDES):
        packed = jnp.zeros((B, L), F32)
        for k, field in enumerate(fields[slab * 8 : slab * 8 + 8]):
            turn = (W + 16 * k) % L
            packed = jnp.where(lane == k, pltpu.roll(field[B:], turn, axis=1), packed)
        out_ref[pl.ds(slab * B, B), :] = packed
    for f, field in enumerate(fields):
        out_ref[pl.ds((SIDES + f) * B, B), :] = field[:B]


def unpack_side(packed, f):
    return pltpu.roll(packed, L - W - 16 * (f % 8), axis=1)


def read_field(ref, f):
    side = ref[pl.ds(f // 8 * B, B), :]
    return halves(ref[pl.ds((SIDES + f) * B, B), :], unpack_side(side, f))


def read_row(ref, f, row):
    main = jnp.broadcast_to(ref[pl.ds((SIDES + f) * B + row, 1), :], (8, L))
    side = jnp.broadcast_to(ref[pl.ds(f // 8 * B + row, 1), :], (8, L))
    return main, unpack_side(side, f)


def read_diag(ref, side, f):
    slabs = ref.shape[0] // (B + 2)
    base = slabs * B + side * slabs
    main = jnp.broadcast_to(ref[pl.ds(base + SIDES + f, 1), :], (8, L))
    packed = jnp.broadcast_to(ref[pl.ds(base + f // 8, 1), :], (8, L))
    return main, unpack_side(packed, f)


def spread8(pair):
    return halves(
        jnp.concatenate([pair[0], pair[0]], axis=0), jnp.concatenate([pair[1], pair[1]], axis=0)
    )


def partial_sum(f, inner, is_open, outward, in_rows):
    row = row_ids(PLANE) % B
    total = f[0]
    total = total + jnp.where(is_open(1), ring(f[1], 1), f[2])
    total = total + jnp.where(is_open(2), ring(f[2], -1), f[1])
    up, down = in_rows
    moved = jnp.where(is_open(up), pltpu.roll(f[up], 1, axis=0), f[down])
    total = total + jnp.where(row == 0, 0.0, moved)
    moved = jnp.where(is_open(down), pltpu.roll(f[down], PLANE - 1, axis=0), f[up])
    total = total + jnp.where(row == B - 1, 0.0, moved)
    return total + jnp.where(is_open(outward), inner, f[OPP[outward]])


def open_bits(bits):
    return lambda which: is_open(bits, which)


def open_mask(own, inner, in_rows):
    shifted = {
        1: ring(own, 1),
        2: ring(own, -1),
        in_rows[0]: pltpu.roll(own, 1, axis=0),
        in_rows[1]: pltpu.roll(own, PLANE - 1, axis=0),
    }
    return lambda which: shifted.get(which, inner) > 0


def write_y_messages(pops_refs, post_ref, aux_ref, y_refs, bits_ref=None, ring_ref=None):
    row = row_ids(PLANE) % B
    for side in range(2):
        names = (Y_DN, Y_UP)[side]
        edge, inner = ((0, 1), (B - 1, B - 2))[side]
        normal = (4, 3)[side]
        if ring_ref is None:
            opened = open_bits(face_rows(bits_ref, edge))
        else:
            opened = open_mask(face_rows(ring_ref, edge), face_rows(ring_ref, inner), (5, 6))
        f = [face_rows(post_ref, edge, i) for i in range(7)]
        part = partial_sum(f, face_rows(post_ref, inner, normal), opened, normal, (5, 6))
        fields = [flow_rows(pops_refs, edge, c) for c in names]
        fields += [face_rows(aux_ref, edge, k) for k in range(4)]
        fields += [part, f[normal], jnp.where(row == 0, f[6], f[5])]
        if ring_ref is not None:
            fields.append(face_rows(ring_ref, edge))
        write_message(y_refs[side], fields)


def write_z_messages(pops_refs, post_ref, aux_ref, z_refs, bits_ref=None, ring_ref=None):
    row = row_ids(PLANE) % B
    for side in range(2):
        names = (Z_DN, Z_UP)[side]
        edge, inner = ((0, 1), (B - 1, B - 2))[side]
        normal = (6, 5)[side]
        if ring_ref is None:
            opened = open_bits(plane(bits_ref, edge))
        else:
            opened = open_mask(plane(ring_ref, edge), plane(ring_ref, inner), (3, 4))
        f = [plane(post_ref, edge, i) for i in range(7)]
        part = partial_sum(f, plane(post_ref, inner, normal), opened, normal, (3, 4))
        fields = [flow_plane(pops_refs, edge, c) for c in names]
        fields += [plane(aux_ref, edge, k) for k in range(4)]
        fields += [part, f[normal], jnp.where(row == 0, f[4], f[3])]
        if ring_ref is not None:
            fields.append(plane(ring_ref, edge))
        write_message(z_refs[side], fields)


def relax(f, which, rho, vx, vy, vz, base):
    a = along(which, vx, vy, vz)
    scale = (OMEGA_FLOW * WEIGHTS[which]) * rho
    return (1.0 - OMEGA_FLOW) * f + scale * (base + a * (3.0 + 4.5 * a))


def lifted(conc, vx, vy, vz):
    vz = vz + FORCE_GAIN * (conc - REST_CONC)
    return vz, 1.0 - 1.5 * (vx * vx + vy * vy + vz * vz)


def stream_solute(z, post_ref, bits, ghost_ref, below, above):
    def fill(side):
        return spread(
            ghost_ref[pl.ds(side * PLANE + z, 1), :], ghost_ref[pl.ds(side * PLANE + B + z, 1), :]
        )

    post = [plane(post_ref, z, i) for i in range(7)]
    moved = [
        None,
        ring(post[1], 1),
        ring(post[2], -1),
        shift_rows(post[3], 1, fill(0)),
        shift_rows(post[4], -1, fill(1)),
        below,
        above,
    ]
    return [post[0]] + [chosen(bits, moved[i], post, i) for i in range(1, 7)]


def set_ghosts(ghost_ref, y_refs):
    for side in range(2):
        ghost_ref[pl.ds(side * PLANE, PLANE), :] = read_field(y_refs[side], NORM)


def collide_face(msg, names, conc, put):
    rho, vx, vy, vz = (read_field(msg, k) for k in range(RHO, RHO + 4))
    vz, base = lifted(conc, vx, vy, vz)
    for k, which in enumerate(names):
        put(which, relax(read_field(msg, k), which, rho, vx, vy, vz, base))


def collide_y_halos(post_ref, open_ref, y_refs, z_refs, flow_ref):
    row = row_ids(PLANE) % B
    for side in range(2):
        msg = y_refs[side]
        own = face_rows(post_ref, (0, B - 1)[side], (4, 3)[side])
        conc = read_field(msg, PART)
        conc = conc + jnp.where(get_open(open_ref, 0, side), own, read_field(msg, NORM))
        if z_refs is not None:
            ends = jnp.where(
                row == 0,
                spread8(read_diag(z_refs[0], side, TRANS)),
                spread8(read_diag(z_refs[1], side, TRANS)),
            )
            ends = jnp.where(get_open(open_ref, 1, side), ends, read_field(msg, TRANS))
            conc = conc + ends
        at = PADDED + (7, 24)[side]

        def put(which, v):
            for tile in range(2):
                part = v[tile * B : (tile + 1) * B]
                if z_refs is None:
                    flow_ref[which, pl.ds(at + tile * 32, B, stride=PADDED), :] = part
                else:
                    for z in (0, B - 1):
                        flow_ref[which, pl.ds(at + tile * 32 + z * PADDED, 1), :] = part[z : z + 1]

        collide_face(msg, (Y_UP, Y_DN)[side], conc, put)


def collide_z_halos(post_ref, open_ref, y_refs, z_refs, flow_ref):
    row = row_ids(PLANE) % B
    for side in range(2):
        msg = z_refs[side]
        own = plane(post_ref, (0, B - 1)[side], (6, 5)[side])
        ends = jnp.where(
            row == 0, spread8(read_diag(msg, 0, NORM)), spread8(read_diag(msg, 1, NORM))
        )
        ends = jnp.where(get_open(open_ref, 3, side), ends, read_field(msg, TRANS))
        conc = read_field(msg, PART)
        conc = conc + jnp.where(get_open(open_ref, 2, side), own, read_field(msg, NORM))
        conc = conc + jnp.where((row == 0) | (row == B - 1), ends, 0.0)
        zz = (0, B + 1)[side]
        collide_face(
            msg, (Z_UP, Z_DN)[side], conc, lambda which, v: put_padded(flow_ref, which, zz, v)
        )
    for y_side in range(2):
        for z_side in range(2):
            which = DIRS.index((0, 1 - 2 * y_side, 1 - 2 * z_side))
            names = (Y_UP, Y_DN)[y_side]
            msg = z_refs[z_side]
            z_row = (0, B - 1)[z_side]
            y_row = (0, B - 1)[y_side]
            from_y = read_row(y_refs[y_side], TRANS, z_row)
            from_z = read_row(msg, TRANS, y_row)
            get = [read_diag(msg, y_side, f) for f in range(TRANS + 1)]
            for tile in range(2):
                open_y = open_ref[pl.ds(open_at(1, y_side, tile) + z_row, 1), :]
                open_z = open_ref[pl.ds(open_at(3, z_side, tile) + y_row, 1), :]
                conc = get[PART][tile]
                conc = conc + jnp.where(open_y > 0, from_y[tile], get[TRANS][tile])
                conc = conc + jnp.where(open_z > 0, from_z[tile], get[NORM][tile])
                rho, vx, vy, vz = (get[k][tile] for k in range(RHO, RHO + 4))
                vz, base = lifted(conc, vx, vy, vz)
                v = relax(get[names.index(which)][tile], which, rho, vx, vy, vz, base)
                at = (0, B + 1)[z_side] * PADDED + tile * 32 + (7, 24)[y_side]
                flow_ref[which, pl.ds(at, 1), :] = v[:1]


def collide_flow(z, pops_refs, aux_ref, bits, conc, flow_ref):
    porous = jnp.where(is_open(bits, 0), 1.0, 0.0)
    rho, vx, vy, vz = (plane(aux_ref, z, k) for k in range(4))
    vz = vz + porous * (FORCE_GAIN * (conc - REST_CONC))
    base = 1.0 - 1.5 * (vx * vx + vy * vy + vz * vz)
    omega = OMEGA_FLOW * porous
    keep = 1.0 - omega
    scaled = omega * rho
    v = keep * flow_plane(pops_refs, z, 0) + (WEIGHTS[0] * scaled) * base
    put_padded(flow_ref, 0, z + 1, v)
    for i, j in PAIRS:
        a = along(i, vx, vy, vz)
        scale = WEIGHTS[i] * scaled
        even = scale * (base + 4.5 * (a * a))
        odd = scale * (3.0 * a)
        put_padded(flow_ref, i, z + 1, keep * flow_plane(pops_refs, z, i) + (even + odd))
        put_padded(flow_ref, j, z + 1, keep * flow_plane(pops_refs, z, j) + (even - odd))


def stream_flow(z, bits, flow_ref):
    post = [padded_plane(flow_ref, z + 1, 0, i) for i in range(19)]
    out = [post[0]]
    for which in range(1, 19):
        cx, cy, cz = DIRS[which]
        moved = post[which]
        if cy or cz:
            moved = padded_plane(flow_ref, z + 1 - cz, cy, which)
        if cx:
            moved = ring(moved, cx)
        out.append(chosen(bits, moved, post, which))
    return out


def first_kernel(
    dense_ref, right_ref, left_ref, pops_ref, side_ref, aux_ref, ring_ref,
    post_ref, ydn_ref, yup_ref, zdn_ref, zup_ref, turn_ref,
):
    turn_ref[pl.ds(0, BLOCKROWS // 8, stride=8), :] = right_ref[...]
    turn_ref[pl.ds(7, BLOCKROWS // 8, stride=8), :] = left_ref[...]
    lane = lanes(8)
    near = (lane < W) | (lane >= L - W)

    def body(z, carry):
        solute = []
        for i in range(7):
            at = pl.multiple_of(i * 256 + z * B, B)
            side = [
                jnp.where(near, turn_blocks(turn_ref[pl.ds(at + 8 * k, 8), :]), 0.0)
                for k in range(2)
            ]
            solute.append(jnp.concatenate([dense_ref[pl.ds(at, B), :]] + side, axis=0))
        post = solute_collide(solute, [plane(aux_ref, z, k) for k in range(1, 4)])
        for i in range(7):
            post_ref[i, pl.ds(pl.multiple_of(z * PLANE, PLANE), PLANE), :] = post[i]
        return carry

    lax.fori_loop(0, B, body, 0)
    pops_refs = pops_ref, side_ref
    write_y_messages(pops_refs, post_ref, aux_ref, (ydn_ref, yup_ref), ring_ref=ring_ref)
    write_z_messages(pops_refs, post_ref, aux_ref, (zdn_ref, zup_ref), ring_ref=ring_ref)


def pull(z, refs, bits_ref, flow_ref, solute_ref):
    pops_ref, side_ref, post_ref, aux_ref = refs
    at = pl.ds(pl.multiple_of(z * PLANE, PLANE), PLANE)
    main = pl.ds(pl.multiple_of(z * B, B), B)
    bits = bits_ref[at, :]
    pops = stream_flow(z, bits, flow_ref)
    for i in range(19):
        pops_ref[i, main, :] = pops[i][:B]
        if side_ref is not None:
            side_ref[i, main, :] = pops[i][B:]
    if side_ref is None:
        return
    rho, velocity = moments(pops, jnp.where(is_open(bits, 0), 1.0, 0.0))
    for k, v in enumerate([rho] + velocity):
        aux_ref[k, at, :] = v
    post = solute_collide([solute_ref[i, at, :] for i in range(7)], velocity)
    for i in range(7):
        post_ref[i, at, :] = post[i]


def push(z, refs, bits, solute, flow_ref, solute_ref, turn_ref):
    pops_ref, side_ref, post_ref, aux_ref = refs
    for i in range(7):
        if turn_ref is None:
            solute_ref[i, pl.ds(pl.multiple_of(z * PLANE, PLANE), PLANE), :] = solute[i]
        else:
            for half in range(2):
                at = pl.multiple_of(i * 256 + z * B + half * 8, 8)
                turn_ref[pl.ds(at, 8), :] = turn_blocks(solute[i][half * 8 : half * 8 + 8])
    collide_flow(z, (pops_ref, side_ref), aux_ref, bits, sum(solute), flow_ref)


def inner_kernel(last, *refs):
    pops_in, side_in, post_in, aux_in, bits_ref, open_ref, ylo_ref, yhi_ref = refs[:8]
    if last:
        pops_ref, flow_ref, turn_ref, ghost_ref = refs[8:]
        state, out = (pops_ref, side_in, post_in, aux_in), (pops_ref, None, None, None)
        solute_ref = None
    else:
        pops_ref, side_ref, post_ref, aux_ref, flow_ref, solute_ref, ghost_ref = refs[8:]
        state = out = (pops_ref, side_ref, post_ref, aux_ref)
        turn_ref = None
    set_ghosts(ghost_ref, (ylo_ref, yhi_ref))
    collide_y_halos(state[2], open_ref, (ylo_ref, yhi_ref), None, flow_ref)

    def first(z, carry):
        bits = plane(bits_ref, z)
        post_ref = state[2]
        solute = stream_solute(
            z, post_ref, bits, ghost_ref, plane(post_ref, z - 1, 5), plane(post_ref, z + 1, 6)
        )
        push(z, state, bits, solute, flow_ref, solute_ref, turn_ref)
        return carry

    def second(z, carry):
        pull(z, out, bits_ref, flow_ref, solute_ref)
        return carry

    lax.fori_loop(1, B - 1, first, 0)
    lax.fori_loop(2, B - 2, second, 0)


def edge_kernel(last, *refs):
    if last:
        slot_ref, refs = refs[0], refs[1:]
    pops_in, side_in, post_in, aux_in, flow_in, solute_ref, bits_ref, open_ref = refs[:8]
    y_refs, z_refs = refs[8:10], refs[10:12]
    if last:
        pops_ref, flow_ref, turn_ref, send_ref, ghost_ref = refs[12:]
        state, out = (pops_ref, side_in, post_in, aux_in), (pops_ref, None, None, None)
    else:
        pops_ref, side_ref, post_ref, aux_ref, flow_ref, ydn_ref, yup_ref, ghost_ref = refs[12:]
        state = out = (pops_ref, side_ref, post_ref, aux_ref)
        turn_ref = None
    set_ghosts(ghost_ref, y_refs)
    post_ref = state[2]
    collide_y_halos(post_ref, open_ref, y_refs, z_refs, flow_ref)
    collide_z_halos(post_ref, open_ref, y_refs, z_refs, flow_ref)
    for z in (0, B - 1):
        bits = plane(bits_ref, z)
        below = read_field(z_refs[0], NORM) if z == 0 else plane(post_ref, z - 1, 5)
        above = read_field(z_refs[1], NORM) if z == B - 1 else plane(post_ref, z + 1, 6)
        solute = stream_solute(z, post_ref, bits, ghost_ref, below, above)
        push(z, state, bits, solute, flow_ref, solute_ref, turn_ref)

    def second(k, carry):
        pull(k + 12 * (k // 2), out, bits_ref, flow_ref, solute_ref)
        return carry

    lax.fori_loop(0, 4, second, 0)
    if not last:
        write_y_messages(
            (pops_ref, side_ref), post_ref, aux_ref, (ydn_ref, yup_ref), bits_ref=bits_ref
        )
        return
    for owner in range(8):
        tile = jnp.int32(0)
        for j in range(8):
            slot = slot_ref[0, 0, j]
            tile = jnp.where((slot >= 0) & (slot // 8 == owner), j, tile)
        send_ref[owner] = turn_ref[pl.ds(tile, BLOCKROWS // 8, stride=8), :]


def z_kernel(pops_ref, side_ref, post_ref, aux_ref, bits_ref, zdn_ref, zup_ref):
    write_z_messages(
        (pops_ref, side_ref), post_ref, aux_ref, (zdn_ref, zup_ref), bits_ref=bits_ref
    )


def scatter_kernel(slot_ref, recv_ref, out_ref):
    for s in range(8):
        home = slot_ref[s]
        block = recv_ref[jnp.maximum(home, 0) // 8]
        out_ref[pl.ds(s, BLOCKROWS // 8, stride=8), :] = jnp.where(home >= 0, block, 0.0)


def neighbours(low, high, axis):
    count = lax.axis_size(axis)
    up = [(i, (i + 1) % count) for i in range(count)]
    down = [(i, (i - 1) % count) for i in range(count)]
    return lax.ppermute(high, axis, up), lax.ppermute(low, axis, down)


def inside():
    flags = []
    for axis in ("gx", "gy", "gz"):
        at = lax.axis_index(axis)
        flags += [at > 0, at < lax.axis_size(axis) - 1]
    return jnp.stack(flags).astype(F32)


def with_edges(face, halos, row):
    slabs = face.shape[0] // B
    rows = [face] + [halo.reshape(slabs, B, L)[:, row] for halo in halos]
    pad = -slabs * (B + 2) % 8
    return jnp.concatenate(rows + [jnp.zeros((pad, L), F32)], axis=0)


def exchange_z(halos, zdn, zup):
    return neighbours(with_edges(zdn, halos, 0), with_edges(zup, halos, B - 1), "gz")


def shards(populations, solute_state, pore_mask, block_slot, slot_block):
    flags = inside()
    state = solute_state.reshape(7, 8, 32, L).transpose(0, 2, 1, 3).reshape(BLOCKROWS, L)
    send = call(gather_kernel, shape(8, 224, L), [SMEM, VMEM], [], 1, 2 * 10**6)(slot_block, state)
    recv = lax.all_to_all(send, "gz", split_axis=0, concat_axis=0, tiled=True)

    pops = populations.reshape(19, 256, L)
    mask = pore_mask.reshape(256, L)
    low, high = call(columns_kernel, (shape(320, L),) * 2, [VMEM] * 2, [], 10**7, 3 * 10**6)(
        pops, mask
    )
    left, right = neighbours(low, high, "gx")
    side, ring_mask, aux = call(
        ring_kernel,
        (shape(19, 256, L), shape(ROWS, L), shape(4, ROWS, L)),
        [SMEM] + [VMEM] * 4,
        [],
        10**7,
        10**7,
    )(flags, pops, mask, right, left)

    def block_of(tile):
        owner = jnp.maximum(block_slot[0, 0, tile], 0) // 8
        return lax.dynamic_index_in_dim(recv, owner, 0, keepdims=False)

    left, right = neighbours(block_of(0), block_of(7), "gx")
    turn = pltpu.VMEM((BLOCKROWS, L), F32)
    dense = call(spread_kernel, shape(BLOCKROWS, L), [SMEM, VMEM], [turn], 10**7, 2 * 10**6)(
        block_slot, recv
    )
    message = shape((SIDES + MASK + 1) * B, L)
    post, ydn, yup, zdn, zup = call(
        first_kernel, (shape(7, ROWS, L),) + (message,) * 4, [VMEM] * 7, [turn], 10**7, 10**7
    )(dense, right, left, pops, side, aux, ring_mask)

    ghost = pltpu.VMEM((2 * PLANE, L), F32)
    states = (held(19, 256, L), held(19, 256, L), held(7, ROWS, L), held(4, ROWS, L))
    flow_out, solute_out = held(19, PADROWS, L), held(7, ROWS, L)
    bits_out, open_out = held(ROWS, L, dtype=jnp.int32), held(PLANE * 8, L)
    message = held((SIDES + MASK) * B, L)
    state = (pops, side, post, aux)
    for step in range(STEPS):
        last = step == STEPS - 1
        y_halos = neighbours(ydn, yup, "gy")
        z_halos = exchange_z(y_halos, zdn, zup)
        if step == 0:
            mask, bits, opens = call(
                inner_open_kernel,
                (held(PADROWS, L), bits_out, open_out),
                [SMEM] + [VMEM] * 3,
                [],
                10**7,
                10**6,
                keep=True,
            )(flags, ring_mask, *y_halos)
        if last:
            outs = (states[0], flow_out, held(BLOCKROWS, L))
            aliases = {0: 0}
        else:
            outs = states + (flow_out, solute_out)
            aliases = {0: 0, 1: 1, 2: 2, 3: 3}
        moved = call(
            functools.partial(inner_kernel, last),
            outs,
            [VMEM] * 8,
            [ghost],
            10**8,
            2 * 10**7,
            aliases=aliases,
            keep=True,
        )(*state, bits, opens, *y_halos)
        if step == 0:
            mask, bits, opens = call(
                edge_open_kernel,
                (held(PADROWS, L), bits_out, open_out),
                [SMEM] + [VMEM] * 5,
                [],
                10**6,
                10**6,
                aliases={3: 0, 4: 1, 5: 2},
                keep=True,
            )(flags, *z_halos, mask, bits, opens)
        if last:
            pops, flow, turned = moved
            pops, flow, turned, send = call(
                functools.partial(edge_kernel, True),
                (states[0], flow_out, held(BLOCKROWS, L), shape(8, 224, L)),
                [SMEM] + [VMEM] * 12,
                [ghost],
                10**7,
                10**7,
                aliases={1: 0, 5: 1, 6: 2},
                keep=True,
            )(block_slot, pops, *state[1:], flow, turned, bits, opens, *y_halos, *z_halos)
            break
        *state, flow, solute = moved
        *state, flow, ydn, yup = call(
            functools.partial(edge_kernel, False),
            states + (flow_out, message, message),
            [VMEM] * 12,
            [ghost],
            10**7,
            10**7,
            aliases={0: 0, 1: 1, 2: 2, 3: 3, 4: 4},
            keep=True,
        )(*state, flow, solute, bits, opens, *y_halos, *z_halos)
        zdn, zup = call(
            z_kernel, (message, message), [VMEM] * 5, [], 10**6, 10**6, keep=True
        )(*state, bits)

    recv = lax.all_to_all(send, "gz", split_axis=0, concat_axis=0, tiled=True)
    out = call(scatter_kernel, shape(BLOCKROWS, L), [SMEM, VMEM], [], 1, 2 * 10**6)(
        slot_block, recv
    )
    new_solute = out.reshape(7, 32, 8, L).transpose(0, 2, 1, 3).reshape(7, 8, 4096)
    return pops.reshape(19, B, B, L), new_solute


def solution(mesh):
    in_specs = (
        P(None, "gz", "gy", "gx"),
        P(None, ("gx", "gy", "gz"), None),
        P("gz", "gy", "gx"),
        P("gz", "gy", "gx"),
        P(("gx", "gy", "gz")),
    )
    out_specs = (P(None, "gz", "gy", "gx"), P(None, ("gx", "gy", "gz"), None))
    return jax.shard_map(shards, mesh=mesh, in_specs=in_specs, out_specs=out_specs, check_vma=False)
```

time: 196 us -> 150 us (0.77)
  Pallas kernels: 71.2 us -> 48.4 us
  waiting for transfers between devices: 58.3 us -> 46.2 us
  local copies, waits for them, and re-layouts: 15.9 us -> 7.68 us
  other arithmetic: 6.31 us -> 0.42 us
    ppermute x26 -> x20, waiting for transfers between devices: 42 us -> 9.33 us  [neighbours(): return (lax.ppermute(high, axis, up), lax.ppermute(low, axis, down))]
    pallas_call x9 -> x17, Pallas kernels: 68 us -> 45 us  [the longest x13 27.3 us: placed(): run(*(pltpu.with_memory_space_constraint(x, pltpu.VMEM) if spec is VMEM e...]
    all_to_all x2, waiting for transfers between devices: 16.3 us -> 36.9 us  [shards(): recv = lax.all_to_all(send, 'gz', split_axis=0, concat_axis=0, tiled=True)]
    concatenate x4 -> x2, local copies, waits for them, and re-layouts: 4.67 us -> 0.15 us  [with_edges(): return jnp.concatenate(rows + [jnp.zeros((pad, L), F32)], axis=0)]
    unnamed x36 -> x26, local copies, waits for them, and re-layouts: 9.58 us -> 5.98 us
    mul x6 -> x0, other arithmetic: 3.05 us -> none  [the longest x2 1.83 us: padded_mask(): side = jnp.concatenate([right * has_right, gap, left * has_left], axis=2)]
    ppermute x26 -> x20, starting transfers between devices: 29.2 us -> 30.3 us  [neighbours(): return (lax.ppermute(high, axis, up), lax.ppermute(low, axis, down))]
  transfers between devices with their start and end apart: 28 -> 22, of which waited for: 20 -> 6; matrix products, arithmetic and copies ran while one was open for 5% -> 3% of each run, Pallas kernels for 14% -> 23%
where the time goes in v1:
time: 150 us; the launch traced here: 147 us
  Pallas kernels  48.4 us (32%)
  waiting for transfers between devices  46.2 us (31%)
  starting transfers between devices  42.1 us (28%)
  local copies, waits for them, and re-layouts  7.68 us (5%)
  between operations  2.4 us (2%)
    all_to_all x2, waiting for transfers between devices, shards(): recv = lax.all_to_all(send, 'gz', split_axis=0, concat_axis=0, tiled=True)  36.9 us
    ppermute x20, starting transfers between devices, neighbours(): return (lax.ppermute(high, axis, up), lax.ppermute(low, axis, down))  30.3 us
    pallas_call x13, Pallas kernels, placed(): run(*(pltpu.with_memory_space_constraint(x, pltpu.VMEM) if spec is VMEM e...  27.3 us
    all_to_all x2, starting transfers between devices, shards(): recv = lax.all_to_all(send, 'gz', split_axis=0, concat_axis=0, tiled=True)  11.7 us
    ppermute x20, waiting for transfers between devices, neighbours(): return (lax.ppermute(high, axis, up), lax.ppermute(low, axis, down))  9.33 us
    unnamed x26, local copies, waits for them, and re-layouts  5.98 us
    pallas_call x1, Pallas kernels, shards(): call(ring_kernel, (shape(19, 256, L), shape(ROWS, L), shape(4, ROWS, L)),...  5.5 us
    pallas_call x1, Pallas kernels, shards(): call(columns_kernel, (shape(320, L),) * 2, [VMEM] * 2, [], 10 ** 7, 3 * 1...  4.89 us
  transfers between devices with their start and end apart: 22, of which 6 were waited for; matrix products, arithmetic and copies ran while one was open for 3% of the time, Pallas kernels for 23%

profile of v1, /device:TPU:7, one launch (start us, length us, event | category | flops | bytes accessed | tf_op | source)
XLA Modules:
  0.0 147.2 jit_solution(6343922729713966668)
XLA Ops:
  0.6 1.2 copy-done.1
  1.8 0.7 copy-done.4
  2.5 1.8 %shard_map.70 = f32[8,224,128]{2,1,0:T(8,128)} custom-call(s32[8]{0:T(128)S(1)} %copy-done.4, f32[1792,128]{1,0:T(8,128)S(1)} %bitcast.86), custom_call_target="tpu_custom_call" | custom-call | flops 1 | bytes 2000000 | tf_op jit(solution)/shard_map/pallas_call | solution.py:822
  4.2 8.2 %all-to-all-start = ((f32[8,224,128]{2,1,0:T(8,128)}), f32[8,224,128]{2,1,0:T(8,128)S(1)}, u32[]{:S(2)}, u32[]{:S(2)}) async-start(f32[8,224,128]{2,1,0:T(8,128)} %shard_map.70), calls=%async_computation | async-start | bytes 1835008 | tf_op jit(solution)/shard_map/all_to_all | solution.py:823
  12.4 1.7 %copy.135 = f32[19,16,16,128]{3,2,1,0:T(8,128)S(1)} copy(f32[19,16,16,128]{3,2,1,0:T(8,128)} %param.5) | data formatting | bytes 4980736
  14.2 4.9 %shard_map.68 = (f32[320,128]{1,0:T(8,128)}, f32[320,128]{1,0:T(8,128)}) custom-call(f32[19,256,128]{2,1,0:T(8,128)S(1)} %bitcast.79, s32[256,128]{1,0:T(8,128)S(1)} %bitcast.87), custom_call_target="tpu_custom_call" | custom-call | flops 10000000 | bytes 3000000 | tf_op jit(solution)/shard_map/pallas_call | solution.py:827
  19.1 2.7 %collective-permute-start = (f32[320,128]{1,0:T(8,128)}, f32[320,128]{1,0:T(8,128)}, u32[]{:S(2)}, u32[]{:S(2)}) collective-permute-start(f32[320,128]{1,0:T(8,128)} %get-tuple-element.64), channel_id=1, source_target_pairs={{0,192},{64,0},{128,64},{192,128},{1,193},{65,1},{129,65},{193,129... | collective-permute-start | bytes 491528 | tf_op jit(solution)/shard_map/ppermute | solution.py:797
  21.8 0.0 collective-permute-start.1
  21.8 0.6 fusion.8
  23.8 15.1 %all-to-all-done.recv_ref = f32[8,224,128]{2,1,0:T(8,128)S(1)} async-done(((f32[8,224,128]{2,1,0:T(8,128)}), f32[8,224,128]{2,1,0:T(8,128)S(1)}, u32[]{:S(2)}, u32[]{:S(2)}) %all-to-all-start) | async-done | bytes 917536 | tf_op jit(solution)/shard_map/all_to_all | solution.py:823
  38.8 0.7 dynamic-slice_bitcast_fusion
  39.5 2.7 %collective-permute-start.2 = (f32[224,128]{1,0:T(8,128)}, f32[224,128]{1,0:T(8,128)}, u32[]{:S(2)}, u32[]{:S(2)}) collective-permute-start(f32[224,128]{1,0:T(8,128)} %get-tuple-element.127), channel_id=1, source_target_pairs={{0,192},{64,0},{128,64},{192,128},{1,193},{65,1},{129,65},{193,129... | collective-permute-start | bytes 344072 | tf_op jit(solution)/shard_map/ppermute | solution.py:797
  42.2 0.0 collective-permute-start.3
  42.2 0.1 stack.27
  42.4 0.0 collective-permute-done.right_ref
  42.4 5.5 %shard_map.69 = (f32[19,256,128]{2,1,0:T(8,128)S(1)}, f32[512,128]{1,0:T(8,128)S(1)}, f32[4,512,128]{2,1,0:T(8,128)S(1)}) custom-call(f32[6]{0:T(128)S(1)} %convert_element_type.3.flag_ref, f32[19,256,128]{2,1,0:T(8,128)S(1)} %bitcast.80, s32[256,128]{1,0:T(8,128)S(1)} %bitcast.88, f32[320,128]{1,0:T(8,128)} %collective-permute-done.right_ref, ...), custom_call_target="tpu_custom_call" | custom-call | flops 10000000 | bytes 10000000 | tf_op jit(solution)/shard_map/pallas_call | solution.py:831
  47.9 3.0 %shard_map.71.dense_ref = f32[1792,128]{1,0:T(8,128)S(1)} custom-call(s32[1,1,8]{2,1,0:T(1,128)S(1)} %copy-done.3, f32[8,224,128]{2,1,0:T(8,128)S(1)} %all-to-all-done.recv_ref), custom_call_target="tpu_custom_call" | custom-call | flops 10000000 | bytes 2000000 | tf_op jit(solution)/shard_map/pallas_call | solution.py:846
  50.9 4.2 %shard_map.72 = (f32[7,512,128]{2,1,0:T(8,128)S(1)}, f32[240,128]{1,0:T(8,128)S(1)}, f32[240,128]{1,0:T(8,128)S(1)}, f32[240,128]{1,0:T(8,128)S(1)}, f32[240,128]{1,0:T(8,128)S(1)}) custom-call(f32[1792,128]{1,0:T(8,128)S(1)} %shard_map.71.dense_ref, f32[224,128]{1,0:T(8,128)} %collective-permute-done.2.right_ref, ...), custom_call_target="tpu_custom_call" | custom-call | flops 10000000 | bytes 10000000 | tf_op jit(solution)/shard_map/pallas_call | solution.py:850
  55.2 0.8 collective-permute-start.5
  56.0 0.1 pad.31.clone
  56.0 2.2 %collective-permute-start.4 = (f32[240,128]{1,0:T(8,128)S(1)}, f32[240,128]{1,0:T(8,128)S(1)}, u32[]{:S(2)}, u32[]{:S(2)}) collective-permute-start(f32[240,128]{1,0:T(8,128)S(1)} %get-tuple-element.70), channel_id=1, source_target_pairs={{0,8},{8,16},{16,24},{24,32},{32,40},{40,48},{48,56},{56,0},{1,9},... | collective-permute-start | bytes 368648 | tf_op jit(solution)/shard_map/ppermute | solution.py:797
  58.2 2.5 %collective-permute-done.5.yhi_ref.refs_7_.refs_9_ = f32[240,128]{1,0:T(8,128)S(1)} collective-permute-done((f32[240,128]{1,0:T(8,128)S(1)}, f32[240,128]{1,0:T(8,128)S(1)}, u32[]{:S(2)}, u32[]{:S(2)}) %collective-permute-start.5) | collective-permute-done | bytes 122912 | tf_op jit(solution)/shard_map/ppermute | solution.py:797
  60.8 0.1 maximum_maximum_fusion.1
  60.9 0.1 collective-permute-start.6
  61.0 2.7 %collective-permute-start.7 = (f32[272,128]{1,0:T(8,128)S(1)}, f32[272,128]{1,0:T(8,128)S(1)}, u32[]{:S(2)}, u32[]{:S(2)}) collective-permute-start(f32[272,128]{1,0:T(8,128)S(1)} %get-tuple-element.144), channel_id=1, source_target_pairs={{0,7},{1,0},{2,1},{3,2},{4,3},{5,4},{6,5},{7,6},{8,15},{9,8},{10,9... | collective-permute-start | bytes 417800 | tf_op jit(solution)/shard_map/ppermute | solution.py:797
  63.6 2.3 %shard_map.73 = (f32[1152,128]{1,0:T(8,128)S(1)}, s32[512,128]{1,0:T(8,128)S(1)}, f32[256,128]{1,0:T(8,128)S(1)}) custom-call(f32[6]{0:T(128)S(1)} %convert_element_type.3.flag_ref, f32[512,128]{1,0:T(8,128)S(1)} %get-tuple-element.68.ring_ref, f32[240,128]{1,0:T(8,128)S(1)} %collective-permute-done.4.ylo_ref.refs_6_.refs_8_, ...), custom_call_target="tpu_custom_call" | custom-call | flops 10000000 | bytes 1000000 | tf_op jit(solution)/shard_map/pallas_call | solution.py:73
  66.0 4.2 %shard_map.74 = (f32[19,256,128]{2,1,0:T(8,128)S(1)}, f32[19,256,128]{2,1,0:T(8,128)S(1)}, f32[7,512,128]{2,1,0:T(8,128)S(1)}, f32[4,512,128]{2,1,0:T(8,128)S(1)...) custom-call(f32[19,256,128]{2,1,0:T(8,128)S(1)} %bitcast.82, ...), custom_call_target="tpu_custom_call", output_to_operand_aliasing={{0}: (0, {}), {1}: (1, {}), {2}: (2, {}), {3}: (3, {})} | custom-call | flops 100000000 | bytes 20000000 | tf_op jit(solution)/shard_map/pallas_call | solution.py:73
  70.2 0.9 shard_map.75
  71.0 1.5 shard_map.76
  72.5 0.4 collective-permute-start.9
  72.9 0.1 pad.23.clone
  72.9 3.2 %collective-permute-start.8 = (f32[224,128]{1,0:T(8,128)S(1)}, f32[224,128]{1,0:T(8,128)S(1)}, u32[]{:S(2)}, u32[]{:S(2)}) collective-permute-start(f32[224,128]{1,0:T(8,128)S(1)} %get-tuple-element.89), channel_id=1, source_target_pairs={{0,8},{8,16},{16,24},{24,32},{32,40},{40,48},{48,56},{56,0},{1,9},... | collective-permute-start | bytes 344072 | tf_op jit(solution)/shard_map/ppermute | solution.py:797
  76.2 0.2 shard_map.78
  76.3 2.2 %collective-permute-done.9.refs_7_.refs_9_ = f32[224,128]{1,0:T(8,128)S(1)} collective-permute-done((f32[224,128]{1,0:T(8,128)S(1)}, f32[224,128]{1,0:T(8,128)S(1)}, u32[]{:S(2)}, u32[]{:S(2)}) %collective-permute-start.9) | collective-permute-done | bytes 114720 | tf_op jit(solution)/shard_map/ppermute | solution.py:797
  78.6 0.1 maximum_maximum_fusion.3
  78.7 0.1 collective-permute-start.10
  78.8 2.7 %collective-permute-start.11 = (f32[256,128]{1,0:T(8,128)S(1)}, f32[256,128]{1,0:T(8,128)S(1)}, u32[]{:S(2)}, u32[]{:S(2)}) collective-permute-start(f32[256,128]{1,0:T(8,128)S(1)} %get-tuple-element.150), channel_id=1, source_target_pairs={{0,7},{1,0},{2,1},{3,2},{4,3},{5,4},{6,5},{7,6},{8,15},{9,8},{10,9... | collective-permute-start | bytes 393224 | tf_op jit(solution)/shard_map/ppermute | solution.py:797
  81.5 4.1 %shard_map.77 = (f32[19,256,128]{2,1,0:T(8,128)S(1)}, f32[19,256,128]{2,1,0:T(8,128)S(1)}, f32[7,512,128]{2,1,0:T(8,128)S(1)}, f32[4,512,128]{2,1,0:T(8,128)S(1)...) custom-call(f32[19,256,128]{2,1,0:T(8,128)S(1)} %get-tuple-element.8, ...), custom_call_target="tpu_custom_call", output_to_operand_aliasing={{0}: (0, {}), {1}: (1, {}), {2}: (2, {}), {3}: (3, {})} | custom-call | flops 100000000 | bytes 20000000 | tf_op jit(solution)/shard_map/pallas_call | solution.py:73
  85.7 1.5 shard_map.79
  87.1 0.0 collective-permute-start.13
  87.1 3.6 %collective-permute-start.12 = (f32[224,128]{1,0:T(8,128)S(1)}, f32[224,128]{1,0:T(8,128)S(1)}, u32[]{:S(2)}, u32[]{:S(2)}) collective-permute-start(f32[224,128]{1,0:T(8,128)S(1)} %get-tuple-element.103), channel_id=1, source_target_pairs={{0,8},{8,16},{16,24},{24,32},{32,40},{40,48},{48,56},{56,0},{1,9},... | collective-permute-start | bytes 344072 | tf_op jit(solution)/shard_map/ppermute | solution.py:797
  90.7 0.2 shard_map.81
  90.9 2.3 %collective-permute-done.13.refs_7_.refs_9_ = f32[224,128]{1,0:T(8,128)S(1)} collective-permute-done((f32[224,128]{1,0:T(8,128)S(1)}, f32[224,128]{1,0:T(8,128)S(1)}, u32[]{:S(2)}, u32[]{:S(2)}) %collective-permute-start.13) | collective-permute-done | bytes 114720 | tf_op jit(solution)/shard_map/ppermute | solution.py:797
  93.3 0.1 maximum_maximum_fusion.5
  93.4 0.3 collective-permute-start.14
  93.6 2.7 %collective-permute-start.15 = (f32[256,128]{1,0:T(8,128)S(1)}, f32[256,128]{1,0:T(8,128)S(1)}, u32[]{:S(2)}, u32[]{:S(2)}) collective-permute-start(f32[256,128]{1,0:T(8,128)S(1)} %get-tuple-element.148), channel_id=1, source_target_pairs={{0,7},{1,0},{2,1},{3,2},{4,3},{5,4},{6,5},{7,6},{8,15},{9,8},{10,9... | collective-permute-start | bytes 393224 | tf_op jit(solution)/shard_map/ppermute | solution.py:797
  96.3 4.1 %shard_map.80 = (f32[19,256,128]{2,1,0:T(8,128)S(1)}, f32[19,256,128]{2,1,0:T(8,128)S(1)}, f32[7,512,128]{2,1,0:T(8,128)S(1)}, f32[4,512,128]{2,1,0:T(8,128)S(1)...) custom-call(f32[19,256,128]{2,1,0:T(8,128)S(1)} %get-tuple-element.9, ...), custom_call_target="tpu_custom_call", output_to_operand_aliasing={{0}: (0, {}), {1}: (1, {}), {2}: (2, {}), {3}: (3, {})} | custom-call | flops 100000000 | bytes 20000000 | tf_op jit(solution)/shard_map/pallas_call | solution.py:73
  100.5 1.5 shard_map.82
  101.9 0.0 collective-permute-start.17
  101.9 3.5 %collective-permute-start.16 = (f32[224,128]{1,0:T(8,128)S(1)}, f32[224,128]{1,0:T(8,128)S(1)}, u32[]{:S(2)}, u32[]{:S(2)}) collective-permute-start(f32[224,128]{1,0:T(8,128)S(1)} %get-tuple-element.117), channel_id=1, source_target_pairs={{0,8},{8,16},{16,24},{24,32},{32,40},{40,48},{48,56},{56,0},{1,9},... | collective-permute-start | bytes 344072 | tf_op jit(solution)/shard_map/ppermute | solution.py:797
  105.5 0.2 shard_map.84
  105.6 2.3 %collective-permute-done.17.refs_7_.refs_10_ = f32[224,128]{1,0:T(8,128)S(1)} collective-permute-done((f32[224,128]{1,0:T(8,128)S(1)}, f32[224,128]{1,0:T(8,128)S(1)}, u32[]{:S(2)}, u32[]{:S(2)}) %collective-permute-start.17) | collective-permute-done | bytes 114720 | tf_op jit(solution)/shard_map/ppermute | solution.py:797
  108.0 0.1 maximum_maximum_fusion.7
  108.1 0.1 collective-permute-start.18
  108.2 2.7 %collective-permute-start.19 = (f32[256,128]{1,0:T(8,128)S(1)}, f32[256,128]{1,0:T(8,128)S(1)}, u32[]{:S(2)}, u32[]{:S(2)}) collective-permute-start(f32[256,128]{1,0:T(8,128)S(1)} %get-tuple-element.146), channel_id=1, source_target_pairs={{0,7},{1,0},{2,1},{3,2},{4,3},{5,4},{6,5},{7,6},{8,15},{9,8},{10,9... | collective-permute-start | bytes 393224 | tf_op jit(solution)/shard_map/ppermute | solution.py:797
  110.9 4.7 %shard_map.83 = (f32[19,256,128]{2,1,0:T(8,128)S(1)}, f32[19,1152,128]{2,1,0:T(8,128)S(1)}, f32[1792,128]{1,0:T(8,128)S(1)}) custom-call(f32[19,256,128]{2,1,0:T(8,128)S(1)} %get-tuple-element.113.refs_0_.pops_ref, f32[19,256,128]{2,1,0:T(8,128)S(1)} %get-tuple-element.114.refs_1_.side_ref.refs_2_, ...), custom_call_target="tpu_custom_call", output_to_operand_aliasing={{0}: (0, {})} | custom-call | flops 100000000 | bytes 20000000 | tf_op jit(solution)/shard_map/pallas_call | solution.py:73
  115.6 2.1 %shard_map.85 = (f32[19,256,128]{2,1,0:T(8,128)S(1)}, f32[19,1152,128]{2,1,0:T(8,128)S(1)}, f32[1792,128]{1,0:T(8,128)S(1)}, f32[8,224,128]{2,1,0:T(8,128)S(1)}) custom-call(s32[1,1,8]{2,1,0:T(1,128)S(1)} %copy-done.3, f32[19,256,128]{2,1,0:T(8,128)S(1)} %get-tuple-element.119.refs_1_, ...), custom_call_target="tpu_custom_call", output_to_operand_aliasing={{0}: (1, {}), {1}: (5, {}), {2}: (6, {})} | custom-call | flops 10000000 | bytes 10000000 | tf_op jit(solution)/shard_map/pallas_call | solution.py:73
  117.7 0.0 copy-start
  117.7 0.9 copy-done
  118.7 3.6 %all-to-all-start.1 = ((f32[8,224,128]{2,1,0:T(8,128)}), f32[8,224,128]{2,1,0:T(8,128)S(1)}, u32[]{:S(2)}, u32[]{:S(2)}) async-start(f32[8,224,128]{2,1,0:T(8,128)} %copy-done), calls=%async_computation.1 | async-start | bytes 1835008 | tf_op jit(solution)/shard_map/all_to_all | solution.py:929
  122.2 0.0 copy-start.5
  122.2 1.5 copy.136
  123.7 21.8 %all-to-all-done.1.recv_ref = f32[8,224,128]{2,1,0:T(8,128)S(1)} async-done(((f32[8,224,128]{2,1,0:T(8,128)}), f32[8,224,128]{2,1,0:T(8,128)S(1)}, u32[]{:S(2)}, u32[]{:S(2)}) %all-to-all-start.1) | async-done | bytes 917536 | tf_op jit(solution)/shard_map/all_to_all | solution.py:929
  145.5 1.7 %shard_map.86 = f32[1792,128]{1,0:T(8,128)} custom-call(s32[8]{0:T(128)S(1)} %copy-done.5, f32[8,224,128]{2,1,0:T(8,128)S(1)} %all-to-all-done.1.recv_ref), custom_call_target="tpu_custom_call" | custom-call | flops 1 | bytes 2000000 | tf_op jit(solution)/shard_map/pallas_call | solution.py:930
  (47 shorter events, 0.2 us)
Async XLA Ops:
  0.6 1.2 copy-start.1
  1.8 0.7 copy-start.4
  4.2 34.6 %all-to-all-start = ((f32[8,224,128]{2,1,0:T(8,128)}), f32[8,224,128]{2,1,0:T(8,128)S(1)}, u32[]{:S(2)}, u32[]{:S(2)}) async-start(f32[8,224,128]{2,1,0:T(8,128)} %shard_map.70), calls=%async_computation | async-start | bytes 1835008 | tf_op jit(solution)/shard_map/all_to_all | solution.py:823
  12.4 1.8 %copy-start.2 = (s32[16,16,128]{2,1,0:T(8,128)S(1)}, s32[16,16,128]{2,1,0:T(8,128)}, u32[]{:S(2)}) copy-start(s32[16,16,128]{2,1,0:T(8,128)} %param.7) | copy-start | bytes 393220
  14.2 7.6 %copy-start.3 = (s32[1,1,8]{2,1,0:T(1,128)S(1)}, s32[1,1,8]{2,1,0:T(1,128)}, u32[]{:S(2)}) copy-start(s32[1,1,8]{2,1,0:T(1,128)} %refs_0_.1) | copy-start | bytes 100
  19.1 23.3 %collective-permute-start = (f32[320,128]{1,0:T(8,128)}, f32[320,128]{1,0:T(8,128)}, u32[]{:S(2)}, u32[]{:S(2)}) collective-permute-start(f32[320,128]{1,0:T(8,128)} %get-tuple-element.64), channel_id=1, source_target_pairs={{0,192},{64,0},{128,64},{192,128},{1,193},{65,1},{129,65},{193,129... | collective-permute-start | bytes 491528 | tf_op jit(solution)/shard_map/ppermute | solution.py:797
  21.8 20.6 %collective-permute-start.1 = (f32[320,128]{1,0:T(8,128)}, f32[320,128]{1,0:T(8,128)}, u32[]{:S(2)}, u32[]{:S(2)}) collective-permute-start(f32[320,128]{1,0:T(8,128)} %get-tuple-element.65), channel_id=1, source_target_pairs={{0,64},{64,128},{128,192},{192,0},{1,65},{65,129},{129,193},{193,1... | collective-permute-start | bytes 491528 | tf_op jit(solution)/shard_map/ppermute | solution.py:797
  39.5 11.4 %collective-permute-start.2 = (f32[224,128]{1,0:T(8,128)}, f32[224,128]{1,0:T(8,128)}, u32[]{:S(2)}, u32[]{:S(2)}) collective-permute-start(f32[224,128]{1,0:T(8,128)} %get-tuple-element.127), channel_id=1, source_target_pairs={{0,192},{64,0},{128,64},{192,128},{1,193},{65,1},{129,65},{193,129... | collective-permute-start | bytes 344072 | tf_op jit(solution)/shard_map/ppermute | solution.py:797
  42.2 8.7 %collective-permute-start.3 = (f32[224,128]{1,0:T(8,128)}, f32[224,128]{1,0:T(8,128)}, u32[]{:S(2)}, u32[]{:S(2)}) collective-permute-start(f32[224,128]{1,0:T(8,128)} %get-tuple-element.126), channel_id=1, source_target_pairs={{0,64},{64,128},{128,192},{192,0},{1,65},{65,129},{129,193},{193,1... | collective-permute-start | bytes 344072 | tf_op jit(solution)/shard_map/ppermute | solution.py:797
  55.2 5.5 %collective-permute-start.5 = (f32[240,128]{1,0:T(8,128)S(1)}, f32[240,128]{1,0:T(8,128)S(1)}, u32[]{:S(2)}, u32[]{:S(2)}) collective-permute-start(f32[240,128]{1,0:T(8,128)S(1)} %get-tuple-element.71), channel_id=1, source_target_pairs={{0,56},{8,0},{16,8},{24,16},{32,24},{40,32},{48,40},{56,48},{1,57}... | collective-permute-start | bytes 368648 | tf_op jit(solution)/shard_map/ppermute | solution.py:797
  56.0 4.7 %collective-permute-start.4 = (f32[240,128]{1,0:T(8,128)S(1)}, f32[240,128]{1,0:T(8,128)S(1)}, u32[]{:S(2)}, u32[]{:S(2)}) collective-permute-start(f32[240,128]{1,0:T(8,128)S(1)} %get-tuple-element.70), channel_id=1, source_target_pairs={{0,8},{8,16},{16,24},{24,32},{32,40},{40,48},{48,56},{56,0},{1,9},... | collective-permute-start | bytes 368648 | tf_op jit(solution)/shard_map/ppermute | solution.py:797
  60.9 9.3 %collective-permute-start.6 = (f32[272,128]{1,0:T(8,128)S(1)}, f32[272,128]{1,0:T(8,128)S(1)}, u32[]{:S(2)}, u32[]{:S(2)}) collective-permute-start(f32[272,128]{1,0:T(8,128)S(1)} %get-tuple-element.145), channel_id=1, source_target_pairs={{0,1},{1,2},{2,3},{3,4},{4,5},{5,6},{6,7},{7,0},{8,9},{9,10},{10,1... | collective-permute-start | bytes 417800 | tf_op jit(solution)/shard_map/ppermute | solution.py:797
  61.0 9.2 %collective-permute-start.7 = (f32[272,128]{1,0:T(8,128)S(1)}, f32[272,128]{1,0:T(8,128)S(1)}, u32[]{:S(2)}, u32[]{:S(2)}) collective-permute-start(f32[272,128]{1,0:T(8,128)S(1)} %get-tuple-element.144), channel_id=1, source_target_pairs={{0,7},{1,0},{2,1},{3,2},{4,3},{5,4},{6,5},{7,6},{8,15},{9,8},{10,9... | collective-permute-start | bytes 417800 | tf_op jit(solution)/shard_map/ppermute | solution.py:797
  72.5 6.1 %collective-permute-start.9 = (f32[224,128]{1,0:T(8,128)S(1)}, f32[224,128]{1,0:T(8,128)S(1)}, u32[]{:S(2)}, u32[]{:S(2)}) collective-permute-start(f32[224,128]{1,0:T(8,128)S(1)} %get-tuple-element.90), channel_id=1, source_target_pairs={{0,56},{8,0},{16,8},{24,16},{32,24},{40,32},{48,40},{56,48},{1,57}... | collective-permute-start | bytes 344072 | tf_op jit(solution)/shard_map/ppermute | solution.py:797
  72.9 5.7 %collective-permute-start.8 = (f32[224,128]{1,0:T(8,128)S(1)}, f32[224,128]{1,0:T(8,128)S(1)}, u32[]{:S(2)}, u32[]{:S(2)}) collective-permute-start(f32[224,128]{1,0:T(8,128)S(1)} %get-tuple-element.89), channel_id=1, source_target_pairs={{0,8},{8,16},{16,24},{24,32},{32,40},{40,48},{48,56},{56,0},{1,9},... | collective-permute-start | bytes 344072 | tf_op jit(solution)/shard_map/ppermute | solution.py:797
  78.7 6.9 %collective-permute-start.10 = (f32[256,128]{1,0:T(8,128)S(1)}, f32[256,128]{1,0:T(8,128)S(1)}, u32[]{:S(2)}, u32[]{:S(2)}) collective-permute-start(f32[256,128]{1,0:T(8,128)S(1)} %get-tuple-element.151), channel_id=1, source_target_pairs={{0,1},{1,2},{2,3},{3,4},{4,5},{5,6},{6,7},{7,0},{8,9},{9,10},{10,1... | collective-permute-start | bytes 393224 | tf_op jit(solution)/shard_map/ppermute | solution.py:797
  78.8 6.8 %collective-permute-start.11 = (f32[256,128]{1,0:T(8,128)S(1)}, f32[256,128]{1,0:T(8,128)S(1)}, u32[]{:S(2)}, u32[]{:S(2)}) collective-permute-start(f32[256,128]{1,0:T(8,128)S(1)} %get-tuple-element.150), channel_id=1, source_target_pairs={{0,7},{1,0},{2,1},{3,2},{4,3},{5,4},{6,5},{7,6},{8,15},{9,8},{10,9... | collective-permute-start | bytes 393224 | tf_op jit(solution)/shard_map/ppermute | solution.py:797
  87.1 6.1 %collective-permute-start.13 = (f32[224,128]{1,0:T(8,128)S(1)}, f32[224,128]{1,0:T(8,128)S(1)}, u32[]{:S(2)}, u32[]{:S(2)}) collective-permute-start(f32[224,128]{1,0:T(8,128)S(1)} %get-tuple-element.104), channel_id=1, source_target_pairs={{0,56},{8,0},{16,8},{24,16},{32,24},{40,32},{48,40},{56,48},{1,57}... | collective-permute-start | bytes 344072 | tf_op jit(solution)/shard_map/ppermute | solution.py:797
  87.1 6.1 %collective-permute-start.12 = (f32[224,128]{1,0:T(8,128)S(1)}, f32[224,128]{1,0:T(8,128)S(1)}, u32[]{:S(2)}, u32[]{:S(2)}) collective-permute-start(f32[224,128]{1,0:T(8,128)S(1)} %get-tuple-element.103), channel_id=1, source_target_pairs={{0,8},{8,16},{16,24},{24,32},{32,40},{40,48},{48,56},{56,0},{1,9},... | collective-permute-start | bytes 344072 | tf_op jit(solution)/shard_map/ppermute | solution.py:797
  93.4 7.1 %collective-permute-start.14 = (f32[256,128]{1,0:T(8,128)S(1)}, f32[256,128]{1,0:T(8,128)S(1)}, u32[]{:S(2)}, u32[]{:S(2)}) collective-permute-start(f32[256,128]{1,0:T(8,128)S(1)} %get-tuple-element.149), channel_id=1, source_target_pairs={{0,1},{1,2},{2,3},{3,4},{4,5},{5,6},{6,7},{7,0},{8,9},{9,10},{10,1... | collective-permute-start | bytes 393224 | tf_op jit(solution)/shard_map/ppermute | solution.py:797
  93.6 6.8 %collective-permute-start.15 = (f32[256,128]{1,0:T(8,128)S(1)}, f32[256,128]{1,0:T(8,128)S(1)}, u32[]{:S(2)}, u32[]{:S(2)}) collective-permute-start(f32[256,128]{1,0:T(8,128)S(1)} %get-tuple-element.148), channel_id=1, source_target_pairs={{0,7},{1,0},{2,1},{3,2},{4,3},{5,4},{6,5},{7,6},{8,15},{9,8},{10,9... | collective-permute-start | bytes 393224 | tf_op jit(solution)/shard_map/ppermute | solution.py:797
  101.9 6.0 %collective-permute-start.17 = (f32[224,128]{1,0:T(8,128)S(1)}, f32[224,128]{1,0:T(8,128)S(1)}, u32[]{:S(2)}, u32[]{:S(2)}) collective-permute-start(f32[224,128]{1,0:T(8,128)S(1)} %get-tuple-element.118), channel_id=1, source_target_pairs={{0,56},{8,0},{16,8},{24,16},{32,24},{40,32},{48,40},{56,48},{1,57}... | collective-permute-start | bytes 344072 | tf_op jit(solution)/shard_map/ppermute | solution.py:797
  101.9 6.0 %collective-permute-start.16 = (f32[224,128]{1,0:T(8,128)S(1)}, f32[224,128]{1,0:T(8,128)S(1)}, u32[]{:S(2)}, u32[]{:S(2)}) collective-permute-start(f32[224,128]{1,0:T(8,128)S(1)} %get-tuple-element.117), channel_id=1, source_target_pairs={{0,8},{8,16},{16,24},{24,32},{32,40},{40,48},{48,56},{56,0},{1,9},... | collective-permute-start | bytes 344072 | tf_op jit(solution)/shard_map/ppermute | solution.py:797
  108.1 7.5 %collective-permute-start.18 = (f32[256,128]{1,0:T(8,128)S(1)}, f32[256,128]{1,0:T(8,128)S(1)}, u32[]{:S(2)}, u32[]{:S(2)}) collective-permute-start(f32[256,128]{1,0:T(8,128)S(1)} %get-tuple-element.147), channel_id=1, source_target_pairs={{0,1},{1,2},{2,3},{3,4},{4,5},{5,6},{6,7},{7,0},{8,9},{9,10},{10,1... | collective-permute-start | bytes 393224 | tf_op jit(solution)/shard_map/ppermute | solution.py:797
  108.2 7.4 %collective-permute-start.19 = (f32[256,128]{1,0:T(8,128)S(1)}, f32[256,128]{1,0:T(8,128)S(1)}, u32[]{:S(2)}, u32[]{:S(2)}) collective-permute-start(f32[256,128]{1,0:T(8,128)S(1)} %get-tuple-element.146), channel_id=1, source_target_pairs={{0,7},{1,0},{2,1},{3,2},{4,3},{5,4},{6,5},{7,6},{8,15},{9,8},{10,9... | collective-permute-start | bytes 393224 | tf_op jit(solution)/shard_map/ppermute | solution.py:797
  117.7 0.9 copy-start
  118.7 26.8 %all-to-all-start.1 = ((f32[8,224,128]{2,1,0:T(8,128)}), f32[8,224,128]{2,1,0:T(8,128)S(1)}, u32[]{:S(2)}, u32[]{:S(2)}) async-start(f32[8,224,128]{2,1,0:T(8,128)} %copy-done), calls=%async_computation.1 | async-start | bytes 1835008 | tf_op jit(solution)/shard_map/all_to_all | solution.py:929
  122.2 23.3 %copy-start.5 = (s32[8]{0:T(128)S(1)}, s32[8]{0:T(128)}, u32[]{:S(2)}) copy-start(s32[8]{0:T(128)} %slot_ref.5) | copy-start | bytes 100

commit v2 on v1

--- a/solution.py
+++ b/solution.py
@@ -41,6 +41,7 @@
 Z_DN = [i for i in range(19) if DIRS[i][2] == -1]
 RHO, VEL, PART, NORM, TRANS, MASK = 5, 6, 9, 10, 11, 12
 SIDES = 2
+UNROLL = 2
 B = 16
 L = 128
 W = 8
@@ -52,30 +53,30 @@
 F32 = jnp.float32
 VMEM = pl.BlockSpec(memory_space=pltpu.VMEM)
 SMEM = pl.BlockSpec(memory_space=pltpu.SMEM)
-
-
-def call(kernel, out_shape, in_specs, scratch, flops, nbytes, aliases={}, keep=False):
+HBM = pl.BlockSpec(memory_space=pltpu.HBM)
+
+
+def call(
+    kernel, out_shape, in_specs, scratch, flops, nbytes, aliases={}, keep=False, out_specs=None
+):
     run = pl.pallas_call(
         kernel,
         out_shape=out_shape,
         in_specs=in_specs,
-        out_specs=jax.tree.map(lambda _: VMEM, out_shape),
+        out_specs=out_specs or jax.tree.map(lambda _: VMEM, out_shape),
         scratch_shapes=scratch,
         input_output_aliases=aliases,
         compiler_params=pltpu.CompilerParams(vmem_limit_bytes=20 * 1024 * 1024),
         cost_estimate=pl.CostEstimate(flops=flops, bytes_accessed=nbytes, transcendentals=0),
     )
 
-    if not keep:
-        return run
+    def place(x, spec):
+        if spec is HBM or (keep and spec is VMEM):
+            return pltpu.with_memory_space_constraint(x, spec.memory_space)
+        return x
 
     def placed(*args):
-        return run(
-            *(
-                pltpu.with_memory_space_constraint(x, pltpu.VMEM) if spec is VMEM else x
-                for x, spec in zip(args, in_specs)
-            )
-        )
+        return run(*map(place, args, in_specs))
 
     return placed
 
@@ -86,6 +87,10 @@
 
 def held(*dims, dtype=F32):
     return pltpu.VMEM(dims, dtype)
+
+
+def stored(*dims, dtype=F32):
+    return pltpu.HBM(dims, dtype)
 
 
 def lanes(rows):
@@ -104,10 +109,6 @@
 
 def halves(main, side):
     return jnp.concatenate([main, side], axis=0)
-
-
-def spread(main, side):
-    return halves(jnp.broadcast_to(main, (B, L)), jnp.broadcast_to(side, (B, L)))
 
 
 def shift_rows(v, step, fill):
@@ -173,27 +174,52 @@
     return jnp.take_along_axis(x, index, axis=axis, mode="promise_in_bounds")
 
 
-def gather_kernel(slot_ref, state_ref, send_ref):
+def send_blocks(pick, blocks_ref, out_ref, hold_ref, sems):
+    copies = []
     for dest in range(8):
+        hold_ref[dest] = blocks_ref[pl.ds(pick(dest), BLOCKROWS // 8, stride=8), :]
+        copies.append(pltpu.make_async_copy(hold_ref.at[dest], out_ref.at[dest], sems.at[dest]))
+        copies[-1].start()
+    return copies
+
+
+def gather_kernel(slot_ref, state_ref, send_ref, blocks_ref, hold_ref, sems):
+    def slot_for(dest):
         slot = jnp.int32(0)
         for s in range(8):
             home = slot_ref[s]
             slot = jnp.where((home >= 0) & (home // 8 == dest), s, slot)
-        send_ref[dest] = state_ref[pl.ds(slot, BLOCKROWS // 8, stride=8), :]
-
-
-def spread_kernel(slot_ref, recv_ref, dense_ref, turn_ref):
+        return slot
+
+    load = pltpu.make_async_copy(state_ref, blocks_ref, sems.at[8])
+    load.start()
+    load.wait()
+    for copy in send_blocks(slot_for, blocks_ref, send_ref, hold_ref, sems):
+        copy.wait()
+
+
+def spread_kernel(slot_ref, recv_ref, *refs):
+    *refs, turn_ref, sems = refs
+    sources, dense_ref, targets = refs[:6], refs[6], refs[7:]
+    loads = [
+        pltpu.make_async_copy(source, target, sems.at[k])
+        for k, (source, target) in enumerate(zip(sources, targets))
+    ]
+    for load in loads:
+        load.start()
     for tile in range(8):
         owner = jnp.maximum(slot_ref[0, 0, tile], 0) // 8
         turn_ref[pl.ds(tile, BLOCKROWS // 8, stride=8), :] = recv_ref[owner]
 
     def body(group, carry):
-        for i in range(16):
-            at = pl.multiple_of(group * 128 + i * 8, 8)
+        for i in range(32):
+            at = pl.multiple_of(group * 256 + i * 8, 8)
             dense_ref[pl.ds(at, 8), :] = turn_blocks(turn_ref[pl.ds(at, 8), :])
         return carry
 
-    lax.fori_loop(0, BLOCKROWS // 128, body, 0)
+    lax.fori_loop(0, BLOCKROWS // 256, body, 0)
+    for load in loads:
+        load.wait()
 
 
 def pack_columns(load, low_ref, high_ref, at):
@@ -221,7 +247,7 @@
         )
         return carry
 
-    lax.fori_loop(0, 38, body, 0)
+    lax.fori_loop(0, 38, body, 0, unroll=UNROLL)
     for group in range(2):
         pack_columns(
             lambda i: mask_ref[rows(group * 128, i), :].astype(F32),
@@ -239,7 +265,7 @@
 
 def ring_kernel(
     flag_ref, pops_ref, mask_ref, right_ref, left_ref,
-    side_ref, ring_ref, aux_ref,
+    side_ref, ring_ref, aux_ref, mask_out, bits_ref,
 ):
     def body(group, carry):
         at = pl.ds(pl.multiple_of(group * 8, 8), 8)
@@ -249,7 +275,7 @@
             side_ref[group // 2, pl.ds(row, 8), :] = unpack_columns(right, left, i)
         return carry
 
-    lax.fori_loop(0, 38, body, 0)
+    lax.fori_loop(0, 38, body, 0, unroll=UNROLL)
     lane = lanes(8)
     inside = jnp.where(lane < W, flag_ref[1], jnp.where(lane >= L - W, flag_ref[0], 0.0))
     for group in range(2):
@@ -259,18 +285,29 @@
             row = z * PLANE + (i % 2) * 8
             ring_ref[pl.ds(row, 8), :] = mask_ref[pl.ds(group * 128 + i * 8, 8), :].astype(F32)
             ring_ref[pl.ds(row + B, 8), :] = unpack_columns(right, left, i) * inside
+    mask_out[...] = jnp.zeros_like(mask_out)
+    for z in range(B):
+        put_rows(mask_out, z + 1, ring_ref[pl.ds(z * PLANE, PLANE), :])
+
     def flow(z, carry):
+        set_bits(mask_out, bits_ref, z)
         pops = [flow_plane((pops_ref, side_ref), z, i) for i in range(19)]
         rho, velocity = moments(pops, plane(ring_ref, z))
         for k, v in enumerate([rho] + velocity):
             aux_ref[k, pl.ds(pl.multiple_of(z * PLANE, PLANE), PLANE), :] = v
         return carry
 
-    lax.fori_loop(0, B, flow, 0)
+    lax.fori_loop(0, B, flow, 0, unroll=UNROLL)
 
 
 def plane(ref, z, *lead):
     return ref[(*lead, pl.ds(pl.multiple_of(z * PLANE, PLANE), PLANE), slice(None))]
+
+
+def put_face(ref, row, v, *lead):
+    for tile in range(2):
+        at = pl.ds(tile * B + row, B, stride=PLANE)
+        ref[(*lead, at, slice(None))] = v[tile * B : (tile + 1) * B]
 
 
 def flow_plane(refs, z, which):
@@ -323,25 +360,30 @@
     bits_ref[pl.ds(pl.multiple_of(z * PLANE, PLANE), PLANE), :] = bits
 
 
-def inner_open_kernel(flag_ref, ring_ref, ylo_ref, yhi_ref, mask_ref, bits_ref, open_ref):
-    mask_ref[...] = jnp.zeros_like(mask_ref)
-    for z in range(B):
-        put_rows(mask_ref, z + 1, ring_ref[pl.ds(z * PLANE, PLANE), :])
+def side_open_kernel(
+    flag_ref, ylo_ref, yhi_ref, mask_in, bits_in, mask_ref, bits_ref, open_ref
+):
     for side in range(2):
         halo = read_field((ylo_ref, yhi_ref)[side], MASK) * flag_ref[2 + side]
+        edge, row = ((0, 7), (B - 1, 24))[side]
+        own = []
         for tile in range(2):
             part = halo[tile * B : (tile + 1) * B]
-            edge = PADDED + tile * 32 + (7, 24)[side]
-            inner = PADDED + tile * 32 + (8, 23)[side]
-            mask_ref[pl.ds(edge, B, stride=PADDED), :] = part
-            own = mask_ref[pl.ds(inner, B, stride=PADDED), :]
-            put_open(open_ref, 0, side, tile, part * own)
-
-    def body(z, carry):
-        set_bits(mask_ref, bits_ref, z)
-        return carry
-
-    lax.fori_loop(1, B - 1, body, 0)
+            at = PADDED + tile * 32
+            mask_ref[pl.ds(at + row, B, stride=PADDED), :] = part
+            own.append(mask_ref[pl.ds(at + 8 + edge, B, stride=PADDED), :])
+            put_open(open_ref, 0, side, tile, part * own[tile])
+        own = halves(*own)
+        bits = face_rows(bits_ref, edge)
+        for which in (Y_UP, Y_DN)[side]:
+            cx, _, cz = DIRS[which]
+            source = halo
+            if cz:
+                source = pltpu.roll(source, cz % PLANE, axis=0)
+            if cx:
+                source = ring(source, cx)
+            bits = bits + jnp.where(source * own > 0, 1 << which, 0)
+        put_face(bits_ref, edge, bits)
 
 
 def edge_open_kernel(
@@ -513,28 +555,18 @@
     return vz, 1.0 - 1.5 * (vx * vx + vy * vy + vz * vz)
 
 
-def stream_solute(z, post_ref, bits, ghost_ref, below, above):
-    def fill(side):
-        return spread(
-            ghost_ref[pl.ds(side * PLANE + z, 1), :], ghost_ref[pl.ds(side * PLANE + B + z, 1), :]
-        )
-
+def stream_solute(z, post_ref, bits, fills, below, above):
     post = [plane(post_ref, z, i) for i in range(7)]
     moved = [
         None,
         ring(post[1], 1),
         ring(post[2], -1),
-        shift_rows(post[3], 1, fill(0)),
-        shift_rows(post[4], -1, fill(1)),
+        shift_rows(post[3], 1, fills[0]),
+        shift_rows(post[4], -1, fills[1]),
         below,
         above,
     ]
     return [post[0]] + [chosen(bits, moved[i], post, i) for i in range(1, 7)]
-
-
-def set_ghosts(ghost_ref, y_refs):
-    for side in range(2):
-        ghost_ref[pl.ds(side * PLANE, PLANE), :] = read_field(y_refs[side], NORM)
 
 
 def collide_face(msg, names, conc, put):
@@ -612,23 +644,22 @@
                 flow_ref[which, pl.ds(at, 1), :] = v[:1]
 
 
-def collide_flow(z, pops_refs, aux_ref, bits, conc, flow_ref):
-    porous = jnp.where(is_open(bits, 0), 1.0, 0.0)
-    rho, vx, vy, vz = (plane(aux_ref, z, k) for k in range(4))
-    vz = vz + porous * (FORCE_GAIN * (conc - REST_CONC))
+def collide_flow(load, rho, vx, vy, vz, bits, conc, put):
+    porous = is_open(bits, 0)
+    vz = vz + jnp.where(porous, FORCE_GAIN * (conc - REST_CONC), 0.0)
     base = 1.0 - 1.5 * (vx * vx + vy * vy + vz * vz)
-    omega = OMEGA_FLOW * porous
-    keep = 1.0 - omega
-    scaled = omega * rho
-    v = keep * flow_plane(pops_refs, z, 0) + (WEIGHTS[0] * scaled) * base
-    put_padded(flow_ref, 0, z + 1, v)
+    keep = 1.0 - OMEGA_FLOW
+    scaled = OMEGA_FLOW * rho
+    f = load(0)
+    put(0, jnp.where(porous, keep * f + (WEIGHTS[0] * scaled) * base, f))
     for i, j in PAIRS:
         a = along(i, vx, vy, vz)
         scale = WEIGHTS[i] * scaled
         even = scale * (base + 4.5 * (a * a))
         odd = scale * (3.0 * a)
-        put_padded(flow_ref, i, z + 1, keep * flow_plane(pops_refs, z, i) + (even + odd))
-        put_padded(flow_ref, j, z + 1, keep * flow_plane(pops_refs, z, j) + (even - odd))
+        f, g = load(i), load(j)
+        put(i, jnp.where(porous, keep * f + (even + odd), g))
+        put(j, jnp.where(porous, keep * g + (even - odd), f))
 
 
 def stream_flow(z, bits, flow_ref):
@@ -641,13 +672,13 @@
             moved = padded_plane(flow_ref, z + 1 - cz, cy, which)
         if cx:
             moved = ring(moved, cx)
-        out.append(chosen(bits, moved, post, which))
+        out.append(jnp.where(is_open(bits, which), moved, post[OPP[which]]))
     return out
 
 
 def first_kernel(
     dense_ref, right_ref, left_ref, pops_ref, side_ref, aux_ref, ring_ref,
-    post_ref, ydn_ref, yup_ref, zdn_ref, zup_ref, turn_ref,
+    post_ref, ydn_ref, yup_ref, turn_ref,
 ):
     turn_ref[pl.ds(0, BLOCKROWS // 8, stride=8), :] = right_ref[...]
     turn_ref[pl.ds(7, BLOCKROWS // 8, stride=8), :] = left_ref[...]
@@ -668,10 +699,9 @@
             post_ref[i, pl.ds(pl.multiple_of(z * PLANE, PLANE), PLANE), :] = post[i]
         return carry
 
-    lax.fori_loop(0, B, body, 0)
+    lax.fori_loop(0, B, body, 0, unroll=UNROLL)
     pops_refs = pops_ref, side_ref
     write_y_messages(pops_refs, post_ref, aux_ref, (ydn_ref, yup_ref), ring_ref=ring_ref)
-    write_z_messages(pops_refs, post_ref, aux_ref, (zdn_ref, zup_ref), ring_ref=ring_ref)
 
 
 def pull(z, refs, bits_ref, flow_ref, solute_ref):
@@ -694,93 +724,142 @@
         post_ref[i, at, :] = post[i]
 
 
-def push(z, refs, bits, solute, flow_ref, solute_ref, turn_ref):
-    pops_ref, side_ref, post_ref, aux_ref = refs
+def push(z, pops_refs, aux_ref, bits, solute, flow_ref):
+    rho, vx, vy, vz = (plane(aux_ref, z, k) for k in range(4))
+    collide_flow(
+        lambda i: flow_plane(pops_refs, z, i), rho, vx, vy, vz, bits, sum(solute),
+        lambda i, v: put_padded(flow_ref, i, z + 1, v),
+    )
+
+
+def put_solute(solute_ref, z, solute):
     for i in range(7):
-        if turn_ref is None:
-            solute_ref[i, pl.ds(pl.multiple_of(z * PLANE, PLANE), PLANE), :] = solute[i]
-        else:
-            for half in range(2):
-                at = pl.multiple_of(i * 256 + z * B + half * 8, 8)
-                turn_ref[pl.ds(at, 8), :] = turn_blocks(solute[i][half * 8 : half * 8 + 8])
-    collide_flow(z, (pops_ref, side_ref), aux_ref, bits, sum(solute), flow_ref)
+        solute_ref[i, pl.ds(pl.multiple_of(z * PLANE, PLANE), PLANE), :] = solute[i]
+
+
+def turn_plane(turn_ref, z, solute):
+    for i in range(7):
+        for half in range(2):
+            at = pl.multiple_of(i * 256 + z * B + half * 8, 8)
+            turn_ref[pl.ds(at, 8), :] = turn_blocks(solute[i][half * 8 : half * 8 + 8])
+
+
+def core_kernel(first, *refs):
+    pops_ref, side_ref, post_ref, aux_ref, bits_ref = refs[:5]
+    ring_ref, refs = (refs[5], refs[6:]) if first else (None, refs[5:])
+    zdn_ref, zup_ref, flow_ref, solute_ref = refs
+    write_z_messages(
+        (pops_ref, side_ref), post_ref, aux_ref, (zdn_ref, zup_ref), bits_ref, ring_ref
+    )
+    fills = [jnp.zeros((PLANE, L), F32)] * 2
+
+    def body(z, carry):
+        bits = plane(bits_ref, z)
+        solute = stream_solute(
+            z, post_ref, bits, fills, plane(post_ref, z - 1, 5), plane(post_ref, z + 1, 6)
+        )
+        put_solute(solute_ref, z, solute)
+        push(z, (pops_ref, side_ref), aux_ref, bits, solute, flow_ref)
+        return carry
+
+    lax.fori_loop(1, B - 1, body, 0, unroll=UNROLL)
+
+
+def fix_rows(pops_refs, post_ref, aux_ref, bits_ref, y_refs, flow_ref, solute_ref):
+    for side in range(2):
+        edge = (0, B - 1)[side]
+        which = (3, 4)[side]
+        bits = face_rows(bits_ref, edge)
+        post = {i: face_rows(post_ref, edge, i) for i in (3, 4)}
+        new = chosen(bits, read_field(y_refs[side], NORM), post, which)
+        conc = new + sum(face_rows(solute_ref, edge, i) for i in range(7) if i != which)
+        put_face(solute_ref, edge, new, which)
+
+        def put(i, v):
+            for tile in range(2):
+                at = PADDED + tile * 32 + 8 + edge
+                flow_ref[i, pl.ds(at, B, stride=PADDED), :] = v[tile * B : (tile + 1) * B]
+
+        rho, vx, vy, vz = (face_rows(aux_ref, edge, k) for k in range(4))
+        collide_flow(
+            lambda i: flow_rows(pops_refs, edge, i), rho, vx, vy, vz, bits, conc, put
+        )
 
 
 def inner_kernel(last, *refs):
-    pops_in, side_in, post_in, aux_in, bits_ref, open_ref, ylo_ref, yhi_ref = refs[:8]
+    pops_in, side_in, post_in, aux_in, flow_in, solute_in, bits_ref, open_ref = refs[:8]
+    y_refs = refs[8:10]
     if last:
-        pops_ref, flow_ref, turn_ref, ghost_ref = refs[8:]
+        pops_ref, flow_ref, solute_ref, turn_ref = refs[10:]
+        state, out = (pops_ref, side_in, post_in, aux_in), (pops_ref, None, None, None)
+    else:
+        *state, flow_ref, solute_ref = refs[10:]
+        out = state
+    pops_ref, side_ref, post_ref, aux_ref = state
+    fix_rows((pops_ref, side_ref), post_ref, aux_ref, bits_ref, y_refs, flow_ref, solute_ref)
+    collide_y_halos(post_ref, open_ref, y_refs, None, flow_ref)
+
+    def turn(z, carry):
+        turn_plane(turn_ref, z, [plane(solute_ref, z, i) for i in range(7)])
+        return carry
+
+    def body(z, carry):
+        pull(z, out, bits_ref, flow_ref, solute_ref)
+        return carry
+
+    if last:
+        lax.fori_loop(1, B - 1, turn, 0, unroll=UNROLL)
+    lax.fori_loop(2, B - 2, body, 0, unroll=UNROLL)
+
+
+def edge_kernel(last, *refs):
+    if last:
+        slot_ref, refs = refs[0], refs[1:]
+    pops_in, side_in, post_in, aux_in, flow_in, solute_in, bits_ref, open_ref = refs[:8]
+    y_refs, z_refs = refs[8:10], refs[10:12]
+    if last:
+        pops_ref, flow_ref, turn_ref, send_ref, hold_ref, sems = refs[12:]
         state, out = (pops_ref, side_in, post_in, aux_in), (pops_ref, None, None, None)
         solute_ref = None
     else:
-        pops_ref, side_ref, post_ref, aux_ref, flow_ref, solute_ref, ghost_ref = refs[8:]
-        state = out = (pops_ref, side_ref, post_ref, aux_ref)
-        turn_ref = None
-    set_ghosts(ghost_ref, (ylo_ref, yhi_ref))
-    collide_y_halos(state[2], open_ref, (ylo_ref, yhi_ref), None, flow_ref)
-
-    def first(z, carry):
+        *state, flow_ref, solute_ref, ydn_ref, yup_ref = refs[12:]
+        out = state
+    pops_ref, side_ref, post_ref, aux_ref = state
+    solutes = []
+    for z in (0, B - 1):
         bits = plane(bits_ref, z)
-        post_ref = state[2]
-        solute = stream_solute(
-            z, post_ref, bits, ghost_ref, plane(post_ref, z - 1, 5), plane(post_ref, z + 1, 6)
-        )
-        push(z, state, bits, solute, flow_ref, solute_ref, turn_ref)
-        return carry
-
-    def second(z, carry):
-        pull(z, out, bits_ref, flow_ref, solute_ref)
-        return carry
-
-    lax.fori_loop(1, B - 1, first, 0)
-    lax.fori_loop(2, B - 2, second, 0)
-
-
-def edge_kernel(last, *refs):
+        fills = [spread8(read_row(y_refs[side], NORM, z)) for side in range(2)]
+        below = read_field(z_refs[0], NORM) if z == 0 else plane(post_ref, z - 1, 5)
+        above = read_field(z_refs[1], NORM) if z == B - 1 else plane(post_ref, z + 1, 6)
+        solutes.append(stream_solute(z, post_ref, bits, fills, below, above))
+        if last:
+            turn_plane(turn_ref, z, solutes[-1])
+        else:
+            put_solute(solute_ref, z, solutes[-1])
     if last:
-        slot_ref, refs = refs[0], refs[1:]
-    pops_in, side_in, post_in, aux_in, flow_in, solute_ref, bits_ref, open_ref = refs[:8]
-    y_refs, z_refs = refs[8:10], refs[10:12]
-    if last:
-        pops_ref, flow_ref, turn_ref, send_ref, ghost_ref = refs[12:]
-        state, out = (pops_ref, side_in, post_in, aux_in), (pops_ref, None, None, None)
-    else:
-        pops_ref, side_ref, post_ref, aux_ref, flow_ref, ydn_ref, yup_ref, ghost_ref = refs[12:]
-        state = out = (pops_ref, side_ref, post_ref, aux_ref)
-        turn_ref = None
-    set_ghosts(ghost_ref, y_refs)
-    post_ref = state[2]
+
+        def tile_for(owner):
+            tile = jnp.int32(0)
+            for j in range(8):
+                slot = slot_ref[0, 0, j]
+                tile = jnp.where((slot >= 0) & (slot // 8 == owner), j, tile)
+            return tile
+
+        copies = send_blocks(tile_for, turn_ref, send_ref, hold_ref, sems)
     collide_y_halos(post_ref, open_ref, y_refs, z_refs, flow_ref)
     collide_z_halos(post_ref, open_ref, y_refs, z_refs, flow_ref)
-    for z in (0, B - 1):
-        bits = plane(bits_ref, z)
-        below = read_field(z_refs[0], NORM) if z == 0 else plane(post_ref, z - 1, 5)
-        above = read_field(z_refs[1], NORM) if z == B - 1 else plane(post_ref, z + 1, 6)
-        solute = stream_solute(z, post_ref, bits, ghost_ref, below, above)
-        push(z, state, bits, solute, flow_ref, solute_ref, turn_ref)
-
-    def second(k, carry):
-        pull(k + 12 * (k // 2), out, bits_ref, flow_ref, solute_ref)
-        return carry
-
-    lax.fori_loop(0, 4, second, 0)
-    if not last:
+    for z, solute in zip((0, B - 1), solutes):
+        push(z, (pops_ref, side_ref), aux_ref, plane(bits_ref, z), solute, flow_ref)
+
+    for z in (0, 1, B - 2, B - 1):
+        pull(z, out, bits_ref, flow_ref, solute_ref)
+    if last:
+        for copy in copies:
+            copy.wait()
+    else:
         write_y_messages(
             (pops_ref, side_ref), post_ref, aux_ref, (ydn_ref, yup_ref), bits_ref=bits_ref
         )
-        return
-    for owner in range(8):
-        tile = jnp.int32(0)
-        for j in range(8):
-            slot = slot_ref[0, 0, j]
-            tile = jnp.where((slot >= 0) & (slot // 8 == owner), j, tile)
-        send_ref[owner] = turn_ref[pl.ds(tile, BLOCKROWS // 8, stride=8), :]
-
-
-def z_kernel(pops_ref, side_ref, post_ref, aux_ref, bits_ref, zdn_ref, zup_ref):
-    write_z_messages(
-        (pops_ref, side_ref), post_ref, aux_ref, (zdn_ref, zup_ref), bits_ref=bits_ref
-    )
 
 
 def scatter_kernel(slot_ref, recv_ref, out_ref):
@@ -818,79 +897,102 @@
 
 def shards(populations, solute_state, pore_mask, block_slot, slot_block):
     flags = inside()
+    hold = [pltpu.VMEM((8, BLOCKROWS // 8, L), F32), pltpu.SemaphoreType.DMA((9,))]
+    turn = pltpu.VMEM((BLOCKROWS, L), F32)
+    send_out = pltpu.HBM((8, BLOCKROWS // 8, L), F32)
     state = solute_state.reshape(7, 8, 32, L).transpose(0, 2, 1, 3).reshape(BLOCKROWS, L)
-    send = call(gather_kernel, shape(8, 224, L), [SMEM, VMEM], [], 1, 2 * 10**6)(slot_block, state)
+    send = call(
+        gather_kernel, send_out, [SMEM, HBM], [turn] + hold, 1, 2 * 10**6, out_specs=HBM
+    )(slot_block, state)
     recv = lax.all_to_all(send, "gz", split_axis=0, concat_axis=0, tiled=True)
 
     pops = populations.reshape(19, 256, L)
     mask = pore_mask.reshape(256, L)
-    low, high = call(columns_kernel, (shape(320, L),) * 2, [VMEM] * 2, [], 10**7, 3 * 10**6)(
-        pops, mask
-    )
+    low, high = call(columns_kernel, (stored(320, L),) * 2, [VMEM] * 2, [], 1, 1)(pops, mask)
     left, right = neighbours(low, high, "gx")
-    side, ring_mask, aux = call(
+    dims = ((19, 256, L), (ROWS, L), (4, ROWS, L), (PADROWS, L), (ROWS, L))
+    kinds = (F32,) * 4 + (jnp.int32,)
+    side, ring_mask, aux, mask, bits = call(
         ring_kernel,
-        (shape(19, 256, L), shape(ROWS, L), shape(4, ROWS, L)),
+        tuple(stored(*d, dtype=k) for d, k in zip(dims, kinds)),
         [SMEM] + [VMEM] * 4,
         [],
+        1,
+        1,
+    )(flags, pops, mask, right, left)
+
+    after = jnp.minimum(bits[0, 0], 0)
+
+    def block_of(tile):
+        owner = jnp.maximum(block_slot[0, 0, tile], 0) // 8 + after
+        return lax.dynamic_index_in_dim(recv, owner, 0, keepdims=False)
+
+    left, right = neighbours(block_of(0), block_of(7), "gx")
+    state = (pops, side, ring_mask, aux, mask, bits)
+    dense, pops, side, ring_mask, aux, mask, bits = call(
+        spread_kernel,
+        (held(BLOCKROWS, L), held(19, 256, L))
+        + tuple(held(*d, dtype=k) for d, k in zip(dims, kinds)),
+        [SMEM, VMEM] + [HBM] * 6,
+        [turn, pltpu.SemaphoreType.DMA((6,))],
+        10**7,
+        2 * 10**6,
+    )(block_slot, recv, *state)
+    message = held((SIDES + MASK + 1) * B, L)
+    post, ydn, yup = call(
+        first_kernel,
+        (held(7, ROWS, L),) + (message,) * 2,
+        [VMEM] * 7,
+        [turn],
         10**7,
         10**7,
-    )(flags, pops, mask, right, left)
-
-    def block_of(tile):
-        owner = jnp.maximum(block_slot[0, 0, tile], 0) // 8
-        return lax.dynamic_index_in_dim(recv, owner, 0, keepdims=False)
-
-    left, right = neighbours(block_of(0), block_of(7), "gx")
-    turn = pltpu.VMEM((BLOCKROWS, L), F32)
-    dense = call(spread_kernel, shape(BLOCKROWS, L), [SMEM, VMEM], [turn], 10**7, 2 * 10**6)(
-        block_slot, recv
-    )
-    message = shape((SIDES + MASK + 1) * B, L)
-    post, ydn, yup, zdn, zup = call(
-        first_kernel, (shape(7, ROWS, L),) + (message,) * 4, [VMEM] * 7, [turn], 10**7, 10**7
+        keep=True,
     )(dense, right, left, pops, side, aux, ring_mask)
 
-    ghost = pltpu.VMEM((2 * PLANE, L), F32)
     states = (held(19, 256, L), held(19, 256, L), held(7, ROWS, L), held(4, ROWS, L))
-    flow_out, solute_out = held(19, PADROWS, L), held(7, ROWS, L)
-    bits_out, open_out = held(ROWS, L, dtype=jnp.int32), held(PLANE * 8, L)
+    works = (held(19, PADROWS, L), held(7, ROWS, L))
+    opens_out = (held(PADROWS, L), held(ROWS, L, dtype=jnp.int32), held(PLANE * 8, L))
     message = held((SIDES + MASK) * B, L)
     state = (pops, side, post, aux)
     for step in range(STEPS):
         last = step == STEPS - 1
         y_halos = neighbours(ydn, yup, "gy")
+        zdn, zup, *work = call(
+            functools.partial(core_kernel, step == 0),
+            (held(*ydn.shape),) * 2 + works,
+            [VMEM] * (6 if step == 0 else 5),
+            [],
+            10**7,
+            10**7,
+            keep=True,
+        )(*state, bits, *([ring_mask] if step == 0 else []))
         z_halos = exchange_z(y_halos, zdn, zup)
         if step == 0:
             mask, bits, opens = call(
-                inner_open_kernel,
-                (held(PADROWS, L), bits_out, open_out),
-                [SMEM] + [VMEM] * 3,
+                side_open_kernel,
+                opens_out,
+                [SMEM] + [VMEM] * 4,
                 [],
-                10**7,
                 10**6,
+                10**6,
+                aliases={3: 0, 4: 1},
                 keep=True,
-            )(flags, ring_mask, *y_halos)
-        if last:
-            outs = (states[0], flow_out, held(BLOCKROWS, L))
-            aliases = {0: 0}
-        else:
-            outs = states + (flow_out, solute_out)
-            aliases = {0: 0, 1: 1, 2: 2, 3: 3}
+            )(flags, *y_halos, mask, bits)
+        outs = states[:1] + works + (held(BLOCKROWS, L),) if last else states + works
         moved = call(
             functools.partial(inner_kernel, last),
             outs,
-            [VMEM] * 8,
-            [ghost],
-            10**8,
-            2 * 10**7,
-            aliases=aliases,
+            [VMEM] * 10,
+            [],
+            10**7,
+            10**7,
+            aliases={0: 0, 4: 1, 5: 2} if last else {i: i for i in range(6)},
             keep=True,
-        )(*state, bits, opens, *y_halos)
+        )(*state, *work, bits, opens, *y_halos)
         if step == 0:
             mask, bits, opens = call(
                 edge_open_kernel,
-                (held(PADROWS, L), bits_out, open_out),
+                opens_out,
                 [SMEM] + [VMEM] * 5,
                 [],
                 10**6,
@@ -899,32 +1001,29 @@
                 keep=True,
             )(flags, *z_halos, mask, bits, opens)
         if last:
-            pops, flow, turned = moved
-            pops, flow, turned, send = call(
+            pops, flow, _, turned = moved
+            pops, _, _, send = call(
                 functools.partial(edge_kernel, True),
-                (states[0], flow_out, held(BLOCKROWS, L), shape(8, 224, L)),
+                (states[0], works[0], held(BLOCKROWS, L), send_out),
                 [SMEM] + [VMEM] * 12,
-                [ghost],
+                hold,
                 10**7,
                 10**7,
                 aliases={1: 0, 5: 1, 6: 2},
                 keep=True,
+                out_specs=(VMEM, VMEM, VMEM, HBM),
             )(block_slot, pops, *state[1:], flow, turned, bits, opens, *y_halos, *z_halos)
             break
-        *state, flow, solute = moved
-        *state, flow, ydn, yup = call(
+        *state, _, _, ydn, yup = call(
             functools.partial(edge_kernel, False),
-            states + (flow_out, message, message),
+            states + works + (message, message),
             [VMEM] * 12,
-            [ghost],
+            [],
             10**7,
             10**7,
-            aliases={0: 0, 1: 1, 2: 2, 3: 3, 4: 4},
+            aliases={i: i for i in range(6)},
             keep=True,
-        )(*state, flow, solute, bits, opens, *y_halos, *z_halos)
-        zdn, zup = call(
-            z_kernel, (message, message), [VMEM] * 5, [], 10**6, 10**6, keep=True
-        )(*state, bits)
+        )(*moved, bits, opens, *y_halos, *z_halos)
 
     recv = lax.all_to_all(send, "gz", split_axis=0, concat_axis=0, tiled=True)
     out = call(scatter_kernel, shape(BLOCKROWS, L), [SMEM, VMEM], [], 1, 2 * 10**6)(

time: 150 us -> 137 us (0.913); the launches traced: 147 us -> 137 us
  waiting for transfers between devices: 46.2 us -> 38.4 us
  local copies, waits for them, and re-layouts: 7.68 us -> 4.48 us
    all_to_all x2, waiting for transfers between devices: 36.9 us -> 30.2 us  [shards(): recv = lax.all_to_all(send, 'gz', split_axis=0, concat_axis=0, tiled=True)]
    unnamed x26 -> x23, local copies, waits for them, and re-layouts: 5.98 us -> 2.3 us
    pallas_call x19 -> x20, Pallas kernels: 48.4 us -> 48.5 us  [placed(): return run(*map(place, args, in_specs))]
  transfers between devices with their start and end apart: 22 -> 22, of which waited for: 6 -> 11; matrix products, arithmetic and copies ran while one was open for 3% -> 3% of each run, Pallas kernels for 23% -> 26%
where the time goes in v2:
time: 137 us
  Pallas kernels  48.5 us (35%)
  starting transfers between devices  42.3 us (31%)
  waiting for transfers between devices  38.4 us (28%)
  local copies, waits for them, and re-layouts  4.48 us (3%)
  between operations  2.92 us (2%)
    pallas_call x20, Pallas kernels, placed(): return run(*map(place, args, in_specs))  48.5 us
    all_to_all x2, waiting for transfers between devices, shards(): recv = lax.all_to_all(send, 'gz', split_axis=0, concat_axis=0, tiled=True)  30.2 us
    ppermute x20, starting transfers between devices, neighbours(): return (lax.ppermute(high, axis, up), lax.ppermute(low, axis, down))  29.8 us
    all_to_all x2, starting transfers between devices, shards(): recv = lax.all_to_all(send, 'gz', split_axis=0, concat_axis=0, tiled=True)  12.5 us
    ppermute x20, waiting for transfers between devices, neighbours(): return (lax.ppermute(high, axis, up), lax.ppermute(low, axis, down))  8.12 us
  transfers between devices with their start and end apart: 22, of which 11 were waited for; matrix products, arithmetic and copies ran while one was open for 3% of the time, Pallas kernels for 26%

profile of v2, /device:TPU:7, one launch (start us, length us, event | category | flops | bytes accessed | tf_op | source)
XLA Modules:
  0.0 136.9 jit_solution(6716589760085911397)
XLA Ops:
  0.6 0.0 copy-start
  0.7 0.8 copy-done.3
  1.5 2.8 %shard_map.68 = f32[8,224,128]{2,1,0:T(8,128)} custom-call(s32[8]{0:T(128)S(1)} %copy-done.3, f32[1792,128]{1,0:T(8,128)} %bitcast.94), custom_call_target="tpu_custom_call" | custom-call | flops 1 | bytes 2000000 | tf_op jit(solution)/shard_map/pallas_call | solution.py:79
  4.2 0.0 copy-start.2
  4.2 8.2 %all-to-all-start = ((f32[8,224,128]{2,1,0:T(8,128)}), f32[8,224,128]{2,1,0:T(8,128)S(1)}, u32[]{:S(2)}, u32[]{:S(2)}) async-start(f32[8,224,128]{2,1,0:T(8,128)} %shard_map.68), calls=%async_computation | async-start | bytes 1835008 | tf_op jit(solution)/shard_map/all_to_all | solution.py:907
  12.5 3.5 %shard_map.69 = (f32[320,128]{1,0:T(8,128)}, f32[320,128]{1,0:T(8,128)}) custom-call(f32[19,256,128]{2,1,0:T(8,128)S(1)} %bitcast.82, s32[256,128]{1,0:T(8,128)S(1)} %bitcast.86), custom_call_target="tpu_custom_call" | custom-call | flops 1 | bytes 1 | tf_op jit(solution)/shard_map/pallas_call | solution.py:79
  15.9 2.7 %collective-permute-start = (f32[320,128]{1,0:T(8,128)}, f32[320,128]{1,0:T(8,128)}, u32[]{:S(2)}, u32[]{:S(2)}) collective-permute-start(f32[320,128]{1,0:T(8,128)} %get-tuple-element.81), channel_id=1, source_target_pairs={{0,192},{64,0},{128,64},{192,128},{1,193},{65,1},{129,65},{193,129... | collective-permute-start | bytes 491528 | tf_op jit(solution)/shard_map/ppermute | solution.py:876
  18.7 0.6 fusion.8
  20.5 0.1 stack.27
  20.6 0.9 collective-permute-done.right_ref
  21.5 3.0 %collective-permute-done.1.left_ref = f32[320,128]{1,0:T(8,128)} collective-permute-done((f32[320,128]{1,0:T(8,128)}, f32[320,128]{1,0:T(8,128)}, u32[]{:S(2)}, u32[]{:S(2)}) %collective-permute-start.1) | collective-permute-done | bytes 163872 | tf_op jit(solution)/shard_map/ppermute | solution.py:876
  24.5 7.2 %shard_map.70 = (f32[19,256,128]{2,1,0:T(8,128)}, f32[512,128]{1,0:T(8,128)}, f32[4,512,128]{2,1,0:T(8,128)}, f32[1152,128]{1,0:T(8,128)}, s32[512,128]{1,0:T(8,128)}) custom-call(f32[6]{0:T(128)S(1)} %convert_element_type.3.flag_ref, f32[19,256,128]{2,1,0:T(8,128)S(1)} %bitcast.83, s32[256,128]{1,0:T(8,128)S(1)} %bitcast.87, ...), custom_call_target="tpu_custom_call" | custom-call | flops 1 | bytes 1 | tf_op jit(solution)/shard_map/pallas_call | solution.py:79
  31.7 1.2 slice.58
  33.5 5.3 %all-to-all-done.recv_ref = f32[8,224,128]{2,1,0:T(8,128)S(1)} async-done(((f32[8,224,128]{2,1,0:T(8,128)}), f32[8,224,128]{2,1,0:T(8,128)S(1)}, u32[]{:S(2)}, u32[]{:S(2)}) %all-to-all-start) | async-done | bytes 917536 | tf_op jit(solution)/shard_map/all_to_all | solution.py:907
  38.8 2.8 %collective-permute-start.2 = (f32[224,128]{1,0:T(8,128)S(1)}, f32[224,128]{1,0:T(8,128)S(1)}, u32[]{:S(2)}, u32[]{:S(2)}) collective-permute-start(f32[224,128]{1,0:T(8,128)S(1)} %get-tuple-element.161), channel_id=1, source_target_pairs={{0,192},{64,0},{128,64},{192,128},{1,193},{65,1},{129,65},{193,129... | collective-permute-start | bytes 344072 | tf_op jit(solution)/shard_map/ppermute | solution.py:876
  41.7 3.6 %shard_map.71 = (f32[1792,128]{1,0:T(8,128)S(1)}, f32[19,256,128]{2,1,0:T(8,128)S(1)}, f32[19,256,128]{2,1,0:T(8,128)S(1)}, f32[512,128]{1,0:T(8,128)S(1)}, f32[...) custom-call(s32[1,1,8]{2,1,0:T(1,128)S(1)} %copy-done.2, ...), custom_call_target="tpu_custom_call" | custom-call | flops 10000000 | bytes 2000000 | tf_op jit(solution)/shard_map/pallas_call | solution.py:79
  45.3 1.2 collective-permute-done.3.left_ref
  46.5 2.0 %shard_map.72 = (f32[7,512,128]{2,1,0:T(8,128)S(1)}, f32[240,128]{1,0:T(8,128)S(1)}, f32[240,128]{1,0:T(8,128)S(1)}) custom-call(f32[1792,128]{1,0:T(8,128)S(1)} %get-tuple-element.90.dense_ref, f32[224,128]{1,0:T(8,128)S(1)} %collective-permute-done.2.right_ref, f32[224,128]{1,0:T(8,128)S(1)} %collective-permute-done.3.left_ref, ...), custom_call_target="tpu_custom_call" | custom-call | flops 10000000 | bytes 10000000 | tf_op jit(solution)/shard_map/pallas_call | solution.py:79
  48.5 1.9 %collective-permute-start.5 = (f32[240,128]{1,0:T(8,128)S(1)}, f32[240,128]{1,0:T(8,128)S(1)}, u32[]{:S(2)}, u32[]{:S(2)}) collective-permute-start(f32[240,128]{1,0:T(8,128)S(1)} %get-tuple-element.98), channel_id=1, source_target_pairs={{0,56},{8,0},{16,8},{24,16},{32,24},{40,32},{48,40},{56,48},{1,57}... | collective-permute-start | bytes 368648 | tf_op jit(solution)/shard_map/ppermute | solution.py:876
  50.5 0.1 pad.31.clone
  50.5 1.0 collective-permute-start.4
  51.6 2.2 %shard_map.73 = (f32[240,128]{1,0:T(8,128)S(1)}, f32[240,128]{1,0:T(8,128)S(1)}, f32[19,1152,128]{2,1,0:T(8,128)S(1)}, f32[7,512,128]{2,1,0:T(8,128)S(1)}) custom-call(f32[19,256,128]{2,1,0:T(8,128)S(1)} %get-tuple-element.88.pops_ref.refs_0_, f32[19,256,128]{2,1,0:T(8,128)S(1)} %get-tuple-element.89.side_ref.refs_1_, ...), custom_call_target="tpu_custom_call" | custom-call | flops 10000000 | bytes 10000000 | tf_op jit(solution)/shard_map/pallas_call | solution.py:79
  53.7 0.3 collective-permute-done.5.yhi_ref.refs_9_
  54.1 0.1 maximum_maximum_fusion.1
  54.2 0.1 collective-permute-start.6
  54.3 2.7 %collective-permute-start.7 = (f32[272,128]{1,0:T(8,128)S(1)}, f32[272,128]{1,0:T(8,128)S(1)}, u32[]{:S(2)}, u32[]{:S(2)}) collective-permute-start(f32[272,128]{1,0:T(8,128)S(1)} %get-tuple-element.178), channel_id=1, source_target_pairs={{0,7},{1,0},{2,1},{3,2},{4,3},{5,4},{6,5},{7,6},{8,15},{9,8},{10,9... | collective-permute-start | bytes 417800 | tf_op jit(solution)/shard_map/ppermute | solution.py:876
  57.0 0.7 shard_map.74
  57.7 2.7 %shard_map.75 = (f32[19,256,128]{2,1,0:T(8,128)S(1)}, f32[19,256,128]{2,1,0:T(8,128)S(1)}, f32[7,512,128]{2,1,0:T(8,128)S(1)}, f32[4,512,128]{2,1,0:T(8,128)S(1)...) custom-call(f32[19,256,128]{2,1,0:T(8,128)S(1)} %get-tuple-element.8, ...), custom_call_target="tpu_custom_call", output_to_operand_aliasing={{0}: (0, {}), {1}: (1, {}), {2}: (2, {}), {3}: (3, {}), {4}... | custom-call | flops 10000000 | bytes 10000000 | tf_op jit(solution)/shard_map/pallas_call | solution.py:79
  60.4 0.9 shard_map.76
  61.3 1.2 shard_map.77
  62.5 1.4 collective-permute-start.9
  63.9 0.1 pad.23.clone
  64.0 2.2 %collective-permute-start.8 = (f32[224,128]{1,0:T(8,128)S(1)}, f32[224,128]{1,0:T(8,128)S(1)}, u32[]{:S(2)}, u32[]{:S(2)}) collective-permute-start(f32[224,128]{1,0:T(8,128)S(1)} %get-tuple-element.119), channel_id=1, source_target_pairs={{0,8},{8,16},{16,24},{24,32},{32,40},{40,48},{48,56},{56,0},{1,9},... | collective-permute-start | bytes 344072 | tf_op jit(solution)/shard_map/ppermute | solution.py:876
  66.2 2.1 %shard_map.78 = (f32[224,128]{1,0:T(8,128)S(1)}, f32[224,128]{1,0:T(8,128)S(1)}, f32[19,1152,128]{2,1,0:T(8,128)S(1)}, f32[7,512,128]{2,1,0:T(8,128)S(1)}) custom-call(f32[19,256,128]{2,1,0:T(8,128)S(1)} %get-tuple-element.113.refs_0_, f32[19,256,128]{2,1,0:T(8,128)S(1)} %get-tuple-element.114.refs_1_, f32[7,512,128]{2,1,0:T(8,128)S(1)} %get-tuple-element.115.refs_2_, ...), custom_call_target="tpu_custom_call" | custom-call | flops 10000000 | bytes 10000000 | tf_op jit(solution)/shard_map/pallas_call | solution.py:79
  68.4 0.2 collective-permute-done.9.refs_9_
  68.7 0.1 maximum_maximum_fusion.3
  68.8 0.1 collective-permute-start.10
  68.9 2.8 %collective-permute-start.11 = (f32[256,128]{1,0:T(8,128)S(1)}, f32[256,128]{1,0:T(8,128)S(1)}, u32[]{:S(2)}, u32[]{:S(2)}) collective-permute-start(f32[256,128]{1,0:T(8,128)S(1)} %get-tuple-element.184), channel_id=1, source_target_pairs={{0,7},{1,0},{2,1},{3,2},{4,3},{5,4},{6,5},{7,6},{8,15},{9,8},{10,9... | collective-permute-start | bytes 393224 | tf_op jit(solution)/shard_map/ppermute | solution.py:876
  71.7 2.7 %shard_map.79 = (f32[19,256,128]{2,1,0:T(8,128)S(1)}, f32[19,256,128]{2,1,0:T(8,128)S(1)}, f32[7,512,128]{2,1,0:T(8,128)S(1)}, f32[4,512,128]{2,1,0:T(8,128)S(1)...) custom-call(f32[19,256,128]{2,1,0:T(8,128)S(1)} %get-tuple-element.1, ...), custom_call_target="tpu_custom_call", output_to_operand_aliasing={{0}: (0, {}), {1}: (1, {}), {2}: (2, {}), {3}: (3, {}), {4}... | custom-call | flops 10000000 | bytes 10000000 | tf_op jit(solution)/shard_map/pallas_call | solution.py:79
  74.4 1.1 collective-permute-done.10.refs_10_
  75.6 1.2 shard_map.80
  76.8 0.4 collective-permute-start.13
  77.2 2.5 %collective-permute-start.12 = (f32[224,128]{1,0:T(8,128)S(1)}, f32[224,128]{1,0:T(8,128)S(1)}, u32[]{:S(2)}, u32[]{:S(2)}) collective-permute-start(f32[224,128]{1,0:T(8,128)S(1)} %get-tuple-element.135), channel_id=1, source_target_pairs={{0,8},{8,16},{16,24},{24,32},{32,40},{40,48},{48,56},{56,0},{1,9},... | collective-permute-start | bytes 344072 | tf_op jit(solution)/shard_map/ppermute | solution.py:876
  79.8 2.1 %shard_map.81 = (f32[224,128]{1,0:T(8,128)S(1)}, f32[224,128]{1,0:T(8,128)S(1)}, f32[19,1152,128]{2,1,0:T(8,128)S(1)}, f32[7,512,128]{2,1,0:T(8,128)S(1)}) custom-call(f32[19,256,128]{2,1,0:T(8,128)S(1)} %get-tuple-element.129.refs_0_, f32[19,256,128]{2,1,0:T(8,128)S(1)} %get-tuple-element.130.refs_1_, f32[7,512,128]{2,1,0:T(8,128)S(1)} %get-tuple-element.131.refs_2_, ...), custom_call_target="tpu_custom_call" | custom-call | flops 10000000 | bytes 10000000 | tf_op jit(solution)/shard_map/pallas_call | solution.py:79
  81.9 0.3 collective-permute-done.13.refs_9_
  82.3 0.1 maximum_maximum_fusion.5
  82.4 0.1 collective-permute-start.14
  82.5 2.7 %collective-permute-start.15 = (f32[256,128]{1,0:T(8,128)S(1)}, f32[256,128]{1,0:T(8,128)S(1)}, u32[]{:S(2)}, u32[]{:S(2)}) collective-permute-start(f32[256,128]{1,0:T(8,128)S(1)} %get-tuple-element.182), channel_id=1, source_target_pairs={{0,7},{1,0},{2,1},{3,2},{4,3},{5,4},{6,5},{7,6},{8,15},{9,8},{10,9... | collective-permute-start | bytes 393224 | tf_op jit(solution)/shard_map/ppermute | solution.py:876
  85.3 2.7 %shard_map.82 = (f32[19,256,128]{2,1,0:T(8,128)S(1)}, f32[19,256,128]{2,1,0:T(8,128)S(1)}, f32[7,512,128]{2,1,0:T(8,128)S(1)}, f32[4,512,128]{2,1,0:T(8,128)S(1)...) custom-call(f32[19,256,128]{2,1,0:T(8,128)S(1)} %get-tuple-element.1, ...), custom_call_target="tpu_custom_call", output_to_operand_aliasing={{0}: (0, {}), {1}: (1, {}), {2}: (2, {}), {3}: (3, {}), {4}... | custom-call | flops 10000000 | bytes 10000000 | tf_op jit(solution)/shard_map/pallas_call | solution.py:79
  88.0 0.6 collective-permute-done.14.refs_10_
  88.6 1.2 shard_map.83
  89.8 0.4 collective-permute-start.17
  90.2 2.7 %collective-permute-start.16 = (f32[224,128]{1,0:T(8,128)S(1)}, f32[224,128]{1,0:T(8,128)S(1)}, u32[]{:S(2)}, u32[]{:S(2)}) collective-permute-start(f32[224,128]{1,0:T(8,128)S(1)} %get-tuple-element.151), channel_id=1, source_target_pairs={{0,8},{8,16},{16,24},{24,32},{32,40},{40,48},{48,56},{56,0},{1,9},... | collective-permute-start | bytes 344072 | tf_op jit(solution)/shard_map/ppermute | solution.py:876
  92.9 2.1 %shard_map.84 = (f32[224,128]{1,0:T(8,128)S(1)}, f32[224,128]{1,0:T(8,128)S(1)}, f32[19,1152,128]{2,1,0:T(8,128)S(1)}, f32[7,512,128]{2,1,0:T(8,128)S(1)}) custom-call(f32[19,256,128]{2,1,0:T(8,128)S(1)} %get-tuple-element.145.refs_0_, f32[19,256,128]{2,1,0:T(8,128)S(1)} %get-tuple-element.146.refs_1_.refs_2_, ...), custom_call_target="tpu_custom_call" | custom-call | flops 10000000 | bytes 10000000 | tf_op jit(solution)/shard_map/pallas_call | solution.py:79
  95.0 0.3 collective-permute-done.17.refs_9_.refs_10_
  95.4 0.1 maximum_maximum_fusion.7
  95.5 0.1 collective-permute-start.18
  95.6 3.2 %collective-permute-start.19 = (f32[256,128]{1,0:T(8,128)S(1)}, f32[256,128]{1,0:T(8,128)S(1)}, u32[]{:S(2)}, u32[]{:S(2)}) collective-permute-start(f32[256,128]{1,0:T(8,128)S(1)} %get-tuple-element.180), channel_id=1, source_target_pairs={{0,7},{1,0},{2,1},{3,2},{4,3},{5,4},{6,5},{7,6},{8,15},{9,8},{10,9... | collective-permute-start | bytes 393224 | tf_op jit(solution)/shard_map/ppermute | solution.py:876
  98.8 3.6 %shard_map.85 = (f32[19,256,128]{2,1,0:T(8,128)S(1)}, f32[19,1152,128]{2,1,0:T(8,128)S(1)}, f32[7,512,128]{2,1,0:T(8,128)S(1)}, f32[1792,128]{1,0:T(8,128)S(1)}) custom-call(f32[19,256,128]{2,1,0:T(8,128)S(1)} %get-tuple-element.145.refs_0_, ...), custom_call_target="tpu_custom_call", output_to_operand_aliasing={{0}: (0, {}), {1}: (4, {}), {2}: (5, {})} | custom-call | flops 10000000 | bytes 10000000 | tf_op jit(solution)/shard_map/pallas_call | solution.py:79
  102.4 2.2 %shard_map.86 = (f32[19,256,128]{2,1,0:T(8,128)S(1)}, f32[19,1152,128]{2,1,0:T(8,128)S(1)}, f32[1792,128]{1,0:T(8,128)S(1)}, f32[8,224,128]{2,1,0:T(8,128)}) custom-call(s32[1,1,8]{2,1,0:T(1,128)S(1)} %copy-done.2, f32[19,256,128]{2,1,0:T(8,128)S(1)} %get-tuple-element.153.refs_1_, ...), custom_call_target="tpu_custom_call", output_to_operand_aliasing={{0}: (1, {}), {1}: (5, {}), {2}: (6, {})} | custom-call | flops 10000000 | bytes 10000000 | tf_op jit(solution)/shard_map/pallas_call | solution.py:79
  104.6 4.3 %all-to-all-start.1 = ((f32[8,224,128]{2,1,0:T(8,128)}), f32[8,224,128]{2,1,0:T(8,128)S(1)}, u32[]{:S(2)}, u32[]{:S(2)}) async-start(f32[8,224,128]{2,1,0:T(8,128)} %get-tuple-element.159), calls=%async_computation.1 | async-start | bytes 1835008 | tf_op jit(solution)/shard_map/all_to_all | solution.py:1028
  108.9 1.5 %copy.161 = f32[19,16,16,128]{3,2,1,0:T(8,128)} copy(f32[19,16,16,128]{3,2,1,0:T(8,128)S(1)} %bitcast.80) | data formatting | bytes 4980736
  110.3 24.9 %all-to-all-done.1.recv_ref = f32[8,224,128]{2,1,0:T(8,128)S(1)} async-done(((f32[8,224,128]{2,1,0:T(8,128)}), f32[8,224,128]{2,1,0:T(8,128)S(1)}, u32[]{:S(2)}, u32[]{:S(2)}) %all-to-all-start.1) | async-done | bytes 917536 | tf_op jit(solution)/shard_map/all_to_all | solution.py:1028
  135.2 1.7 %shard_map.87 = f32[1792,128]{1,0:T(8,128)} custom-call(s32[8]{0:T(128)S(1)} %copy-done.4, f32[8,224,128]{2,1,0:T(8,128)S(1)} %all-to-all-done.1.recv_ref), custom_call_target="tpu_custom_call" | custom-call | flops 1 | bytes 2000000 | tf_op jit(solution)/shard_map/pallas_call | solution.py:79
  (46 shorter events, 0.2 us)
Async XLA Ops:
  0.6 11.8 %copy-start = (f32[19,16,16,128]{3,2,1,0:T(8,128)S(1)}, f32[19,16,16,128]{3,2,1,0:T(8,128)}, u32[]{:S(2)}) copy-start(f32[19,16,16,128]{3,2,1,0:T(8,128)} %param.5) | copy-start | bytes 7471108
  0.6 11.8 %copy-start.1 = (s32[16,16,128]{2,1,0:T(8,128)S(1)}, s32[16,16,128]{2,1,0:T(8,128)}, u32[]{:S(2)}) copy-start(s32[16,16,128]{2,1,0:T(8,128)} %param.7) | copy-start | bytes 393220
  0.7 0.8 copy-start.3
  4.2 14.4 %copy-start.2 = (s32[1,1,8]{2,1,0:T(1,128)S(1)}, s32[1,1,8]{2,1,0:T(1,128)}, u32[]{:S(2)}) copy-start(s32[1,1,8]{2,1,0:T(1,128)} %refs_0_.1) | copy-start | bytes 100
  4.2 34.6 %all-to-all-start = ((f32[8,224,128]{2,1,0:T(8,128)}), f32[8,224,128]{2,1,0:T(8,128)S(1)}, u32[]{:S(2)}, u32[]{:S(2)}) async-start(f32[8,224,128]{2,1,0:T(8,128)} %shard_map.68), calls=%async_computation | async-start | bytes 1835008 | tf_op jit(solution)/shard_map/all_to_all | solution.py:907
  15.9 5.6 %collective-permute-start = (f32[320,128]{1,0:T(8,128)}, f32[320,128]{1,0:T(8,128)}, u32[]{:S(2)}, u32[]{:S(2)}) collective-permute-start(f32[320,128]{1,0:T(8,128)} %get-tuple-element.81), channel_id=1, source_target_pairs={{0,192},{64,0},{128,64},{192,128},{1,193},{65,1},{129,65},{193,129... | collective-permute-start | bytes 491528 | tf_op jit(solution)/shard_map/ppermute | solution.py:876
  18.7 5.9 %collective-permute-start.1 = (f32[320,128]{1,0:T(8,128)}, f32[320,128]{1,0:T(8,128)}, u32[]{:S(2)}, u32[]{:S(2)}) collective-permute-start(f32[320,128]{1,0:T(8,128)} %get-tuple-element.82), channel_id=1, source_target_pairs={{0,64},{64,128},{128,192},{192,0},{1,65},{65,129},{129,193},{193,1... | collective-permute-start | bytes 491528 | tf_op jit(solution)/shard_map/ppermute | solution.py:876
  38.8 6.4 %collective-permute-start.2 = (f32[224,128]{1,0:T(8,128)S(1)}, f32[224,128]{1,0:T(8,128)S(1)}, u32[]{:S(2)}, u32[]{:S(2)}) collective-permute-start(f32[224,128]{1,0:T(8,128)S(1)} %get-tuple-element.161), channel_id=1, source_target_pairs={{0,192},{64,0},{128,64},{192,128},{1,193},{65,1},{129,65},{193,129... | collective-permute-start | bytes 344072 | tf_op jit(solution)/shard_map/ppermute | solution.py:876
  41.7 4.9 %collective-permute-start.3 = (f32[224,128]{1,0:T(8,128)S(1)}, f32[224,128]{1,0:T(8,128)S(1)}, u32[]{:S(2)}, u32[]{:S(2)}) collective-permute-start(f32[224,128]{1,0:T(8,128)S(1)} %get-tuple-element.160), channel_id=1, source_target_pairs={{0,64},{64,128},{128,192},{192,0},{1,65},{65,129},{129,193},{193,1... | collective-permute-start | bytes 344072 | tf_op jit(solution)/shard_map/ppermute | solution.py:876
  48.5 5.5 %collective-permute-start.5 = (f32[240,128]{1,0:T(8,128)S(1)}, f32[240,128]{1,0:T(8,128)S(1)}, u32[]{:S(2)}, u32[]{:S(2)}) collective-permute-start(f32[240,128]{1,0:T(8,128)S(1)} %get-tuple-element.98), channel_id=1, source_target_pairs={{0,56},{8,0},{16,8},{24,16},{32,24},{40,32},{48,40},{56,48},{1,57}... | collective-permute-start | bytes 368648 | tf_op jit(solution)/shard_map/ppermute | solution.py:876
  50.5 3.5 %collective-permute-start.4 = (f32[240,128]{1,0:T(8,128)S(1)}, f32[240,128]{1,0:T(8,128)S(1)}, u32[]{:S(2)}, u32[]{:S(2)}) collective-permute-start(f32[240,128]{1,0:T(8,128)S(1)} %get-tuple-element.97), channel_id=1, source_target_pairs={{0,8},{8,16},{16,24},{24,32},{32,40},{40,48},{48,56},{56,0},{1,9},... | collective-permute-start | bytes 368648 | tf_op jit(solution)/shard_map/ppermute | solution.py:876
  54.2 6.2 %collective-permute-start.6 = (f32[272,128]{1,0:T(8,128)S(1)}, f32[272,128]{1,0:T(8,128)S(1)}, u32[]{:S(2)}, u32[]{:S(2)}) collective-permute-start(f32[272,128]{1,0:T(8,128)S(1)} %get-tuple-element.179), channel_id=1, source_target_pairs={{0,1},{1,2},{2,3},{3,4},{4,5},{5,6},{6,7},{7,0},{8,9},{9,10},{10,1... | collective-permute-start | bytes 417800 | tf_op jit(solution)/shard_map/ppermute | solution.py:876
  54.3 6.1 %collective-permute-start.7 = (f32[272,128]{1,0:T(8,128)S(1)}, f32[272,128]{1,0:T(8,128)S(1)}, u32[]{:S(2)}, u32[]{:S(2)}) collective-permute-start(f32[272,128]{1,0:T(8,128)S(1)} %get-tuple-element.178), channel_id=1, source_target_pairs={{0,7},{1,0},{2,1},{3,2},{4,3},{5,4},{6,5},{7,6},{8,15},{9,8},{10,9... | collective-permute-start | bytes 417800 | tf_op jit(solution)/shard_map/ppermute | solution.py:876
  62.5 6.1 %collective-permute-start.9 = (f32[224,128]{1,0:T(8,128)S(1)}, f32[224,128]{1,0:T(8,128)S(1)}, u32[]{:S(2)}, u32[]{:S(2)}) collective-permute-start(f32[224,128]{1,0:T(8,128)S(1)} %get-tuple-element.120), channel_id=1, source_target_pairs={{0,56},{8,0},{16,8},{24,16},{32,24},{40,32},{48,40},{56,48},{1,57}... | collective-permute-start | bytes 344072 | tf_op jit(solution)/shard_map/ppermute | solution.py:876
  64.0 4.7 %collective-permute-start.8 = (f32[224,128]{1,0:T(8,128)S(1)}, f32[224,128]{1,0:T(8,128)S(1)}, u32[]{:S(2)}, u32[]{:S(2)}) collective-permute-start(f32[224,128]{1,0:T(8,128)S(1)} %get-tuple-element.119), channel_id=1, source_target_pairs={{0,8},{8,16},{16,24},{24,32},{32,40},{40,48},{48,56},{56,0},{1,9},... | collective-permute-start | bytes 344072 | tf_op jit(solution)/shard_map/ppermute | solution.py:876
  68.8 6.8 %collective-permute-start.10 = (f32[256,128]{1,0:T(8,128)S(1)}, f32[256,128]{1,0:T(8,128)S(1)}, u32[]{:S(2)}, u32[]{:S(2)}) collective-permute-start(f32[256,128]{1,0:T(8,128)S(1)} %get-tuple-element.185), channel_id=1, source_target_pairs={{0,1},{1,2},{2,3},{3,4},{4,5},{5,6},{6,7},{7,0},{8,9},{9,10},{10,1... | collective-permute-start | bytes 393224 | tf_op jit(solution)/shard_map/ppermute | solution.py:876
  68.9 6.7 %collective-permute-start.11 = (f32[256,128]{1,0:T(8,128)S(1)}, f32[256,128]{1,0:T(8,128)S(1)}, u32[]{:S(2)}, u32[]{:S(2)}) collective-permute-start(f32[256,128]{1,0:T(8,128)S(1)} %get-tuple-element.184), channel_id=1, source_target_pairs={{0,7},{1,0},{2,1},{3,2},{4,3},{5,4},{6,5},{7,6},{8,15},{9,8},{10,9... | collective-permute-start | bytes 393224 | tf_op jit(solution)/shard_map/ppermute | solution.py:876
  76.8 5.4 %collective-permute-start.13 = (f32[224,128]{1,0:T(8,128)S(1)}, f32[224,128]{1,0:T(8,128)S(1)}, u32[]{:S(2)}, u32[]{:S(2)}) collective-permute-start(f32[224,128]{1,0:T(8,128)S(1)} %get-tuple-element.136), channel_id=1, source_target_pairs={{0,56},{8,0},{16,8},{24,16},{32,24},{40,32},{48,40},{56,48},{1,57}... | collective-permute-start | bytes 344072 | tf_op jit(solution)/shard_map/ppermute | solution.py:876
  77.2 5.0 %collective-permute-start.12 = (f32[224,128]{1,0:T(8,128)S(1)}, f32[224,128]{1,0:T(8,128)S(1)}, u32[]{:S(2)}, u32[]{:S(2)}) collective-permute-start(f32[224,128]{1,0:T(8,128)S(1)} %get-tuple-element.135), channel_id=1, source_target_pairs={{0,8},{8,16},{16,24},{24,32},{32,40},{40,48},{48,56},{56,0},{1,9},... | collective-permute-start | bytes 344072 | tf_op jit(solution)/shard_map/ppermute | solution.py:876
  82.4 6.2 %collective-permute-start.14 = (f32[256,128]{1,0:T(8,128)S(1)}, f32[256,128]{1,0:T(8,128)S(1)}, u32[]{:S(2)}, u32[]{:S(2)}) collective-permute-start(f32[256,128]{1,0:T(8,128)S(1)} %get-tuple-element.183), channel_id=1, source_target_pairs={{0,1},{1,2},{2,3},{3,4},{4,5},{5,6},{6,7},{7,0},{8,9},{9,10},{10,1... | collective-permute-start | bytes 393224 | tf_op jit(solution)/shard_map/ppermute | solution.py:876
  82.5 6.1 %collective-permute-start.15 = (f32[256,128]{1,0:T(8,128)S(1)}, f32[256,128]{1,0:T(8,128)S(1)}, u32[]{:S(2)}, u32[]{:S(2)}) collective-permute-start(f32[256,128]{1,0:T(8,128)S(1)} %get-tuple-element.182), channel_id=1, source_target_pairs={{0,7},{1,0},{2,1},{3,2},{4,3},{5,4},{6,5},{7,6},{8,15},{9,8},{10,9... | collective-permute-start | bytes 393224 | tf_op jit(solution)/shard_map/ppermute | solution.py:876
  89.8 5.5 %collective-permute-start.17 = (f32[224,128]{1,0:T(8,128)S(1)}, f32[224,128]{1,0:T(8,128)S(1)}, u32[]{:S(2)}, u32[]{:S(2)}) collective-permute-start(f32[224,128]{1,0:T(8,128)S(1)} %get-tuple-element.152), channel_id=1, source_target_pairs={{0,56},{8,0},{16,8},{24,16},{32,24},{40,32},{48,40},{56,48},{1,57}... | collective-permute-start | bytes 344072 | tf_op jit(solution)/shard_map/ppermute | solution.py:876
  90.2 5.2 %collective-permute-start.16 = (f32[224,128]{1,0:T(8,128)S(1)}, f32[224,128]{1,0:T(8,128)S(1)}, u32[]{:S(2)}, u32[]{:S(2)}) collective-permute-start(f32[224,128]{1,0:T(8,128)S(1)} %get-tuple-element.151), channel_id=1, source_target_pairs={{0,8},{8,16},{16,24},{24,32},{32,40},{40,48},{48,56},{56,0},{1,9},... | collective-permute-start | bytes 344072 | tf_op jit(solution)/shard_map/ppermute | solution.py:876
  95.5 6.8 %collective-permute-start.18 = (f32[256,128]{1,0:T(8,128)S(1)}, f32[256,128]{1,0:T(8,128)S(1)}, u32[]{:S(2)}, u32[]{:S(2)}) collective-permute-start(f32[256,128]{1,0:T(8,128)S(1)} %get-tuple-element.181), channel_id=1, source_target_pairs={{0,1},{1,2},{2,3},{3,4},{4,5},{5,6},{6,7},{7,0},{8,9},{9,10},{10,1... | collective-permute-start | bytes 393224 | tf_op jit(solution)/shard_map/ppermute | solution.py:876
  95.6 6.8 %collective-permute-start.19 = (f32[256,128]{1,0:T(8,128)S(1)}, f32[256,128]{1,0:T(8,128)S(1)}, u32[]{:S(2)}, u32[]{:S(2)}) collective-permute-start(f32[256,128]{1,0:T(8,128)S(1)} %get-tuple-element.180), channel_id=1, source_target_pairs={{0,7},{1,0},{2,1},{3,2},{4,3},{5,4},{6,5},{7,6},{8,15},{9,8},{10,9... | collective-permute-start | bytes 393224 | tf_op jit(solution)/shard_map/ppermute | solution.py:876
  104.6 30.7 %all-to-all-start.1 = ((f32[8,224,128]{2,1,0:T(8,128)}), f32[8,224,128]{2,1,0:T(8,128)S(1)}, u32[]{:S(2)}, u32[]{:S(2)}) async-start(f32[8,224,128]{2,1,0:T(8,128)} %get-tuple-element.159), calls=%async_computation.1 | async-start | bytes 1835008 | tf_op jit(solution)/shard_map/all_to_all | solution.py:1028
  108.8 26.4 %copy-start.4 = (s32[8]{0:T(128)S(1)}, s32[8]{0:T(128)}, u32[]{:S(2)}) copy-start(s32[8]{0:T(128)} %slot_ref.5) | copy-start | bytes 100

commit v3 on v2

--- a/solution.py
+++ b/solution.py
@@ -49,7 +49,9 @@
 ROWS = B * PLANE
 PADDED = 64
 PADROWS = (B + 2) * PADDED
-BLOCKROWS = 7 * 32 * 8
+ROW = 7 * 32
+HALF = ROW // 2
+BLOCKROWS = ROW * 8
 F32 = jnp.float32
 VMEM = pl.BlockSpec(memory_space=pltpu.VMEM)
 SMEM = pl.BlockSpec(memory_space=pltpu.SMEM)
@@ -89,10 +91,6 @@
     return pltpu.VMEM(dims, dtype)
 
 
-def stored(*dims, dtype=F32):
-    return pltpu.HBM(dims, dtype)
-
-
 def lanes(rows):
     return lax.broadcasted_iota(jnp.int32, (rows, L), 1)
 
@@ -174,42 +172,77 @@
     return jnp.take_along_axis(x, index, axis=axis, mode="promise_in_bounds")
 
 
-def send_blocks(pick, blocks_ref, out_ref, hold_ref, sems):
-    copies = []
-    for dest in range(8):
-        hold_ref[dest] = blocks_ref[pl.ds(pick(dest), BLOCKROWS // 8, stride=8), :]
-        copies.append(pltpu.make_async_copy(hold_ref.at[dest], out_ref.at[dest], sems.at[dest]))
-        copies[-1].start()
-    return copies
-
-
-def gather_kernel(slot_ref, state_ref, send_ref, blocks_ref, hold_ref, sems):
-    def slot_for(dest):
-        slot = jnp.int32(0)
-        for s in range(8):
-            home = slot_ref[s]
-            slot = jnp.where((home >= 0) & (home // 8 == dest), s, slot)
-        return slot
-
-    load = pltpu.make_async_copy(state_ref, blocks_ref, sems.at[8])
+PARTS = (
+    (0, 0, 0, ROW, 0),
+    (7, 1, 0, ROW, 0),
+    (1, 2, 0, ROW, 0),
+    (6, 3, 0, ROW, 0),
+    (2, 4, 0, ROW, 0),
+    (5, 5, 0, ROW, 0),
+    (3, 6, 0, ROW, 0),
+    (4, 5, ROW, HALF, 0),
+    (4, 6, ROW, HALF, HALF),
+)
+
+
+def find(slots, home):
+    found = jnp.int32(-1)
+    for k, slot in enumerate(slots):
+        found = jnp.where((slot >= 0) & (slot // 8 == home), k, found)
+    return found
+
+
+def fill_messages(me, slots, blocks_ref, outs):
+    own, up1, down1, up2, down2, up3, down3 = outs
+    for off, ref in ((0, own), (1, up1), (7, down1), (2, up2), (6, down2), (3, up3), (5, down3)):
+        at = jnp.maximum(find(slots, (me + off) & 7), 0)
+        ref[pl.ds(0, ROW), :] = blocks_ref[pl.ds(at, ROW, stride=8), :]
+    at = jnp.maximum(find(slots, (me + 4) & 7), 0)
+    up1[pl.ds(ROW, HALF), :] = blocks_ref[pl.ds(at, HALF, stride=8), :]
+    down1[pl.ds(ROW, HALF), :] = blocks_ref[pl.ds(HALF * 8 + at, HALF, stride=8), :]
+
+
+def receive(me, slots, refs, out_ref):
+    for k, slot in enumerate(slots):
+
+        @pl.when(slot < 0)
+        def _():
+            out_ref[pl.ds(k, ROW, stride=8), :] = jnp.zeros((ROW, L), F32)
+
+    for off, k, at, count, first in PARTS:
+        slot = find(slots, (me + off) & 7)
+
+        @pl.when(slot >= 0)
+        def _():
+            out_ref[pl.ds(first * 8 + slot, count, stride=8), :] = refs[k][pl.ds(at, count), :]
+
+
+def gather_kernel(me_ref, slot_ref, state_ref, *refs):
+    *outs, blocks_ref, sem = refs
+    load = pltpu.make_async_copy(state_ref, blocks_ref, sem)
     load.start()
     load.wait()
-    for copy in send_blocks(slot_for, blocks_ref, send_ref, hold_ref, sems):
-        copy.wait()
-
-
-def spread_kernel(slot_ref, recv_ref, *refs):
-    *refs, turn_ref, sems = refs
-    sources, dense_ref, targets = refs[:6], refs[6], refs[7:]
-    loads = [
-        pltpu.make_async_copy(source, target, sems.at[k])
-        for k, (source, target) in enumerate(zip(sources, targets))
-    ]
-    for load in loads:
-        load.start()
-    for tile in range(8):
-        owner = jnp.maximum(slot_ref[0, 0, tile], 0) // 8
-        turn_ref[pl.ds(tile, BLOCKROWS // 8, stride=8), :] = recv_ref[owner]
+    fill_messages(me_ref[0], [slot_ref[s] for s in range(8)], blocks_ref, outs)
+
+
+def pick_kernel(me_ref, slot_ref, *refs):
+    for tile, out_ref in ((0, refs[-2]), (7, refs[-1])):
+        slot = slot_ref[0, 0, tile]
+
+        @pl.when(slot < 0)
+        def _():
+            out_ref[...] = jnp.zeros((ROW, L), F32)
+
+        for off, k, at, count, first in PARTS:
+
+            @pl.when((slot >= 0) & (slot // 8 == ((me_ref[0] + off) & 7)))
+            def _():
+                out_ref[pl.ds(first, count), :] = refs[k][pl.ds(at, count), :]
+
+
+def spread_kernel(me_ref, slot_ref, *refs):
+    *blocks, dense_ref, turn_ref = refs
+    receive(me_ref[0], [slot_ref[0, 0, tile] for tile in range(8)], blocks, turn_ref)
 
     def body(group, carry):
         for i in range(32):
@@ -218,8 +251,6 @@
         return carry
 
     lax.fori_loop(0, BLOCKROWS // 256, body, 0)
-    for load in loads:
-        load.wait()
 
 
 def pack_columns(load, low_ref, high_ref, at):
@@ -264,9 +295,12 @@
 
 
 def ring_kernel(
-    flag_ref, pops_ref, mask_ref, right_ref, left_ref,
-    side_ref, ring_ref, aux_ref, mask_out, bits_ref,
+    flag_ref, pops_in, mask_ref, right_ref, left_ref,
+    pops_ref, side_ref, ring_ref, aux_ref, mask_out, bits_ref, sem,
 ):
+    load = pltpu.make_async_copy(pops_in, pops_ref, sem)
+    load.start()
+
     def body(group, carry):
         at = pl.ds(pl.multiple_of(group * 8, 8), 8)
         right, left = right_ref[at, :], left_ref[at, :]
@@ -288,6 +322,8 @@
     mask_out[...] = jnp.zeros_like(mask_out)
     for z in range(B):
         put_rows(mask_out, z + 1, ring_ref[pl.ds(z * PLANE, PLANE), :])
+
+    load.wait()
 
     def flow(z, carry):
         set_bits(mask_out, bits_ref, z)
@@ -786,87 +822,89 @@
         )
 
 
-def inner_kernel(last, *refs):
-    pops_in, side_in, post_in, aux_in, flow_in, solute_in, bits_ref, open_ref = refs[:8]
-    y_refs = refs[8:10]
-    if last:
-        pops_ref, flow_ref, solute_ref, turn_ref = refs[10:]
-        state, out = (pops_ref, side_in, post_in, aux_in), (pops_ref, None, None, None)
-    else:
-        *state, flow_ref, solute_ref = refs[10:]
-        out = state
+def inner_kernel(*refs):
+    bits_ref, open_ref, ylo_ref, yhi_ref = refs[6:10]
+    *state, flow_ref, solute_ref = refs[10:]
     pops_ref, side_ref, post_ref, aux_ref = state
+    y_refs = ylo_ref, yhi_ref
     fix_rows((pops_ref, side_ref), post_ref, aux_ref, bits_ref, y_refs, flow_ref, solute_ref)
     collide_y_halos(post_ref, open_ref, y_refs, None, flow_ref)
+
+    def body(z, carry):
+        pull(z, state, bits_ref, flow_ref, solute_ref)
+        return carry
+
+    lax.fori_loop(2, B - 2, body, 0, unroll=UNROLL)
+
+
+def inner_last_kernel(*refs):
+    pops_ref, side_ref, post_ref, aux_ref = refs[:4]
+    bits_ref, open_ref, ylo_ref, yhi_ref, flow_ref, solute_ref, turn_ref = refs[6:]
+    y_refs = ylo_ref, yhi_ref
+    fix_rows((pops_ref, side_ref), post_ref, aux_ref, bits_ref, y_refs, flow_ref, solute_ref)
 
     def turn(z, carry):
         turn_plane(turn_ref, z, [plane(solute_ref, z, i) for i in range(7)])
         return carry
 
-    def body(z, carry):
-        pull(z, out, bits_ref, flow_ref, solute_ref)
-        return carry
-
-    if last:
-        lax.fori_loop(1, B - 1, turn, 0, unroll=UNROLL)
-    lax.fori_loop(2, B - 2, body, 0, unroll=UNROLL)
-
-
-def edge_kernel(last, *refs):
-    if last:
-        slot_ref, refs = refs[0], refs[1:]
-    pops_in, side_in, post_in, aux_in, flow_in, solute_in, bits_ref, open_ref = refs[:8]
-    y_refs, z_refs = refs[8:10], refs[10:12]
-    if last:
-        pops_ref, flow_ref, turn_ref, send_ref, hold_ref, sems = refs[12:]
-        state, out = (pops_ref, side_in, post_in, aux_in), (pops_ref, None, None, None)
-        solute_ref = None
-    else:
-        *state, flow_ref, solute_ref, ydn_ref, yup_ref = refs[12:]
-        out = state
+    lax.fori_loop(1, B - 1, turn, 0, unroll=UNROLL)
+    collide_y_halos(post_ref, open_ref, y_refs, None, flow_ref)
+
+
+def edge_solute(z, post_ref, bits_ref, y_refs, z_refs):
+    fills = [spread8(read_row(y_refs[side], NORM, z)) for side in range(2)]
+    below = read_field(z_refs[0], NORM) if z == 0 else plane(post_ref, z - 1, 5)
+    above = read_field(z_refs[1], NORM) if z == B - 1 else plane(post_ref, z + 1, 6)
+    return stream_solute(z, post_ref, plane(bits_ref, z), fills, below, above)
+
+
+def edge_kernel(*refs):
+    bits_ref, open_ref, ylo_ref, yhi_ref, zlo_ref, zhi_ref = refs[6:12]
+    *state, flow_ref, solute_ref, ydn_ref, yup_ref = refs[12:]
     pops_ref, side_ref, post_ref, aux_ref = state
-    solutes = []
+    y_refs, z_refs = (ylo_ref, yhi_ref), (zlo_ref, zhi_ref)
     for z in (0, B - 1):
-        bits = plane(bits_ref, z)
-        fills = [spread8(read_row(y_refs[side], NORM, z)) for side in range(2)]
-        below = read_field(z_refs[0], NORM) if z == 0 else plane(post_ref, z - 1, 5)
-        above = read_field(z_refs[1], NORM) if z == B - 1 else plane(post_ref, z + 1, 6)
-        solutes.append(stream_solute(z, post_ref, bits, fills, below, above))
-        if last:
-            turn_plane(turn_ref, z, solutes[-1])
-        else:
-            put_solute(solute_ref, z, solutes[-1])
-    if last:
-
-        def tile_for(owner):
-            tile = jnp.int32(0)
-            for j in range(8):
-                slot = slot_ref[0, 0, j]
-                tile = jnp.where((slot >= 0) & (slot // 8 == owner), j, tile)
-            return tile
-
-        copies = send_blocks(tile_for, turn_ref, send_ref, hold_ref, sems)
+        solute = edge_solute(z, post_ref, bits_ref, y_refs, z_refs)
+        put_solute(solute_ref, z, solute)
+        push(z, (pops_ref, side_ref), aux_ref, plane(bits_ref, z), solute, flow_ref)
     collide_y_halos(post_ref, open_ref, y_refs, z_refs, flow_ref)
     collide_z_halos(post_ref, open_ref, y_refs, z_refs, flow_ref)
-    for z, solute in zip((0, B - 1), solutes):
+    for z in (0, 1, B - 2, B - 1):
+        pull(z, state, bits_ref, flow_ref, solute_ref)
+    write_y_messages(
+        (pops_ref, side_ref), post_ref, aux_ref, (ydn_ref, yup_ref), bits_ref=bits_ref
+    )
+
+
+def send_kernel(me_ref, slot_ref, *refs):
+    post_ref, bits_ref, ylo_ref, yhi_ref, zlo_ref, zhi_ref = refs[2:8]
+    solute_ref, turn_ref, *outs = refs[8:]
+    for z in (0, B - 1):
+        solute = edge_solute(z, post_ref, bits_ref, (ylo_ref, yhi_ref), (zlo_ref, zhi_ref))
+        put_solute(solute_ref, z, solute)
+        turn_plane(turn_ref, z, solute)
+    fill_messages(me_ref[0], [slot_ref[0, 0, j] for j in range(8)], turn_ref, outs)
+
+
+def last_kernel(*refs):
+    pops_ref, side_ref, post_ref, aux_ref, flow_in, solute_ref, bits_ref, open_ref = refs[:8]
+    y_refs, z_refs = refs[8:10], refs[10:12]
+    out_ref, flow_ref = refs[12:]
+    for z in (0, B - 1):
+        solute = [plane(solute_ref, z, i) for i in range(7)]
         push(z, (pops_ref, side_ref), aux_ref, plane(bits_ref, z), solute, flow_ref)
-
-    for z in (0, 1, B - 2, B - 1):
-        pull(z, out, bits_ref, flow_ref, solute_ref)
-    if last:
-        for copy in copies:
-            copy.wait()
-    else:
-        write_y_messages(
-            (pops_ref, side_ref), post_ref, aux_ref, (ydn_ref, yup_ref), bits_ref=bits_ref
-        )
-
-
-def scatter_kernel(slot_ref, recv_ref, out_ref):
-    for s in range(8):
-        home = slot_ref[s]
-        block = recv_ref[jnp.maximum(home, 0) // 8]
-        out_ref[pl.ds(s, BLOCKROWS // 8, stride=8), :] = jnp.where(home >= 0, block, 0.0)
+    collide_y_halos(post_ref, open_ref, y_refs, z_refs, flow_ref)
+    collide_z_halos(post_ref, open_ref, y_refs, z_refs, flow_ref)
+
+    def body(z, carry):
+        pull(z, (out_ref, None, None, None), bits_ref, flow_ref, None)
+        return carry
+
+    lax.fori_loop(0, B, body, 0, unroll=UNROLL)
+
+
+def scatter_kernel(me_ref, slot_ref, *refs):
+    receive(me_ref[0], [slot_ref[s] for s in range(8)], refs[:-1], refs[-1])
 
 
 def neighbours(low, high, axis):
@@ -874,6 +912,17 @@
     up = [(i, (i + 1) % count) for i in range(count)]
     down = [(i, (i - 1) % count) for i in range(count)]
     return lax.ppermute(high, axis, up), lax.ppermute(low, axis, down)
+
+
+def exchange_blocks(own, up1, down1, up2, down2, up3, down3):
+    def shifted(x, step):
+        return lax.ppermute(x, "gz", [(i, (i + step) % 8) for i in range(8)])
+
+    up1, down1 = shifted(up1, 1), shifted(down1, -1)
+    up2, down2 = shifted(up2, 2), shifted(down2, -2)
+    up3 = shifted(jnp.concatenate([up3, up1[ROW:]], axis=0), 3)
+    down3 = shifted(jnp.concatenate([down3, down1[ROW:]], axis=0), -3)
+    return own, up1, down1, up2, down2, up3, down3
 
 
 def inside():
@@ -897,47 +946,38 @@
 
 def shards(populations, solute_state, pore_mask, block_slot, slot_block):
     flags = inside()
-    hold = [pltpu.VMEM((8, BLOCKROWS // 8, L), F32), pltpu.SemaphoreType.DMA((9,))]
+    me = lax.axis_index("gz").astype(jnp.int32).reshape(1)
     turn = pltpu.VMEM((BLOCKROWS, L), F32)
-    send_out = pltpu.HBM((8, BLOCKROWS // 8, L), F32)
+    sent = tuple(held(n, L) for n in (ROW, ROW + HALF, ROW + HALF, ROW, ROW, ROW, ROW))
     state = solute_state.reshape(7, 8, 32, L).transpose(0, 2, 1, 3).reshape(BLOCKROWS, L)
     send = call(
-        gather_kernel, send_out, [SMEM, HBM], [turn] + hold, 1, 2 * 10**6, out_specs=HBM
-    )(slot_block, state)
-    recv = lax.all_to_all(send, "gz", split_axis=0, concat_axis=0, tiled=True)
+        gather_kernel, sent, [SMEM, SMEM, HBM], [turn, pltpu.SemaphoreType.DMA], 1, 2 * 10**6
+    )(me, slot_block, state)
+    recv = exchange_blocks(*send)
 
     pops = populations.reshape(19, 256, L)
     mask = pore_mask.reshape(256, L)
-    low, high = call(columns_kernel, (stored(320, L),) * 2, [VMEM] * 2, [], 1, 1)(pops, mask)
+    low, high = call(columns_kernel, (held(320, L),) * 2, [VMEM] * 2, [], 10**6, 13 * 10**6)(
+        pops, mask
+    )
     left, right = neighbours(low, high, "gx")
-    dims = ((19, 256, L), (ROWS, L), (4, ROWS, L), (PADROWS, L), (ROWS, L))
-    kinds = (F32,) * 4 + (jnp.int32,)
-    side, ring_mask, aux, mask, bits = call(
+    dims = ((19, 256, L), (19, 256, L), (ROWS, L), (4, ROWS, L), (PADROWS, L))
+    pops, side, ring_mask, aux, mask, bits = call(
         ring_kernel,
-        tuple(stored(*d, dtype=k) for d, k in zip(dims, kinds)),
-        [SMEM] + [VMEM] * 4,
-        [],
-        1,
-        1,
+        tuple(held(*d) for d in dims) + (held(ROWS, L, dtype=jnp.int32),),
+        [SMEM, HBM] + [VMEM] * 3,
+        [pltpu.SemaphoreType.DMA],
+        10**6,
+        20 * 10**6,
     )(flags, pops, mask, right, left)
 
-    after = jnp.minimum(bits[0, 0], 0)
-
-    def block_of(tile):
-        owner = jnp.maximum(block_slot[0, 0, tile], 0) // 8 + after
-        return lax.dynamic_index_in_dim(recv, owner, 0, keepdims=False)
-
-    left, right = neighbours(block_of(0), block_of(7), "gx")
-    state = (pops, side, ring_mask, aux, mask, bits)
-    dense, pops, side, ring_mask, aux, mask, bits = call(
-        spread_kernel,
-        (held(BLOCKROWS, L), held(19, 256, L))
-        + tuple(held(*d, dtype=k) for d, k in zip(dims, kinds)),
-        [SMEM, VMEM] + [HBM] * 6,
-        [turn, pltpu.SemaphoreType.DMA((6,))],
-        10**7,
-        2 * 10**6,
-    )(block_slot, recv, *state)
+    low, high = call(
+        pick_kernel, (held(ROW, L),) * 2, [SMEM] * 2 + [VMEM] * 8, [], 1, 10**6, keep=True
+    )(me, block_slot, *recv, bits)
+    left, right = neighbours(low, high, "gx")
+    dense = call(
+        spread_kernel, held(BLOCKROWS, L), [SMEM] * 2 + [VMEM] * 7, [turn], 10**6, 10**7, keep=True
+    )(me, block_slot, *recv)
     message = held((SIDES + MASK + 1) * B, L)
     post, ydn, yup = call(
         first_kernel,
@@ -978,15 +1018,16 @@
                 aliases={3: 0, 4: 1},
                 keep=True,
             )(flags, *y_halos, mask, bits)
-        outs = states[:1] + works + (held(BLOCKROWS, L),) if last else states + works
+        if last:
+            break
         moved = call(
-            functools.partial(inner_kernel, last),
-            outs,
+            inner_kernel,
+            states + works,
             [VMEM] * 10,
             [],
             10**7,
             10**7,
-            aliases={0: 0, 4: 1, 5: 2} if last else {i: i for i in range(6)},
+            aliases={i: i for i in range(6)},
             keep=True,
         )(*state, *work, bits, opens, *y_halos)
         if step == 0:
@@ -1000,22 +1041,8 @@
                 aliases={3: 0, 4: 1, 5: 2},
                 keep=True,
             )(flags, *z_halos, mask, bits, opens)
-        if last:
-            pops, flow, _, turned = moved
-            pops, _, _, send = call(
-                functools.partial(edge_kernel, True),
-                (states[0], works[0], held(BLOCKROWS, L), send_out),
-                [SMEM] + [VMEM] * 12,
-                hold,
-                10**7,
-                10**7,
-                aliases={1: 0, 5: 1, 6: 2},
-                keep=True,
-                out_specs=(VMEM, VMEM, VMEM, HBM),
-            )(block_slot, pops, *state[1:], flow, turned, bits, opens, *y_halos, *z_halos)
-            break
         *state, _, _, ydn, yup = call(
-            functools.partial(edge_kernel, False),
+            edge_kernel,
             states + works + (message, message),
             [VMEM] * 12,
             [],
@@ -1025,9 +1052,39 @@
             keep=True,
         )(*moved, bits, opens, *y_halos, *z_halos)
 
-    recv = lax.all_to_all(send, "gz", split_axis=0, concat_axis=0, tiled=True)
-    out = call(scatter_kernel, shape(BLOCKROWS, L), [SMEM, VMEM], [], 1, 2 * 10**6)(
-        slot_block, recv
+    flow, solute, turned = call(
+        inner_last_kernel,
+        works + (held(BLOCKROWS, L),),
+        [VMEM] * 10,
+        [],
+        10**7,
+        10**7,
+        aliases={4: 0, 5: 1},
+        keep=True,
+    )(*state, *work, bits, opens, *y_halos)
+    solute, _, *send = call(
+        send_kernel,
+        (works[1], held(BLOCKROWS, L)) + sent,
+        [SMEM] * 2 + [VMEM] * 8,
+        [],
+        10**6,
+        10**6,
+        aliases={2: 0, 3: 1},
+        keep=True,
+    )(me, block_slot, solute, turned, state[2], bits, *y_halos, *z_halos)
+    recv = exchange_blocks(*send)
+    pops, _ = call(
+        last_kernel,
+        (shape(19, 256, L), works[0]),
+        [VMEM] * 12,
+        [],
+        10**7,
+        10**7,
+        aliases={4: 1},
+        keep=True,
+    )(*state, flow, solute, bits, opens, *y_halos, *z_halos)
+    out = call(scatter_kernel, shape(BLOCKROWS, L), [SMEM] * 2 + [VMEM] * 7, [], 1, 2 * 10**6)(
+        me, slot_block, *recv
     )
     new_solute = out.reshape(7, 32, 8, L).transpose(0, 2, 1, 3).reshape(7, 8, 4096)
     return pops.reshape(19, B, B, L), new_solute

time: 137 us -> 133 us (0.971)
  starting transfers between devices: 42.3 us -> 58.9 us
  waiting for transfers between devices: 38.4 us -> 23.6 us
  Pallas kernels: 48.5 us -> 44.7 us
  between operations: 2.92 us -> 1.11 us
    all_to_all x2 -> x0, waiting for transfers between devices: 30.2 us -> none  [shards(): recv = lax.all_to_all(send, 'gz', split_axis=0, concat_axis=0, tiled=True)]
    ppermute x0 -> x12, starting transfers between devices: none -> 25.4 us  [shifted(): return lax.ppermute(x, 'gz', [(i, (i + step) % 8) for i in range(8)])]
    ppermute x0 -> x12, waiting for transfers between devices: none -> 16.2 us  [shifted(): return lax.ppermute(x, 'gz', [(i, (i + step) % 8) for i in range(8)])]
    all_to_all x2 -> x0, starting transfers between devices: 12.5 us -> none  [shards(): recv = lax.all_to_all(send, 'gz', split_axis=0, concat_axis=0, tiled=True)]
    pallas_call x20 -> x22, Pallas kernels: 48.5 us -> 44.7 us  [placed(): return run(*map(place, args, in_specs))]
    ppermute x20, starting transfers between devices: 29.8 us -> 33.5 us  [neighbours(): return (lax.ppermute(high, axis, up), lax.ppermute(low, axis, down))]
    slice x2 -> x4, local copies, waits for them, and re-layouts: 1.79 us -> 0.02 us  [the longest x2 0.01 us: exchange_blocks(): down3 = shifted(jnp.concatenate([down3, down1[ROW:]], axis=0), -3)]
    unnamed x23 -> x24, local copies, waits for them, and re-layouts: 2.3 us -> 3.34 us
  transfers between devices with their start and end apart: 22 -> 32, of which waited for: 11 -> 16; matrix products, arithmetic and copies ran while one was open for 3% -> 0% of each run, Pallas kernels for 26% -> 25%
where the time goes in v3:
time: 133 us; the launch traced here: 132 us
  starting transfers between devices  58.9 us (44%)
  Pallas kernels  44.7 us (34%)
  waiting for transfers between devices  23.6 us (18%)
  local copies, waits for them, and re-layouts  3.72 us (3%)
    pallas_call x22, Pallas kernels, placed(): return run(*map(place, args, in_specs))  44.7 us
    ppermute x20, starting transfers between devices, neighbours(): return (lax.ppermute(high, axis, up), lax.ppermute(low, axis, down))  33.5 us
    ppermute x12, starting transfers between devices, shifted(): return lax.ppermute(x, 'gz', [(i, (i + step) % 8) for i in range(8)])  25.4 us
    ppermute x12, waiting for transfers between devices, shifted(): return lax.ppermute(x, 'gz', [(i, (i + step) % 8) for i in range(8)])  16.2 us
    ppermute x20, waiting for transfers between devices, neighbours(): return (lax.ppermute(high, axis, up), lax.ppermute(low, axis, down))  7.38 us
    unnamed x24, local copies, waits for them, and re-layouts  3.34 us
  transfers between devices with their start and end apart: 32, of which 16 were waited for; matrix products, arithmetic and copies ran while one was open for 0% of the time, Pallas kernels for 25%

profile of v3, /device:TPU:7, one launch (start us, length us, event | category | flops | bytes accessed | tf_op | source)
XLA Modules:
  0.0 132.5 jit_solution(6653338636082683473)
XLA Ops:
  0.7 0.7 copy-done.4
  1.3 2.0 %shard_map.70 = (f32[224,128]{1,0:T(8,128)S(1)}, f32[336,128]{1,0:T(8,128)S(1)}, f32[336,128]{1,0:T(8,128)S(1)}, f32[224,128]{1,0:T(8,128)S(1)}, f32[224,128]{1,...) custom-call(s32[1]{0:T(128)} %bitcast.8.me_ref, s32[8]{0:T(128)S(1)} %copy-done.4, f32[1792,128]{1,0:T(8,128)} %bitcast.85), custom_call_target="tpu_custom_call" | custom-call | flops 1 | bytes 2000000 | tf_op jit(solution)/shard_map/pallas_call | solution.py:81
  3.3 1.7 %collective-permute-start.2 = (f32[336,128]{1,0:T(8,128)S(1)}, f32[336,128]{1,0:T(8,128)S(1)}, u32[]{:S(2)}, u32[]{:S(2)}) collective-permute-start(f32[336,128]{1,0:T(8,128)S(1)} %get-tuple-element.96), channel_id=1, source_target_pairs={{0,1},{1,2},{2,3},{3,4},{4,5},{5,6},{6,7},{7,0},{8,9},{9,10},{10,1... | collective-permute-start | bytes 516104 | tf_op jit(solution)/shard_map/ppermute | solution.py:919
  5.0 4.0 %collective-permute-start.3 = (f32[336,128]{1,0:T(8,128)S(1)}, f32[336,128]{1,0:T(8,128)S(1)}, u32[]{:S(2)}, u32[]{:S(2)}) collective-permute-start(f32[336,128]{1,0:T(8,128)S(1)} %get-tuple-element.97), channel_id=1, source_target_pairs={{0,7},{1,0},{2,1},{3,2},{4,3},{5,4},{6,5},{7,6},{8,15},{9,8},{10,9... | collective-permute-start | bytes 516104 | tf_op jit(solution)/shard_map/ppermute | solution.py:919
  9.1 1.7 %copy-done = f32[19,16,16,128]{3,2,1,0:T(8,128)S(1)} copy-done((f32[19,16,16,128]{3,2,1,0:T(8,128)S(1)}, f32[19,16,16,128]{3,2,1,0:T(8,128)}, u32[]{:S(2)}) %copy-start) | copy-done | bytes 2490392
  10.8 0.9 copy-done.1
  11.7 2.7 %shard_map.68 = (f32[320,128]{1,0:T(8,128)S(1)}, f32[320,128]{1,0:T(8,128)S(1)}) custom-call(f32[19,256,128]{2,1,0:T(8,128)S(1)} %bitcast.73, s32[256,128]{1,0:T(8,128)S(1)} %bitcast.78), custom_call_target="tpu_custom_call" | custom-call | flops 1000000 | bytes 13000000 | tf_op jit(solution)/shard_map/pallas_call | solution.py:81
  14.4 2.8 %collective-permute-start = (f32[320,128]{1,0:T(8,128)S(1)}, f32[320,128]{1,0:T(8,128)S(1)}, u32[]{:S(2)}, u32[]{:S(2)}) collective-permute-start(f32[320,128]{1,0:T(8,128)S(1)} %get-tuple-element.91), channel_id=1, source_target_pairs={{0,192},{64,0},{128,64},{192,128},{1,193},{65,1},{129,65},{193,129... | collective-permute-start | bytes 491528 | tf_op jit(solution)/shard_map/ppermute | solution.py:914
  17.3 1.6 %collective-permute-start.6 = (f32[336,128]{1,0:T(8,128)S(1)}, f32[336,128]{1,0:T(8,128)S(1)}, u32[]{:S(2)}, u32[]{:S(2)}) collective-permute-start(f32[336,128]{1,0:T(8,128)S(1)} %pad_maximum_fusion), channel_id=1, source_target_pairs={{0,3},{1,4},{2,5},{3,6},{4,7},{5,0},{6,1},{7,2},{8,11},{9,12},{10,... | collective-permute-start | bytes 516104 | tf_op jit(solution)/shard_map/ppermute | solution.py:919
  18.9 3.0 %collective-permute-start.7 = (f32[336,128]{1,0:T(8,128)S(1)}, f32[336,128]{1,0:T(8,128)S(1)}, u32[]{:S(2)}, u32[]{:S(2)}) collective-permute-start(f32[336,128]{1,0:T(8,128)S(1)} %pad_maximum_fusion.1), channel_id=1, source_target_pairs={{0,5},{1,6},{2,7},{3,0},{4,1},{5,2},{6,3},{7,4},{8,13},{9,14},{10,... | collective-permute-start | bytes 516104 | tf_op jit(solution)/shard_map/ppermute | solution.py:919
  21.9 3.6 %collective-permute-start.5 = (f32[224,128]{1,0:T(8,128)S(1)}, f32[224,128]{1,0:T(8,128)S(1)}, u32[]{:S(2)}, u32[]{:S(2)}) collective-permute-start(f32[224,128]{1,0:T(8,128)S(1)} %get-tuple-element.99), channel_id=1, source_target_pairs={{0,6},{1,7},{2,0},{3,1},{4,2},{5,3},{6,4},{7,5},{8,14},{9,15},{10,... | collective-permute-start | bytes 344072 | tf_op jit(solution)/shard_map/ppermute | solution.py:919
  25.6 2.0 %collective-permute-done.1.left_ref = f32[320,128]{1,0:T(8,128)S(1)} collective-permute-done((f32[320,128]{1,0:T(8,128)S(1)}, f32[320,128]{1,0:T(8,128)S(1)}, u32[]{:S(2)}, u32[]{:S(2)}) %collective-permute-start.1) | collective-permute-done | bytes 163872 | tf_op jit(solution)/shard_map/ppermute | solution.py:914
  27.6 4.8 %shard_map.69 = (f32[19,256,128]{2,1,0:T(8,128)S(1)}, f32[19,256,128]{2,1,0:T(8,128)S(1)}, f32[512,128]{1,0:T(8,128)S(1)}, f32[4,512,128]{2,1,0:T(8,128)S(1)}, f...) custom-call(f32[6]{0:T(128)S(1)} %convert_element_type.3.flag_ref, f32[19,256,128]{2,1,0:T(8,128)} %bitcast.72, ...), custom_call_target="tpu_custom_call" | custom-call | flops 1000000 | bytes 20000000 | tf_op jit(solution)/shard_map/pallas_call | solution.py:81
  32.4 0.3 collective-permute-done.4.refs_3_
  32.7 2.0 %collective-permute-done.5.refs_4_ = f32[224,128]{1,0:T(8,128)S(1)} collective-permute-done((f32[224,128]{1,0:T(8,128)S(1)}, f32[224,128]{1,0:T(8,128)S(1)}, u32[]{:S(2)}, u32[]{:S(2)}) %collective-permute-start.5) | collective-permute-done | bytes 114720 | tf_op jit(solution)/shard_map/ppermute | solution.py:919
  34.7 0.7 shard_map.72
  35.6 1.5 %collective-permute-start.9 = (f32[224,128]{1,0:T(8,128)S(1)}, f32[224,128]{1,0:T(8,128)S(1)}, u32[]{:S(2)}, u32[]{:S(2)}) collective-permute-start(f32[224,128]{1,0:T(8,128)S(1)} %get-tuple-element.104), channel_id=1, source_target_pairs={{0,64},{64,128},{128,192},{192,0},{1,65},{65,129},{129,193},{193,1... | collective-permute-start | bytes 344072 | tf_op jit(solution)/shard_map/ppermute | solution.py:914
  37.0 2.2 %shard_map.71.dense_ref = f32[1792,128]{1,0:T(8,128)S(1)} custom-call(s32[1]{0:T(128)} %bitcast.8.me_ref, s32[1,1,8]{2,1,0:T(1,128)S(1)} %copy-done.3, f32[224,128]{1,0:T(8,128)S(1)} %get-tuple-element.95.refs_0_, f32[336,128]{1,0:T(8,128)S(1)} %collective-permute-done.2.refs_1_, f32[336,128]{1,0:T(8,128)S(1)} %collective-permute-done.3.refs_2_, ...), custom_call_target="tpu_custom_call" | custom-call | flops 1000000 | bytes 10000000 | tf_op jit(solution)/shard_map/pallas_call | solution.py:81
  39.2 1.2 collective-permute-done.9.left_ref
  40.5 2.0 %shard_map.73 = (f32[7,512,128]{2,1,0:T(8,128)S(1)}, f32[240,128]{1,0:T(8,128)S(1)}, f32[240,128]{1,0:T(8,128)S(1)}) custom-call(f32[1792,128]{1,0:T(8,128)S(1)} %shard_map.71.dense_ref, f32[224,128]{1,0:T(8,128)S(1)} %collective-permute-done.8.right_ref, f32[224,128]{1,0:T(8,128)S(1)} %collective-permute-done.9.left_ref, ...), custom_call_target="tpu_custom_call" | custom-call | flops 10000000 | bytes 10000000 | tf_op jit(solution)/shard_map/pallas_call | solution.py:81
  42.5 4.5 %collective-permute-start.11 = (f32[240,128]{1,0:T(8,128)S(1)}, f32[240,128]{1,0:T(8,128)S(1)}, u32[]{:S(2)}, u32[]{:S(2)}) collective-permute-start(f32[240,128]{1,0:T(8,128)S(1)} %get-tuple-element.111), channel_id=1, source_target_pairs={{0,56},{8,0},{16,8},{24,16},{32,24},{40,32},{48,40},{56,48},{1,57}... | collective-permute-start | bytes 368648 | tf_op jit(solution)/shard_map/ppermute | solution.py:914
  47.2 2.2 %shard_map.74 = (f32[240,128]{1,0:T(8,128)S(1)}, f32[240,128]{1,0:T(8,128)S(1)}, f32[19,1152,128]{2,1,0:T(8,128)S(1)}, f32[7,512,128]{2,1,0:T(8,128)S(1)}) custom-call(f32[19,256,128]{2,1,0:T(8,128)S(1)} %get-tuple-element.93.pops_ref.refs_0_, f32[19,256,128]{2,1,0:T(8,128)S(1)} %get-tuple-element.94.side_ref.refs_1_, ...), custom_call_target="tpu_custom_call" | custom-call | flops 10000000 | bytes 10000000 | tf_op jit(solution)/shard_map/pallas_call | solution.py:81
  49.3 0.3 collective-permute-done.11.yhi_ref.refs_9_
  49.8 4.4 %collective-permute-start.12 = (f32[272,128]{1,0:T(8,128)S(1)}, f32[272,128]{1,0:T(8,128)S(1)}, u32[]{:S(2)}, u32[]{:S(2)}) collective-permute-start(f32[272,128]{1,0:T(8,128)S(1)} %get-tuple-element.197), channel_id=1, source_target_pairs={{0,1},{1,2},{2,3},{3,4},{4,5},{5,6},{6,7},{7,0},{8,9},{9,10},{10,1... | collective-permute-start | bytes 417800 | tf_op jit(solution)/shard_map/ppermute | solution.py:914
  54.2 0.4 collective-permute-start.13
  54.7 0.7 shard_map.75
  55.4 2.7 %shard_map.76 = (f32[19,256,128]{2,1,0:T(8,128)S(1)}, f32[19,256,128]{2,1,0:T(8,128)S(1)}, f32[7,512,128]{2,1,0:T(8,128)S(1)}, f32[4,512,128]{2,1,0:T(8,128)S(1)...) custom-call(f32[19,256,128]{2,1,0:T(8,128)S(1)} %get-tuple-element.9, ...), custom_call_target="tpu_custom_call", output_to_operand_aliasing={{0}: (0, {}), {1}: (1, {}), {2}: (2, {}), {3}: (3, {}), {4}... | custom-call | flops 10000000 | bytes 10000000 | tf_op jit(solution)/shard_map/pallas_call | solution.py:81
  58.1 0.8 collective-permute-done.13.zhi_ref.refs_11_
  58.9 0.9 shard_map.77
  59.8 1.2 shard_map.78
  61.0 2.9 %collective-permute-start.15 = (f32[224,128]{1,0:T(8,128)S(1)}, f32[224,128]{1,0:T(8,128)S(1)}, u32[]{:S(2)}, u32[]{:S(2)}) collective-permute-start(f32[224,128]{1,0:T(8,128)S(1)} %get-tuple-element.133), channel_id=1, source_target_pairs={{0,56},{8,0},{16,8},{24,16},{32,24},{40,32},{48,40},{56,48},{1,57}... | collective-permute-start | bytes 344072 | tf_op jit(solution)/shard_map/ppermute | solution.py:914
  63.9 1.3 collective-permute-start.14
  65.3 2.1 %shard_map.79 = (f32[224,128]{1,0:T(8,128)S(1)}, f32[224,128]{1,0:T(8,128)S(1)}, f32[19,1152,128]{2,1,0:T(8,128)S(1)}, f32[7,512,128]{2,1,0:T(8,128)S(1)}) custom-call(f32[19,256,128]{2,1,0:T(8,128)S(1)} %get-tuple-element.126.refs_0_, f32[19,256,128]{2,1,0:T(8,128)S(1)} %get-tuple-element.127.refs_1_, f32[7,512,128]{2,1,0:T(8,128)S(1)} %get-tuple-element.128.refs_2_, ...), custom_call_target="tpu_custom_call" | custom-call | flops 10000000 | bytes 10000000 | tf_op jit(solution)/shard_map/pallas_call | solution.py:81
  67.8 1.8 %collective-permute-start.16 = (f32[256,128]{1,0:T(8,128)S(1)}, f32[256,128]{1,0:T(8,128)S(1)}, u32[]{:S(2)}, u32[]{:S(2)}) collective-permute-start(f32[256,128]{1,0:T(8,128)S(1)} %get-tuple-element.203), channel_id=1, source_target_pairs={{0,1},{1,2},{2,3},{3,4},{4,5},{5,6},{6,7},{7,0},{8,9},{9,10},{10,1... | collective-permute-start | bytes 393224 | tf_op jit(solution)/shard_map/ppermute | solution.py:914
  69.7 0.9 collective-permute-start.17
  70.6 2.7 %shard_map.80 = (f32[19,256,128]{2,1,0:T(8,128)S(1)}, f32[19,256,128]{2,1,0:T(8,128)S(1)}, f32[7,512,128]{2,1,0:T(8,128)S(1)}, f32[4,512,128]{2,1,0:T(8,128)S(1)...) custom-call(f32[19,256,128]{2,1,0:T(8,128)S(1)} %get-tuple-element.1, ...), custom_call_target="tpu_custom_call", output_to_operand_aliasing={{0}: (0, {}), {1}: (1, {}), {2}: (2, {}), {3}: (3, {}), {4}... | custom-call | flops 10000000 | bytes 10000000 | tf_op jit(solution)/shard_map/pallas_call | solution.py:81
  73.3 0.4 collective-permute-done.16.refs_10_
  73.9 1.2 shard_map.81
  75.1 1.7 %collective-permute-start.19 = (f32[224,128]{1,0:T(8,128)S(1)}, f32[224,128]{1,0:T(8,128)S(1)}, u32[]{:S(2)}, u32[]{:S(2)}) collective-permute-start(f32[224,128]{1,0:T(8,128)S(1)} %get-tuple-element.149), channel_id=1, source_target_pairs={{0,56},{8,0},{16,8},{24,16},{32,24},{40,32},{48,40},{56,48},{1,57}... | collective-permute-start | bytes 344072 | tf_op jit(solution)/shard_map/ppermute | solution.py:914
  76.8 2.4 %collective-permute-start.18 = (f32[224,128]{1,0:T(8,128)S(1)}, f32[224,128]{1,0:T(8,128)S(1)}, u32[]{:S(2)}, u32[]{:S(2)}) collective-permute-start(f32[224,128]{1,0:T(8,128)S(1)} %get-tuple-element.148), channel_id=1, source_target_pairs={{0,8},{8,16},{16,24},{24,32},{32,40},{40,48},{48,56},{56,0},{1,9},... | collective-permute-start | bytes 344072 | tf_op jit(solution)/shard_map/ppermute | solution.py:914
  79.1 2.1 %shard_map.82 = (f32[224,128]{1,0:T(8,128)S(1)}, f32[224,128]{1,0:T(8,128)S(1)}, f32[19,1152,128]{2,1,0:T(8,128)S(1)}, f32[7,512,128]{2,1,0:T(8,128)S(1)}) custom-call(f32[19,256,128]{2,1,0:T(8,128)S(1)} %get-tuple-element.142.refs_0_, f32[19,256,128]{2,1,0:T(8,128)S(1)} %get-tuple-element.143.refs_1_, f32[7,512,128]{2,1,0:T(8,128)S(1)} %get-tuple-element.144.refs_2_, ...), custom_call_target="tpu_custom_call" | custom-call | flops 10000000 | bytes 10000000 | tf_op jit(solution)/shard_map/pallas_call | solution.py:81
  81.3 0.3 collective-permute-done.19.refs_9_
  82.0 2.6 %collective-permute-start.21 = (f32[256,128]{1,0:T(8,128)S(1)}, f32[256,128]{1,0:T(8,128)S(1)}, u32[]{:S(2)}, u32[]{:S(2)}) collective-permute-start(f32[256,128]{1,0:T(8,128)S(1)} %get-tuple-element.200), channel_id=1, source_target_pairs={{0,7},{1,0},{2,1},{3,2},{4,3},{5,4},{6,5},{7,6},{8,15},{9,8},{10,9... | collective-permute-start | bytes 393224 | tf_op jit(solution)/shard_map/ppermute | solution.py:914
  84.5 2.7 %shard_map.83 = (f32[19,256,128]{2,1,0:T(8,128)S(1)}, f32[19,256,128]{2,1,0:T(8,128)S(1)}, f32[7,512,128]{2,1,0:T(8,128)S(1)}, f32[4,512,128]{2,1,0:T(8,128)S(1)...) custom-call(f32[19,256,128]{2,1,0:T(8,128)S(1)} %get-tuple-element.1, ...), custom_call_target="tpu_custom_call", output_to_operand_aliasing={{0}: (0, {}), {1}: (1, {}), {2}: (2, {}), {3}: (3, {}), {4}... | custom-call | flops 10000000 | bytes 10000000 | tf_op jit(solution)/shard_map/pallas_call | solution.py:81
  87.2 1.0 collective-permute-done.20.refs_10_
  88.3 1.2 shard_map.84
  89.5 0.4 collective-permute-start.23
  89.9 2.6 %collective-permute-start.22 = (f32[224,128]{1,0:T(8,128)S(1)}, f32[224,128]{1,0:T(8,128)S(1)}, u32[]{:S(2)}, u32[]{:S(2)}) collective-permute-start(f32[224,128]{1,0:T(8,128)S(1)} %get-tuple-element.164), channel_id=1, source_target_pairs={{0,8},{8,16},{16,24},{24,32},{32,40},{40,48},{48,56},{56,0},{1,9},... | collective-permute-start | bytes 344072 | tf_op jit(solution)/shard_map/ppermute | solution.py:914
  92.4 2.1 %shard_map.85 = (f32[224,128]{1,0:T(8,128)S(1)}, f32[224,128]{1,0:T(8,128)S(1)}, f32[19,1152,128]{2,1,0:T(8,128)S(1)}, f32[7,512,128]{2,1,0:T(8,128)S(1)}) custom-call(f32[19,256,128]{2,1,0:T(8,128)S(1)} %get-tuple-element.158.refs_0_, f32[19,256,128]{2,1,0:T(8,128)S(1)} %get-tuple-element.159.refs_1_, f32[7,512,128]{2,1,0:T(8,128)S(1)} %get-tuple-element.160.refs_2_, ...), custom_call_target="tpu_custom_call" | custom-call | flops 10000000 | bytes 10000000 | tf_op jit(solution)/shard_map/pallas_call | solution.py:81
  94.6 0.3 collective-permute-done.23.refs_9_.refs_5_
  95.2 3.0 %collective-permute-start.25 = (f32[256,128]{1,0:T(8,128)S(1)}, f32[256,128]{1,0:T(8,128)S(1)}, u32[]{:S(2)}, u32[]{:S(2)}) collective-permute-start(f32[256,128]{1,0:T(8,128)S(1)} %get-tuple-element.198), channel_id=1, source_target_pairs={{0,7},{1,0},{2,1},{3,2},{4,3},{5,4},{6,5},{7,6},{8,15},{9,8},{10,9... | collective-permute-start | bytes 393224 | tf_op jit(solution)/shard_map/ppermute | solution.py:914
  98.2 2.6 %shard_map.86 = (f32[19,1152,128]{2,1,0:T(8,128)S(1)}, f32[7,512,128]{2,1,0:T(8,128)S(1)}, f32[1792,128]{1,0:T(8,128)S(1)}) custom-call(f32[19,256,128]{2,1,0:T(8,128)S(1)} %get-tuple-element.158.refs_0_, f32[19,256,128]{2,1,0:T(8,128)S(1)} %get-tuple-element.159.refs_1_, ...), custom_call_target="tpu_custom_call", output_to_operand_aliasing={{0}: (4, {}), {1}: (5, {})} | custom-call | flops 10000000 | bytes 10000000 | tf_op jit(solution)/shard_map/pallas_call | solution.py:81
  100.8 0.5 collective-permute-done.24.refs_6_.refs_10_
  101.3 1.0 shard_map.87
  102.3 0.8 collective-permute-start.26
  103.1 2.4 %collective-permute-start.27 = (f32[336,128]{1,0:T(8,128)S(1)}, f32[336,128]{1,0:T(8,128)S(1)}, u32[]{:S(2)}, u32[]{:S(2)}) collective-permute-start(f32[336,128]{1,0:T(8,128)S(1)} %get-tuple-element.175), channel_id=1, source_target_pairs={{0,7},{1,0},{2,1},{3,2},{4,3},{5,4},{6,5},{7,6},{8,15},{9,8},{10,9... | collective-permute-start | bytes 516104 | tf_op jit(solution)/shard_map/ppermute | solution.py:919
  105.5 4.3 %collective-permute-done.26.refs_1_ = f32[336,128]{1,0:T(8,128)S(1)} collective-permute-done((f32[336,128]{1,0:T(8,128)S(1)}, f32[336,128]{1,0:T(8,128)S(1)}, u32[]{:S(2)}, u32[]{:S(2)}) %collective-permute-start.26) | collective-permute-done | bytes 172064 | tf_op jit(solution)/shard_map/ppermute | solution.py:919
  109.9 0.3 collective-permute-start.30
  110.2 4.4 %collective-permute-start.31 = (f32[336,128]{1,0:T(8,128)S(1)}, f32[336,128]{1,0:T(8,128)S(1)}, u32[]{:S(2)}, u32[]{:S(2)}) collective-permute-start(f32[336,128]{1,0:T(8,128)S(1)} %pad_maximum_fusion.3), channel_id=1, source_target_pairs={{0,5},{1,6},{2,7},{3,0},{4,1},{5,2},{6,3},{7,4},{8,13},{9,14},{10,... | collective-permute-start | bytes 516104 | tf_op jit(solution)/shard_map/ppermute | solution.py:919
  114.5 3.6 %collective-permute-start.29 = (f32[224,128]{1,0:T(8,128)S(1)}, f32[224,128]{1,0:T(8,128)S(1)}, u32[]{:S(2)}, u32[]{:S(2)}) collective-permute-start(f32[224,128]{1,0:T(8,128)S(1)} %get-tuple-element.177), channel_id=1, source_target_pairs={{0,6},{1,7},{2,0},{3,1},{4,2},{5,3},{6,4},{7,5},{8,14},{9,15},{10,... | collective-permute-start | bytes 344072 | tf_op jit(solution)/shard_map/ppermute | solution.py:919
  118.1 3.1 %shard_map.88 = (f32[19,256,128]{2,1,0:T(8,128)}, f32[19,1152,128]{2,1,0:T(8,128)S(1)}) custom-call(f32[19,256,128]{2,1,0:T(8,128)S(1)} %get-tuple-element.158.refs_0_, f32[19,256,128]{2,1,0:T(8,128)S(1)} %get-tuple-element.159.refs_1_, f32[7,512,128]{2,1,0:T(8,128)S(1)} %get-tuple-element.160.refs_2_, ...), custom_call_target="tpu_custom_call", output_to_operand_aliasing={{1}: (4, {})} | custom-call | flops 10000000 | bytes 10000000 | tf_op jit(solution)/shard_map/pallas_call | solution.py:81
  121.2 5.4 %collective-permute-done.28.refs_3_ = f32[224,128]{1,0:T(8,128)S(1)} collective-permute-done((f32[224,128]{1,0:T(8,128)S(1)}, f32[224,128]{1,0:T(8,128)S(1)}, u32[]{:S(2)}, u32[]{:S(2)}) %collective-permute-start.28) | collective-permute-done | bytes 114720 | tf_op jit(solution)/shard_map/ppermute | solution.py:919
  126.5 4.1 %collective-permute-done.29.refs_4_ = f32[224,128]{1,0:T(8,128)S(1)} collective-permute-done((f32[224,128]{1,0:T(8,128)S(1)}, f32[224,128]{1,0:T(8,128)S(1)}, u32[]{:S(2)}, u32[]{:S(2)}) %collective-permute-start.29) | collective-permute-done | bytes 114720 | tf_op jit(solution)/shard_map/ppermute | solution.py:919
  130.7 1.8 %shard_map.89 = f32[1792,128]{1,0:T(8,128)} custom-call(s32[1]{0:T(128)} %bitcast.8.me_ref, s32[8]{0:T(128)S(1)} %copy-done.5, f32[224,128]{1,0:T(8,128)S(1)} %get-tuple-element.173.refs_0_, f32[336,128]{1,0:T(8,128)S(1)} %collective-permute-done.26.refs_1_, f32[336,128]{1,0:T(8,128)S(1)} %collective-permute-done.27.refs_2_, ...), custom_call_target="tpu_custom_call" | custom-call | flops 1 | bytes 2000000 | tf_op jit(solution)/shard_map/pallas_call | solution.py:81
  (74 shorter events, 1.9 us)
Async XLA Ops:
  0.6 27.0 %copy-start.2 = (s32[16,16,128]{2,1,0:T(8,128)S(1)}, s32[16,16,128]{2,1,0:T(8,128)}, u32[]{:S(2)}) copy-start(s32[16,16,128]{2,1,0:T(8,128)} %param.7) | copy-start | bytes 393220
  0.6 0.7 copy-start.4
  3.3 13.9 %collective-permute-start.2 = (f32[336,128]{1,0:T(8,128)S(1)}, f32[336,128]{1,0:T(8,128)S(1)}, u32[]{:S(2)}, u32[]{:S(2)}) collective-permute-start(f32[336,128]{1,0:T(8,128)S(1)} %get-tuple-element.96), channel_id=1, source_target_pairs={{0,1},{1,2},{2,3},{3,4},{4,5},{5,6},{6,7},{7,0},{8,9},{9,10},{10,1... | collective-permute-start | bytes 516104 | tf_op jit(solution)/shard_map/ppermute | solution.py:919
  5.0 13.8 %collective-permute-start.3 = (f32[336,128]{1,0:T(8,128)S(1)}, f32[336,128]{1,0:T(8,128)S(1)}, u32[]{:S(2)}, u32[]{:S(2)}) collective-permute-start(f32[336,128]{1,0:T(8,128)S(1)} %get-tuple-element.97), channel_id=1, source_target_pairs={{0,7},{1,0},{2,1},{3,2},{4,3},{5,4},{6,5},{7,6},{8,15},{9,8},{10,9... | collective-permute-start | bytes 516104 | tf_op jit(solution)/shard_map/ppermute | solution.py:919
  9.1 1.7 %copy-start = (f32[19,16,16,128]{3,2,1,0:T(8,128)S(1)}, f32[19,16,16,128]{3,2,1,0:T(8,128)}, u32[]{:S(2)}) copy-start(f32[19,16,16,128]{3,2,1,0:T(8,128)} %param.5) | copy-start | bytes 7471108
  10.8 0.9 copy-start.1
  14.4 20.3 %copy-start.3 = (s32[1,1,8]{2,1,0:T(1,128)S(1)}, s32[1,1,8]{2,1,0:T(1,128)}, u32[]{:S(2)}) copy-start(s32[1,1,8]{2,1,0:T(1,128)} %slot_ref.8) | copy-start | bytes 100
  14.4 7.5 %collective-permute-start = (f32[320,128]{1,0:T(8,128)S(1)}, f32[320,128]{1,0:T(8,128)S(1)}, u32[]{:S(2)}, u32[]{:S(2)}) collective-permute-start(f32[320,128]{1,0:T(8,128)S(1)} %get-tuple-element.91), channel_id=1, source_target_pairs={{0,192},{64,0},{128,64},{192,128},{1,193},{65,1},{129,65},{193,129... | collective-permute-start | bytes 491528 | tf_op jit(solution)/shard_map/ppermute | solution.py:914
  17.3 17.5 %collective-permute-start.6 = (f32[336,128]{1,0:T(8,128)S(1)}, f32[336,128]{1,0:T(8,128)S(1)}, u32[]{:S(2)}, u32[]{:S(2)}) collective-permute-start(f32[336,128]{1,0:T(8,128)S(1)} %pad_maximum_fusion), channel_id=1, source_target_pairs={{0,3},{1,4},{2,5},{3,6},{4,7},{5,0},{6,1},{7,2},{8,11},{9,12},{10,... | collective-permute-start | bytes 516104 | tf_op jit(solution)/shard_map/ppermute | solution.py:919
  18.9 15.8 %collective-permute-start.7 = (f32[336,128]{1,0:T(8,128)S(1)}, f32[336,128]{1,0:T(8,128)S(1)}, u32[]{:S(2)}, u32[]{:S(2)}) collective-permute-start(f32[336,128]{1,0:T(8,128)S(1)} %pad_maximum_fusion.1), channel_id=1, source_target_pairs={{0,5},{1,6},{2,7},{3,0},{4,1},{5,2},{6,3},{7,4},{8,13},{9,14},{10,... | collective-permute-start | bytes 516104 | tf_op jit(solution)/shard_map/ppermute | solution.py:919
  21.9 5.7 %collective-permute-start.1 = (f32[320,128]{1,0:T(8,128)S(1)}, f32[320,128]{1,0:T(8,128)S(1)}, u32[]{:S(2)}, u32[]{:S(2)}) collective-permute-start(f32[320,128]{1,0:T(8,128)S(1)} %get-tuple-element.92), channel_id=1, source_target_pairs={{0,64},{64,128},{128,192},{192,0},{1,65},{65,129},{129,193},{193,1... | collective-permute-start | bytes 491528 | tf_op jit(solution)/shard_map/ppermute | solution.py:914
  21.9 10.8 %collective-permute-start.4 = (f32[224,128]{1,0:T(8,128)S(1)}, f32[224,128]{1,0:T(8,128)S(1)}, u32[]{:S(2)}, u32[]{:S(2)}) collective-permute-start(f32[224,128]{1,0:T(8,128)S(1)} %get-tuple-element.98), channel_id=1, source_target_pairs={{0,2},{1,3},{2,4},{3,5},{4,6},{5,7},{6,0},{7,1},{8,10},{9,11},{10,... | collective-permute-start | bytes 344072 | tf_op jit(solution)/shard_map/ppermute | solution.py:919
  21.9 12.8 %collective-permute-start.5 = (f32[224,128]{1,0:T(8,128)S(1)}, f32[224,128]{1,0:T(8,128)S(1)}, u32[]{:S(2)}, u32[]{:S(2)}) collective-permute-start(f32[224,128]{1,0:T(8,128)S(1)} %get-tuple-element.99), channel_id=1, source_target_pairs={{0,6},{1,7},{2,0},{3,1},{4,2},{5,3},{6,4},{7,5},{8,14},{9,15},{10,... | collective-permute-start | bytes 344072 | tf_op jit(solution)/shard_map/ppermute | solution.py:919
  35.5 3.8 %collective-permute-start.8 = (f32[224,128]{1,0:T(8,128)S(1)}, f32[224,128]{1,0:T(8,128)S(1)}, u32[]{:S(2)}, u32[]{:S(2)}) collective-permute-start(f32[224,128]{1,0:T(8,128)S(1)} %get-tuple-element.103), channel_id=1, source_target_pairs={{0,192},{64,0},{128,64},{192,128},{1,193},{65,1},{129,65},{193,129... | collective-permute-start | bytes 344072 | tf_op jit(solution)/shard_map/ppermute | solution.py:914
  35.6 4.9 %collective-permute-start.9 = (f32[224,128]{1,0:T(8,128)S(1)}, f32[224,128]{1,0:T(8,128)S(1)}, u32[]{:S(2)}, u32[]{:S(2)}) collective-permute-start(f32[224,128]{1,0:T(8,128)S(1)} %get-tuple-element.104), channel_id=1, source_target_pairs={{0,64},{64,128},{128,192},{192,0},{1,65},{65,129},{129,193},{193,1... | collective-permute-start | bytes 344072 | tf_op jit(solution)/shard_map/ppermute | solution.py:914
  42.5 7.1 %collective-permute-start.11 = (f32[240,128]{1,0:T(8,128)S(1)}, f32[240,128]{1,0:T(8,128)S(1)}, u32[]{:S(2)}, u32[]{:S(2)}) collective-permute-start(f32[240,128]{1,0:T(8,128)S(1)} %get-tuple-element.111), channel_id=1, source_target_pairs={{0,56},{8,0},{16,8},{24,16},{32,24},{40,32},{48,40},{56,48},{1,57}... | collective-permute-start | bytes 368648 | tf_op jit(solution)/shard_map/ppermute | solution.py:914
  47.0 2.6 %collective-permute-start.10 = (f32[240,128]{1,0:T(8,128)S(1)}, f32[240,128]{1,0:T(8,128)S(1)}, u32[]{:S(2)}, u32[]{:S(2)}) collective-permute-start(f32[240,128]{1,0:T(8,128)S(1)} %get-tuple-element.110), channel_id=1, source_target_pairs={{0,8},{8,16},{16,24},{24,32},{32,40},{40,48},{48,56},{56,0},{1,9},... | collective-permute-start | bytes 368648 | tf_op jit(solution)/shard_map/ppermute | solution.py:914
  49.8 8.3 %collective-permute-start.12 = (f32[272,128]{1,0:T(8,128)S(1)}, f32[272,128]{1,0:T(8,128)S(1)}, u32[]{:S(2)}, u32[]{:S(2)}) collective-permute-start(f32[272,128]{1,0:T(8,128)S(1)} %get-tuple-element.197), channel_id=1, source_target_pairs={{0,1},{1,2},{2,3},{3,4},{4,5},{5,6},{6,7},{7,0},{8,9},{9,10},{10,1... | collective-permute-start | bytes 417800 | tf_op jit(solution)/shard_map/ppermute | solution.py:914
  54.2 4.7 %collective-permute-start.13 = (f32[272,128]{1,0:T(8,128)S(1)}, f32[272,128]{1,0:T(8,128)S(1)}, u32[]{:S(2)}, u32[]{:S(2)}) collective-permute-start(f32[272,128]{1,0:T(8,128)S(1)} %get-tuple-element.196), channel_id=1, source_target_pairs={{0,7},{1,0},{2,1},{3,2},{4,3},{5,4},{6,5},{7,6},{8,15},{9,8},{10,9... | collective-permute-start | bytes 417800 | tf_op jit(solution)/shard_map/ppermute | solution.py:914
  61.0 6.7 %collective-permute-start.15 = (f32[224,128]{1,0:T(8,128)S(1)}, f32[224,128]{1,0:T(8,128)S(1)}, u32[]{:S(2)}, u32[]{:S(2)}) collective-permute-start(f32[224,128]{1,0:T(8,128)S(1)} %get-tuple-element.133), channel_id=1, source_target_pairs={{0,56},{8,0},{16,8},{24,16},{32,24},{40,32},{48,40},{56,48},{1,57}... | collective-permute-start | bytes 344072 | tf_op jit(solution)/shard_map/ppermute | solution.py:914
  63.9 3.7 %collective-permute-start.14 = (f32[224,128]{1,0:T(8,128)S(1)}, f32[224,128]{1,0:T(8,128)S(1)}, u32[]{:S(2)}, u32[]{:S(2)}) collective-permute-start(f32[224,128]{1,0:T(8,128)S(1)} %get-tuple-element.132), channel_id=1, source_target_pairs={{0,8},{8,16},{16,24},{24,32},{32,40},{40,48},{48,56},{56,0},{1,9},... | collective-permute-start | bytes 344072 | tf_op jit(solution)/shard_map/ppermute | solution.py:914
  67.8 5.8 %collective-permute-start.16 = (f32[256,128]{1,0:T(8,128)S(1)}, f32[256,128]{1,0:T(8,128)S(1)}, u32[]{:S(2)}, u32[]{:S(2)}) collective-permute-start(f32[256,128]{1,0:T(8,128)S(1)} %get-tuple-element.203), channel_id=1, source_target_pairs={{0,1},{1,2},{2,3},{3,4},{4,5},{5,6},{6,7},{7,0},{8,9},{9,10},{10,1... | collective-permute-start | bytes 393224 | tf_op jit(solution)/shard_map/ppermute | solution.py:914
  69.7 4.2 %collective-permute-start.17 = (f32[256,128]{1,0:T(8,128)S(1)}, f32[256,128]{1,0:T(8,128)S(1)}, u32[]{:S(2)}, u32[]{:S(2)}) collective-permute-start(f32[256,128]{1,0:T(8,128)S(1)} %get-tuple-element.202), channel_id=1, source_target_pairs={{0,7},{1,0},{2,1},{3,2},{4,3},{5,4},{6,5},{7,6},{8,15},{9,8},{10,9... | collective-permute-start | bytes 393224 | tf_op jit(solution)/shard_map/ppermute | solution.py:914
  75.1 6.5 %collective-permute-start.19 = (f32[224,128]{1,0:T(8,128)S(1)}, f32[224,128]{1,0:T(8,128)S(1)}, u32[]{:S(2)}, u32[]{:S(2)}) collective-permute-start(f32[224,128]{1,0:T(8,128)S(1)} %get-tuple-element.149), channel_id=1, source_target_pairs={{0,56},{8,0},{16,8},{24,16},{32,24},{40,32},{48,40},{56,48},{1,57}... | collective-permute-start | bytes 344072 | tf_op jit(solution)/shard_map/ppermute | solution.py:914
  76.8 4.8 %collective-permute-start.18 = (f32[224,128]{1,0:T(8,128)S(1)}, f32[224,128]{1,0:T(8,128)S(1)}, u32[]{:S(2)}, u32[]{:S(2)}) collective-permute-start(f32[224,128]{1,0:T(8,128)S(1)} %get-tuple-element.148), channel_id=1, source_target_pairs={{0,8},{8,16},{16,24},{24,32},{32,40},{40,48},{48,56},{56,0},{1,9},... | collective-permute-start | bytes 344072 | tf_op jit(solution)/shard_map/ppermute | solution.py:914
  81.8 6.5 %collective-permute-start.20 = (f32[256,128]{1,0:T(8,128)S(1)}, f32[256,128]{1,0:T(8,128)S(1)}, u32[]{:S(2)}, u32[]{:S(2)}) collective-permute-start(f32[256,128]{1,0:T(8,128)S(1)} %get-tuple-element.201), channel_id=1, source_target_pairs={{0,1},{1,2},{2,3},{3,4},{4,5},{5,6},{6,7},{7,0},{8,9},{9,10},{10,1... | collective-permute-start | bytes 393224 | tf_op jit(solution)/shard_map/ppermute | solution.py:914
  82.0 6.3 %collective-permute-start.21 = (f32[256,128]{1,0:T(8,128)S(1)}, f32[256,128]{1,0:T(8,128)S(1)}, u32[]{:S(2)}, u32[]{:S(2)}) collective-permute-start(f32[256,128]{1,0:T(8,128)S(1)} %get-tuple-element.200), channel_id=1, source_target_pairs={{0,7},{1,0},{2,1},{3,2},{4,3},{5,4},{6,5},{7,6},{8,15},{9,8},{10,9... | collective-permute-start | bytes 393224 | tf_op jit(solution)/shard_map/ppermute | solution.py:914
  89.5 5.4 %collective-permute-start.23 = (f32[224,128]{1,0:T(8,128)S(1)}, f32[224,128]{1,0:T(8,128)S(1)}, u32[]{:S(2)}, u32[]{:S(2)}) collective-permute-start(f32[224,128]{1,0:T(8,128)S(1)} %get-tuple-element.165), channel_id=1, source_target_pairs={{0,56},{8,0},{16,8},{24,16},{32,24},{40,32},{48,40},{56,48},{1,57}... | collective-permute-start | bytes 344072 | tf_op jit(solution)/shard_map/ppermute | solution.py:914
  89.9 5.1 %collective-permute-start.22 = (f32[224,128]{1,0:T(8,128)S(1)}, f32[224,128]{1,0:T(8,128)S(1)}, u32[]{:S(2)}, u32[]{:S(2)}) collective-permute-start(f32[224,128]{1,0:T(8,128)S(1)} %get-tuple-element.164), channel_id=1, source_target_pairs={{0,8},{8,16},{16,24},{24,32},{32,40},{40,48},{48,56},{56,0},{1,9},... | collective-permute-start | bytes 344072 | tf_op jit(solution)/shard_map/ppermute | solution.py:914
  95.1 6.2 %collective-permute-start.24 = (f32[256,128]{1,0:T(8,128)S(1)}, f32[256,128]{1,0:T(8,128)S(1)}, u32[]{:S(2)}, u32[]{:S(2)}) collective-permute-start(f32[256,128]{1,0:T(8,128)S(1)} %get-tuple-element.199), channel_id=1, source_target_pairs={{0,1},{1,2},{2,3},{3,4},{4,5},{5,6},{6,7},{7,0},{8,9},{9,10},{10,1... | collective-permute-start | bytes 393224 | tf_op jit(solution)/shard_map/ppermute | solution.py:914
  95.2 6.1 %collective-permute-start.25 = (f32[256,128]{1,0:T(8,128)S(1)}, f32[256,128]{1,0:T(8,128)S(1)}, u32[]{:S(2)}, u32[]{:S(2)}) collective-permute-start(f32[256,128]{1,0:T(8,128)S(1)} %get-tuple-element.198), channel_id=1, source_target_pairs={{0,7},{1,0},{2,1},{3,2},{4,3},{5,4},{6,5},{7,6},{8,15},{9,8},{10,9... | collective-permute-start | bytes 393224 | tf_op jit(solution)/shard_map/ppermute | solution.py:914
  102.3 7.6 %collective-permute-start.26 = (f32[336,128]{1,0:T(8,128)S(1)}, f32[336,128]{1,0:T(8,128)S(1)}, u32[]{:S(2)}, u32[]{:S(2)}) collective-permute-start(f32[336,128]{1,0:T(8,128)S(1)} %get-tuple-element.174), channel_id=1, source_target_pairs={{0,1},{1,2},{2,3},{3,4},{4,5},{5,6},{6,7},{7,0},{8,9},{9,10},{10,1... | collective-permute-start | bytes 516104 | tf_op jit(solution)/shard_map/ppermute | solution.py:919
  103.1 7.1 %collective-permute-start.27 = (f32[336,128]{1,0:T(8,128)S(1)}, f32[336,128]{1,0:T(8,128)S(1)}, u32[]{:S(2)}, u32[]{:S(2)}) collective-permute-start(f32[336,128]{1,0:T(8,128)S(1)} %get-tuple-element.175), channel_id=1, source_target_pairs={{0,7},{1,0},{2,1},{3,2},{4,3},{5,4},{6,5},{7,6},{8,15},{9,8},{10,9... | collective-permute-start | bytes 516104 | tf_op jit(solution)/shard_map/ppermute | solution.py:919
  109.9 20.8 %collective-permute-start.30 = (f32[336,128]{1,0:T(8,128)S(1)}, f32[336,128]{1,0:T(8,128)S(1)}, u32[]{:S(2)}, u32[]{:S(2)}) collective-permute-start(f32[336,128]{1,0:T(8,128)S(1)} %pad_maximum_fusion.2), channel_id=1, source_target_pairs={{0,3},{1,4},{2,5},{3,6},{4,7},{5,0},{6,1},{7,2},{8,11},{9,12},{10,... | collective-permute-start | bytes 516104 | tf_op jit(solution)/shard_map/ppermute | solution.py:919
  110.2 20.5 %collective-permute-start.31 = (f32[336,128]{1,0:T(8,128)S(1)}, f32[336,128]{1,0:T(8,128)S(1)}, u32[]{:S(2)}, u32[]{:S(2)}) collective-permute-start(f32[336,128]{1,0:T(8,128)S(1)} %pad_maximum_fusion.3), channel_id=1, source_target_pairs={{0,5},{1,6},{2,7},{3,0},{4,1},{5,2},{6,3},{7,4},{8,13},{9,14},{10,... | collective-permute-start | bytes 516104 | tf_op jit(solution)/shard_map/ppermute | solution.py:919
  114.5 12.0 %collective-permute-start.28 = (f32[224,128]{1,0:T(8,128)S(1)}, f32[224,128]{1,0:T(8,128)S(1)}, u32[]{:S(2)}, u32[]{:S(2)}) collective-permute-start(f32[224,128]{1,0:T(8,128)S(1)} %get-tuple-element.176), channel_id=1, source_target_pairs={{0,2},{1,3},{2,4},{3,5},{4,6},{5,7},{6,0},{7,1},{8,10},{9,11},{10,... | collective-permute-start | bytes 344072 | tf_op jit(solution)/shard_map/ppermute | solution.py:919
  114.5 16.1 %collective-permute-start.29 = (f32[224,128]{1,0:T(8,128)S(1)}, f32[224,128]{1,0:T(8,128)S(1)}, u32[]{:S(2)}, u32[]{:S(2)}) collective-permute-start(f32[224,128]{1,0:T(8,128)S(1)} %get-tuple-element.177), channel_id=1, source_target_pairs={{0,6},{1,7},{2,0},{3,1},{4,2},{5,3},{6,4},{7,5},{8,14},{9,15},{10,... | collective-permute-start | bytes 344072 | tf_op jit(solution)/shard_map/ppermute | solution.py:919
  118.1 12.6 %copy-start.5 = (s32[8]{0:T(128)S(1)}, s32[8]{0:T(128)}, u32[]{:S(2)}) copy-start(s32[8]{0:T(128)} %slot_ref.9) | copy-start | bytes 100

commit v4 on v3

--- a/solution.py
+++ b/solution.py
@@ -39,7 +39,7 @@
 Y_DN = [i for i in range(19) if DIRS[i][1] == -1]
 Z_UP = [i for i in range(19) if DIRS[i][2] == 1]
 Z_DN = [i for i in range(19) if DIRS[i][2] == -1]
-RHO, VEL, PART, NORM, TRANS, MASK = 5, 6, 9, 10, 11, 12
+RHO, NORM, TRANS, MASK = 5, 9, 10, 11
 SIDES = 2
 UNROLL = 2
 B = 16
@@ -226,18 +226,26 @@
 
 
 def pick_kernel(me_ref, slot_ref, *refs):
-    for tile, out_ref in ((0, refs[-2]), (7, refs[-1])):
+    low_ref, high_ref, hold_ref = refs[-3:]
+    outer = (lanes(HALF) & 8) == 0
+    for tile in (0, 7):
         slot = slot_ref[0, 0, tile]
 
         @pl.when(slot < 0)
         def _():
-            out_ref[...] = jnp.zeros((ROW, L), F32)
+            hold_ref[...] = jnp.zeros((ROW, L), F32)
 
         for off, k, at, count, first in PARTS:
 
             @pl.when((slot >= 0) & (slot // 8 == ((me_ref[0] + off) & 7)))
             def _():
-                out_ref[pl.ds(first, count), :] = refs[k][pl.ds(at, count), :]
+                hold_ref[pl.ds(first, count), :] = refs[k][pl.ds(at, count), :]
+
+        one, two = hold_ref[pl.ds(0, HALF), :], hold_ref[pl.ds(HALF, HALF), :]
+        if tile == 0:
+            low_ref[...] = jnp.where(outer, one, pltpu.roll(two, W, axis=1))
+        else:
+            high_ref[...] = jnp.where(outer, pltpu.roll(two, L - W, axis=1), one)
 
 
 def spread_kernel(me_ref, slot_ref, *refs):
@@ -267,24 +275,35 @@
     high_ref[pl.ds(at, 8), :] = high
 
 
-def columns_kernel(pops_ref, mask_ref, low_ref, high_ref):
+def columns_kernel(pops_in, mask_in, low_ref, high_ref, pops_ref, mask_ref, sems):
+    load = pltpu.make_async_copy(mask_in, mask_ref, sems.at[19])
+    load.start()
+
+    def part(comp):
+        return pltpu.make_async_copy(pops_in.at[comp], pops_ref.at[comp], sems.at[comp])
+
+    for comp in range(19):
+        part(comp).start()
+
     def rows(start, i):
         return pl.ds(pl.multiple_of(start + i * 8, 8), 8)
 
-    def body(group, carry):
-        at = (group % 2) * 128
+    for comp in range(19):
+        part(comp).wait()
+        for half in range(2):
+            pack_columns(
+                lambda i: pops_ref[comp, rows(half * 128, i), :],
+                low_ref,
+                high_ref,
+                (2 * comp + half) * 8,
+            )
+    load.wait()
+    for half in range(2):
         pack_columns(
-            lambda i: pops_ref[group // 2, rows(at, i), :], low_ref, high_ref, group * 8
-        )
-        return carry
-
-    lax.fori_loop(0, 38, body, 0, unroll=UNROLL)
-    for group in range(2):
-        pack_columns(
-            lambda i: mask_ref[rows(group * 128, i), :].astype(F32),
+            lambda i: mask_ref[rows(half * 128, i), :].astype(F32),
             low_ref,
             high_ref,
-            (38 + group) * 8,
+            (38 + half) * 8,
         )
 
 
@@ -554,7 +573,8 @@
         part = partial_sum(f, face_rows(post_ref, inner, normal), opened, normal, (5, 6))
         fields = [flow_rows(pops_refs, edge, c) for c in names]
         fields += [face_rows(aux_ref, edge, k) for k in range(4)]
-        fields += [part, f[normal], jnp.where(row == 0, f[6], f[5])]
+        fields[-1] = fields[-1] + FORCE_GAIN * (part - REST_CONC)
+        fields += [f[normal], jnp.where(row == 0, f[6], f[5])]
         if ring_ref is not None:
             fields.append(face_rows(ring_ref, edge))
         write_message(y_refs[side], fields)
@@ -574,7 +594,8 @@
         part = partial_sum(f, plane(post_ref, inner, normal), opened, normal, (3, 4))
         fields = [flow_plane(pops_refs, edge, c) for c in names]
         fields += [plane(aux_ref, edge, k) for k in range(4)]
-        fields += [part, f[normal], jnp.where(row == 0, f[4], f[3])]
+        fields[-1] = fields[-1] + FORCE_GAIN * (part - REST_CONC)
+        fields += [f[normal], jnp.where(row == 0, f[4], f[3])]
         if ring_ref is not None:
             fields.append(plane(ring_ref, edge))
         write_message(z_refs[side], fields)
@@ -587,7 +608,7 @@
 
 
 def lifted(conc, vx, vy, vz):
-    vz = vz + FORCE_GAIN * (conc - REST_CONC)
+    vz = vz + FORCE_GAIN * conc
     return vz, 1.0 - 1.5 * (vx * vx + vy * vy + vz * vz)
 
 
@@ -617,8 +638,7 @@
     for side in range(2):
         msg = y_refs[side]
         own = face_rows(post_ref, (0, B - 1)[side], (4, 3)[side])
-        conc = read_field(msg, PART)
-        conc = conc + jnp.where(get_open(open_ref, 0, side), own, read_field(msg, NORM))
+        conc = jnp.where(get_open(open_ref, 0, side), own, read_field(msg, NORM))
         if z_refs is not None:
             ends = jnp.where(
                 row == 0,
@@ -650,8 +670,7 @@
             row == 0, spread8(read_diag(msg, 0, NORM)), spread8(read_diag(msg, 1, NORM))
         )
         ends = jnp.where(get_open(open_ref, 3, side), ends, read_field(msg, TRANS))
-        conc = read_field(msg, PART)
-        conc = conc + jnp.where(get_open(open_ref, 2, side), own, read_field(msg, NORM))
+        conc = jnp.where(get_open(open_ref, 2, side), own, read_field(msg, NORM))
         conc = conc + jnp.where((row == 0) | (row == B - 1), ends, 0.0)
         zz = (0, B + 1)[side]
         collide_face(
@@ -670,8 +689,7 @@
             for tile in range(2):
                 open_y = open_ref[pl.ds(open_at(1, y_side, tile) + z_row, 1), :]
                 open_z = open_ref[pl.ds(open_at(3, z_side, tile) + y_row, 1), :]
-                conc = get[PART][tile]
-                conc = conc + jnp.where(open_y > 0, from_y[tile], get[TRANS][tile])
+                conc = jnp.where(open_y > 0, from_y[tile], get[TRANS][tile])
                 conc = conc + jnp.where(open_z > 0, from_z[tile], get[NORM][tile])
                 rho, vx, vy, vz = (get[k][tile] for k in range(RHO, RHO + 4))
                 vz, base = lifted(conc, vx, vy, vz)
@@ -716,8 +734,11 @@
     dense_ref, right_ref, left_ref, pops_ref, side_ref, aux_ref, ring_ref,
     post_ref, ydn_ref, yup_ref, turn_ref,
 ):
-    turn_ref[pl.ds(0, BLOCKROWS // 8, stride=8), :] = right_ref[...]
-    turn_ref[pl.ds(7, BLOCKROWS // 8, stride=8), :] = left_ref[...]
+    right, left = right_ref[...], left_ref[...]
+    turn_ref[pl.ds(0, HALF, stride=8), :] = right
+    turn_ref[pl.ds(HALF * 8, HALF, stride=8), :] = pltpu.roll(right, L - W, axis=1)
+    turn_ref[pl.ds(7, HALF, stride=8), :] = left
+    turn_ref[pl.ds(HALF * 8 + 7, HALF, stride=8), :] = pltpu.roll(left, W, axis=1)
     lane = lanes(8)
     near = (lane < W) | (lane >= L - W)
 
@@ -957,9 +978,18 @@
 
     pops = populations.reshape(19, 256, L)
     mask = pore_mask.reshape(256, L)
-    low, high = call(columns_kernel, (held(320, L),) * 2, [VMEM] * 2, [], 10**6, 13 * 10**6)(
-        pops, mask
-    )
+    low, high = call(
+        columns_kernel,
+        (held(320, L),) * 2,
+        [HBM] * 2,
+        [
+            pltpu.VMEM((19, 256, L), F32),
+            pltpu.VMEM((256, L), jnp.int32),
+            pltpu.SemaphoreType.DMA((20,)),
+        ],
+        10**6,
+        13 * 10**6,
+    )(pops, mask)
     left, right = neighbours(low, high, "gx")
     dims = ((19, 256, L), (19, 256, L), (ROWS, L), (4, ROWS, L), (PADROWS, L))
     pops, side, ring_mask, aux, mask, bits = call(
@@ -972,7 +1002,13 @@
     )(flags, pops, mask, right, left)
 
     low, high = call(
-        pick_kernel, (held(ROW, L),) * 2, [SMEM] * 2 + [VMEM] * 8, [], 1, 10**6, keep=True
+        pick_kernel,
+        (held(HALF, L),) * 2,
+        [SMEM] * 2 + [VMEM] * 8,
+        [pltpu.VMEM((ROW, L), F32)],
+        1,
+        10**6,
+        keep=True,
     )(me, block_slot, *recv, bits)
     left, right = neighbours(low, high, "gx")
     dense = call(

time: 133 us -> 130 us (0.977)
  local copies, waits for them, and re-layouts: 3.72 us -> 1.11 us
  Pallas kernels: 44.7 us -> 46.1 us
    unnamed x24 -> x20, local copies, waits for them, and re-layouts: 3.34 us -> 0.73 us
    pallas_call x22, Pallas kernels: 44.7 us -> 46.1 us  [placed(): return run(*map(place, args, in_specs))]
  transfers between devices with their start and end apart: 32 -> 32, of which waited for: 16 -> 16; matrix products, arithmetic and copies ran while one was open for 0% -> 0% of each run, Pallas kernels for 25% -> 26%
where the time goes in v4:
time: 130 us
  starting transfers between devices  58.3 us (45%)
  Pallas kernels  46.1 us (35%)
  waiting for transfers between devices  22.9 us (18%)
    pallas_call x22, Pallas kernels, placed(): return run(*map(place, args, in_specs))  46.1 us
    ppermute x20, starting transfers between devices, neighbours(): return (lax.ppermute(high, axis, up), lax.ppermute(low, axis, down))  33 us
    ppermute x12, starting transfers between devices, shifted(): return lax.ppermute(x, 'gz', [(i, (i + step) % 8) for i in range(8)])  25.4 us
    ppermute x12, waiting for transfers between devices, shifted(): return lax.ppermute(x, 'gz', [(i, (i + step) % 8) for i in range(8)])  16.4 us
    ppermute x20, waiting for transfers between devices, neighbours(): return (lax.ppermute(high, axis, up), lax.ppermute(low, axis, down))  6.5 us
  transfers between devices with their start and end apart: 32, of which 16 were waited for; matrix products, arithmetic and copies ran while one was open for 0% of the time, Pallas kernels for 26%

profile of v4, /device:TPU:7, one launch (start us, length us, event | category | flops | bytes accessed | tf_op | source)
XLA Modules:
  0.0 130.0 jit_solution(12345497353486690953)
XLA Ops:
  0.7 0.7 copy-done.2
  1.3 2.0 %shard_map.70 = (f32[224,128]{1,0:T(8,128)S(1)}, f32[336,128]{1,0:T(8,128)S(1)}, f32[336,128]{1,0:T(8,128)S(1)}, f32[224,128]{1,0:T(8,128)S(1)}, f32[224,128]{1,...) custom-call(s32[1]{0:T(128)} %bitcast.8.me_ref, s32[8]{0:T(128)S(1)} %copy-done.2, f32[1792,128]{1,0:T(8,128)} %bitcast.85), custom_call_target="tpu_custom_call" | custom-call | flops 1 | bytes 2000000 | tf_op jit(solution)/shard_map/pallas_call | solution.py:81
  3.3 1.7 %collective-permute-start.2 = (f32[336,128]{1,0:T(8,128)S(1)}, f32[336,128]{1,0:T(8,128)S(1)}, u32[]{:S(2)}, u32[]{:S(2)}) collective-permute-start(f32[336,128]{1,0:T(8,128)S(1)} %get-tuple-element.96), channel_id=1, source_target_pairs={{0,1},{1,2},{2,3},{3,4},{4,5},{5,6},{6,7},{7,0},{8,9},{9,10},{10,1... | collective-permute-start | bytes 516104 | tf_op jit(solution)/shard_map/ppermute | solution.py:940
  5.0 4.0 %collective-permute-start.3 = (f32[336,128]{1,0:T(8,128)S(1)}, f32[336,128]{1,0:T(8,128)S(1)}, u32[]{:S(2)}, u32[]{:S(2)}) collective-permute-start(f32[336,128]{1,0:T(8,128)S(1)} %get-tuple-element.97), channel_id=1, source_target_pairs={{0,7},{1,0},{2,1},{3,2},{4,3},{5,4},{6,5},{7,6},{8,15},{9,8},{10,9... | collective-permute-start | bytes 516104 | tf_op jit(solution)/shard_map/ppermute | solution.py:940
  9.1 3.8 %shard_map.68 = (f32[320,128]{1,0:T(8,128)S(1)}, f32[320,128]{1,0:T(8,128)S(1)}) custom-call(f32[19,256,128]{2,1,0:T(8,128)} %bitcast.82, s32[256,128]{1,0:T(8,128)} %bitcast.76), custom_call_target="tpu_custom_call" | custom-call | flops 1000000 | bytes 13000000 | tf_op jit(solution)/shard_map/pallas_call | solution.py:81
  12.8 2.8 %collective-permute-start = (f32[320,128]{1,0:T(8,128)S(1)}, f32[320,128]{1,0:T(8,128)S(1)}, u32[]{:S(2)}, u32[]{:S(2)}) collective-permute-start(f32[320,128]{1,0:T(8,128)S(1)} %get-tuple-element.91), channel_id=1, source_target_pairs={{0,192},{64,0},{128,64},{192,128},{1,193},{65,1},{129,65},{193,129... | collective-permute-start | bytes 491528 | tf_op jit(solution)/shard_map/ppermute | solution.py:935
  15.7 1.6 %collective-permute-start.6 = (f32[336,128]{1,0:T(8,128)S(1)}, f32[336,128]{1,0:T(8,128)S(1)}, u32[]{:S(2)}, u32[]{:S(2)}) collective-permute-start(f32[336,128]{1,0:T(8,128)S(1)} %pad_maximum_fusion), channel_id=1, source_target_pairs={{0,3},{1,4},{2,5},{3,6},{4,7},{5,0},{6,1},{7,2},{8,11},{9,12},{10,... | collective-permute-start | bytes 516104 | tf_op jit(solution)/shard_map/ppermute | solution.py:940
  17.3 3.0 %collective-permute-start.7 = (f32[336,128]{1,0:T(8,128)S(1)}, f32[336,128]{1,0:T(8,128)S(1)}, u32[]{:S(2)}, u32[]{:S(2)}) collective-permute-start(f32[336,128]{1,0:T(8,128)S(1)} %pad_maximum_fusion.1), channel_id=1, source_target_pairs={{0,5},{1,6},{2,7},{3,0},{4,1},{5,2},{6,3},{7,4},{8,13},{9,14},{10,... | collective-permute-start | bytes 516104 | tf_op jit(solution)/shard_map/ppermute | solution.py:940
  20.4 3.6 %collective-permute-start.5 = (f32[224,128]{1,0:T(8,128)S(1)}, f32[224,128]{1,0:T(8,128)S(1)}, u32[]{:S(2)}, u32[]{:S(2)}) collective-permute-start(f32[224,128]{1,0:T(8,128)S(1)} %get-tuple-element.99), channel_id=1, source_target_pairs={{0,6},{1,7},{2,0},{3,1},{4,2},{5,3},{6,4},{7,5},{8,14},{9,15},{10,... | collective-permute-start | bytes 344072 | tf_op jit(solution)/shard_map/ppermute | solution.py:940
  24.0 2.0 %collective-permute-done.1.left_ref = f32[320,128]{1,0:T(8,128)S(1)} collective-permute-done((f32[320,128]{1,0:T(8,128)S(1)}, f32[320,128]{1,0:T(8,128)S(1)}, u32[]{:S(2)}, u32[]{:S(2)}) %collective-permute-start.1) | collective-permute-done | bytes 163872 | tf_op jit(solution)/shard_map/ppermute | solution.py:935
  26.0 4.8 %shard_map.69 = (f32[19,256,128]{2,1,0:T(8,128)S(1)}, f32[19,256,128]{2,1,0:T(8,128)S(1)}, f32[512,128]{1,0:T(8,128)S(1)}, f32[4,512,128]{2,1,0:T(8,128)S(1)}, f...) custom-call(f32[6]{0:T(128)S(1)} %convert_element_type.3.flag_ref, f32[19,256,128]{2,1,0:T(8,128)} %bitcast.83, ...), custom_call_target="tpu_custom_call" | custom-call | flops 1000000 | bytes 20000000 | tf_op jit(solution)/shard_map/pallas_call | solution.py:81
  30.8 0.4 collective-permute-done.4.refs_3_
  31.1 2.0 %collective-permute-done.5.refs_4_ = f32[224,128]{1,0:T(8,128)S(1)} collective-permute-done((f32[224,128]{1,0:T(8,128)S(1)}, f32[224,128]{1,0:T(8,128)S(1)}, u32[]{:S(2)}, u32[]{:S(2)}) %collective-permute-start.5) | collective-permute-done | bytes 114720 | tf_op jit(solution)/shard_map/ppermute | solution.py:940
  33.1 0.9 shard_map.72
  34.0 2.5 %collective-permute-start.8 = (f32[112,128]{1,0:T(8,128)S(1)}, f32[112,128]{1,0:T(8,128)S(1)}, u32[]{:S(2)}, u32[]{:S(2)}) collective-permute-start(f32[112,128]{1,0:T(8,128)S(1)} %get-tuple-element.103), channel_id=1, source_target_pairs={{0,192},{64,0},{128,64},{192,128},{1,193},{65,1},{129,65},{193,129... | collective-permute-start | bytes 172040 | tf_op jit(solution)/shard_map/ppermute | solution.py:935
  36.6 2.2 %shard_map.71.dense_ref = f32[1792,128]{1,0:T(8,128)S(1)} custom-call(s32[1]{0:T(128)} %bitcast.8.me_ref, s32[1,1,8]{2,1,0:T(1,128)S(1)} %copy-done.1, f32[224,128]{1,0:T(8,128)S(1)} %get-tuple-element.95.refs_0_, f32[336,128]{1,0:T(8,128)S(1)} %collective-permute-done.2.refs_1_, f32[336,128]{1,0:T(8,128)S(1)} %collective-permute-done.3.refs_2_, ...), custom_call_target="tpu_custom_call" | custom-call | flops 1000000 | bytes 10000000 | tf_op jit(solution)/shard_map/pallas_call | solution.py:81
  38.8 2.0 %collective-permute-done.9.left_ref = f32[112,128]{1,0:T(8,128)S(1)} collective-permute-done((f32[112,128]{1,0:T(8,128)S(1)}, f32[112,128]{1,0:T(8,128)S(1)}, u32[]{:S(2)}, u32[]{:S(2)}) %collective-permute-start.9) | collective-permute-done | bytes 57376 | tf_op jit(solution)/shard_map/ppermute | solution.py:935
  40.8 2.0 %shard_map.73 = (f32[7,512,128]{2,1,0:T(8,128)S(1)}, f32[224,128]{1,0:T(8,128)S(1)}, f32[224,128]{1,0:T(8,128)S(1)}) custom-call(f32[1792,128]{1,0:T(8,128)S(1)} %shard_map.71.dense_ref, f32[112,128]{1,0:T(8,128)S(1)} %collective-permute-done.8.right_ref, f32[112,128]{1,0:T(8,128)S(1)} %collective-permute-done.9.left_ref, ...), custom_call_target="tpu_custom_call" | custom-call | flops 10000000 | bytes 10000000 | tf_op jit(solution)/shard_map/pallas_call | solution.py:81
  42.9 2.9 %collective-permute-start.11 = (f32[224,128]{1,0:T(8,128)S(1)}, f32[224,128]{1,0:T(8,128)S(1)}, u32[]{:S(2)}, u32[]{:S(2)}) collective-permute-start(f32[224,128]{1,0:T(8,128)S(1)} %get-tuple-element.111), channel_id=1, source_target_pairs={{0,56},{8,0},{16,8},{24,16},{32,24},{40,32},{48,40},{56,48},{1,57}... | collective-permute-start | bytes 344072 | tf_op jit(solution)/shard_map/ppermute | solution.py:935
  45.9 2.2 %shard_map.74 = (f32[224,128]{1,0:T(8,128)S(1)}, f32[224,128]{1,0:T(8,128)S(1)}, f32[19,1152,128]{2,1,0:T(8,128)S(1)}, f32[7,512,128]{2,1,0:T(8,128)S(1)}) custom-call(f32[19,256,128]{2,1,0:T(8,128)S(1)} %get-tuple-element.93.pops_ref.refs_0_, f32[19,256,128]{2,1,0:T(8,128)S(1)} %get-tuple-element.94.side_ref.refs_1_, ...), custom_call_target="tpu_custom_call" | custom-call | flops 10000000 | bytes 10000000 | tf_op jit(solution)/shard_map/pallas_call | solution.py:81
  48.2 0.2 collective-permute-done.11.yhi_ref.refs_9_
  48.5 4.4 %collective-permute-start.12 = (f32[256,128]{1,0:T(8,128)S(1)}, f32[256,128]{1,0:T(8,128)S(1)}, u32[]{:S(2)}, u32[]{:S(2)}) collective-permute-start(f32[256,128]{1,0:T(8,128)S(1)} %get-tuple-element.203), channel_id=1, source_target_pairs={{0,1},{1,2},{2,3},{3,4},{4,5},{5,6},{6,7},{7,0},{8,9},{9,10},{10,1... | collective-permute-start | bytes 393224 | tf_op jit(solution)/shard_map/ppermute | solution.py:935
  52.9 0.3 collective-permute-start.13
  53.2 0.7 shard_map.75
  53.9 2.7 %shard_map.76 = (f32[19,256,128]{2,1,0:T(8,128)S(1)}, f32[19,256,128]{2,1,0:T(8,128)S(1)}, f32[7,512,128]{2,1,0:T(8,128)S(1)}, f32[4,512,128]{2,1,0:T(8,128)S(1)...) custom-call(f32[19,256,128]{2,1,0:T(8,128)S(1)} %get-tuple-element.9, ...), custom_call_target="tpu_custom_call", output_to_operand_aliasing={{0}: (0, {}), {1}: (1, {}), {2}: (2, {}), {3}: (3, {}), {4}... | custom-call | flops 10000000 | bytes 10000000 | tf_op jit(solution)/shard_map/pallas_call | solution.py:81
  56.6 0.5 collective-permute-done.13.zhi_ref.refs_11_
  57.1 0.9 shard_map.77
  58.0 1.2 shard_map.78
  59.2 2.7 %collective-permute-start.15 = (f32[208,128]{1,0:T(8,128)S(1)}, f32[208,128]{1,0:T(8,128)S(1)}, u32[]{:S(2)}, u32[]{:S(2)}) collective-permute-start(f32[208,128]{1,0:T(8,128)S(1)} %get-tuple-element.133), channel_id=1, source_target_pairs={{0,56},{8,0},{16,8},{24,16},{32,24},{40,32},{48,40},{56,48},{1,57}... | collective-permute-start | bytes 319496 | tf_op jit(solution)/shard_map/ppermute | solution.py:935
  62.0 1.3 %collective-permute-start.14 = (f32[208,128]{1,0:T(8,128)S(1)}, f32[208,128]{1,0:T(8,128)S(1)}, u32[]{:S(2)}, u32[]{:S(2)}) collective-permute-start(f32[208,128]{1,0:T(8,128)S(1)} %get-tuple-element.132), channel_id=1, source_target_pairs={{0,8},{8,16},{16,24},{24,32},{32,40},{40,48},{48,56},{56,0},{1,9},... | collective-permute-start | bytes 319496 | tf_op jit(solution)/shard_map/ppermute | solution.py:935
  63.4 2.2 %shard_map.79 = (f32[208,128]{1,0:T(8,128)S(1)}, f32[208,128]{1,0:T(8,128)S(1)}, f32[19,1152,128]{2,1,0:T(8,128)S(1)}, f32[7,512,128]{2,1,0:T(8,128)S(1)}) custom-call(f32[19,256,128]{2,1,0:T(8,128)S(1)} %get-tuple-element.126.refs_0_, f32[19,256,128]{2,1,0:T(8,128)S(1)} %get-tuple-element.127.refs_1_, f32[7,512,128]{2,1,0:T(8,128)S(1)} %get-tuple-element.128.refs_2_, ...), custom_call_target="tpu_custom_call" | custom-call | flops 10000000 | bytes 10000000 | tf_op jit(solution)/shard_map/pallas_call | solution.py:81
  65.8 1.7 %collective-permute-start.16 = (f32[240,128]{1,0:T(8,128)S(1)}, f32[240,128]{1,0:T(8,128)S(1)}, u32[]{:S(2)}, u32[]{:S(2)}) collective-permute-start(f32[240,128]{1,0:T(8,128)S(1)} %get-tuple-element.201), channel_id=1, source_target_pairs={{0,1},{1,2},{2,3},{3,4},{4,5},{5,6},{6,7},{7,0},{8,9},{9,10},{10,1... | collective-permute-start | bytes 368648 | tf_op jit(solution)/shard_map/ppermute | solution.py:935
  67.6 1.0 collective-permute-start.17
  68.6 2.7 %shard_map.80 = (f32[19,256,128]{2,1,0:T(8,128)S(1)}, f32[19,256,128]{2,1,0:T(8,128)S(1)}, f32[7,512,128]{2,1,0:T(8,128)S(1)}, f32[4,512,128]{2,1,0:T(8,128)S(1)...) custom-call(f32[19,256,128]{2,1,0:T(8,128)S(1)} %get-tuple-element.1, ...), custom_call_target="tpu_custom_call", output_to_operand_aliasing={{0}: (0, {}), {1}: (1, {}), {2}: (2, {}), {3}: (3, {}), {4}... | custom-call | flops 10000000 | bytes 10000000 | tf_op jit(solution)/shard_map/pallas_call | solution.py:81
  71.3 0.2 collective-permute-done.16.refs_10_
  71.6 1.2 shard_map.81
  72.8 1.7 %collective-permute-start.19 = (f32[208,128]{1,0:T(8,128)S(1)}, f32[208,128]{1,0:T(8,128)S(1)}, u32[]{:S(2)}, u32[]{:S(2)}) collective-permute-start(f32[208,128]{1,0:T(8,128)S(1)} %get-tuple-element.149), channel_id=1, source_target_pairs={{0,56},{8,0},{16,8},{24,16},{32,24},{40,32},{48,40},{56,48},{1,57}... | collective-permute-start | bytes 319496 | tf_op jit(solution)/shard_map/ppermute | solution.py:935
  74.5 2.5 %collective-permute-start.18 = (f32[208,128]{1,0:T(8,128)S(1)}, f32[208,128]{1,0:T(8,128)S(1)}, u32[]{:S(2)}, u32[]{:S(2)}) collective-permute-start(f32[208,128]{1,0:T(8,128)S(1)} %get-tuple-element.148), channel_id=1, source_target_pairs={{0,8},{8,16},{16,24},{24,32},{32,40},{40,48},{48,56},{56,0},{1,9},... | collective-permute-start | bytes 319496 | tf_op jit(solution)/shard_map/ppermute | solution.py:935
  77.0 2.2 %shard_map.82 = (f32[208,128]{1,0:T(8,128)S(1)}, f32[208,128]{1,0:T(8,128)S(1)}, f32[19,1152,128]{2,1,0:T(8,128)S(1)}, f32[7,512,128]{2,1,0:T(8,128)S(1)}) custom-call(f32[19,256,128]{2,1,0:T(8,128)S(1)} %get-tuple-element.142.refs_0_, f32[19,256,128]{2,1,0:T(8,128)S(1)} %get-tuple-element.143.refs_1_, f32[7,512,128]{2,1,0:T(8,128)S(1)} %get-tuple-element.144.refs_2_, ...), custom_call_target="tpu_custom_call" | custom-call | flops 10000000 | bytes 10000000 | tf_op jit(solution)/shard_map/pallas_call | solution.py:81
  79.2 0.2 collective-permute-done.19.refs_9_
  79.6 0.3 collective-permute-start.20
  79.9 2.5 %collective-permute-start.21 = (f32[240,128]{1,0:T(8,128)S(1)}, f32[240,128]{1,0:T(8,128)S(1)}, u32[]{:S(2)}, u32[]{:S(2)}) collective-permute-start(f32[240,128]{1,0:T(8,128)S(1)} %get-tuple-element.198), channel_id=1, source_target_pairs={{0,7},{1,0},{2,1},{3,2},{4,3},{5,4},{6,5},{7,6},{8,15},{9,8},{10,9... | collective-permute-start | bytes 368648 | tf_op jit(solution)/shard_map/ppermute | solution.py:935
  82.3 2.7 %shard_map.83 = (f32[19,256,128]{2,1,0:T(8,128)S(1)}, f32[19,256,128]{2,1,0:T(8,128)S(1)}, f32[7,512,128]{2,1,0:T(8,128)S(1)}, f32[4,512,128]{2,1,0:T(8,128)S(1)...) custom-call(f32[19,256,128]{2,1,0:T(8,128)S(1)} %get-tuple-element.1, ...), custom_call_target="tpu_custom_call", output_to_operand_aliasing={{0}: (0, {}), {1}: (1, {}), {2}: (2, {}), {3}: (3, {}), {4}... | custom-call | flops 10000000 | bytes 10000000 | tf_op jit(solution)/shard_map/pallas_call | solution.py:81
  85.0 0.7 collective-permute-done.20.refs_10_
  85.7 1.2 shard_map.84
  86.9 0.4 collective-permute-start.23
  87.3 2.6 %collective-permute-start.22 = (f32[208,128]{1,0:T(8,128)S(1)}, f32[208,128]{1,0:T(8,128)S(1)}, u32[]{:S(2)}, u32[]{:S(2)}) collective-permute-start(f32[208,128]{1,0:T(8,128)S(1)} %get-tuple-element.164), channel_id=1, source_target_pairs={{0,8},{8,16},{16,24},{24,32},{32,40},{40,48},{48,56},{56,0},{1,9},... | collective-permute-start | bytes 319496 | tf_op jit(solution)/shard_map/ppermute | solution.py:935
  89.9 2.1 %shard_map.85 = (f32[208,128]{1,0:T(8,128)S(1)}, f32[208,128]{1,0:T(8,128)S(1)}, f32[19,1152,128]{2,1,0:T(8,128)S(1)}, f32[7,512,128]{2,1,0:T(8,128)S(1)}) custom-call(f32[19,256,128]{2,1,0:T(8,128)S(1)} %get-tuple-element.158.refs_0_, f32[19,256,128]{2,1,0:T(8,128)S(1)} %get-tuple-element.159.refs_1_, f32[7,512,128]{2,1,0:T(8,128)S(1)} %get-tuple-element.160.refs_2_, ...), custom_call_target="tpu_custom_call" | custom-call | flops 10000000 | bytes 10000000 | tf_op jit(solution)/shard_map/pallas_call | solution.py:81
  92.1 0.2 collective-permute-done.23.refs_9_.refs_5_
  92.5 0.7 collective-permute-start.24
  93.2 2.6 %collective-permute-start.25 = (f32[240,128]{1,0:T(8,128)S(1)}, f32[240,128]{1,0:T(8,128)S(1)}, u32[]{:S(2)}, u32[]{:S(2)}) collective-permute-start(f32[240,128]{1,0:T(8,128)S(1)} %get-tuple-element.196), channel_id=1, source_target_pairs={{0,7},{1,0},{2,1},{3,2},{4,3},{5,4},{6,5},{7,6},{8,15},{9,8},{10,9... | collective-permute-start | bytes 368648 | tf_op jit(solution)/shard_map/ppermute | solution.py:935
  95.8 2.6 %shard_map.86 = (f32[19,1152,128]{2,1,0:T(8,128)S(1)}, f32[7,512,128]{2,1,0:T(8,128)S(1)}, f32[1792,128]{1,0:T(8,128)S(1)}) custom-call(f32[19,256,128]{2,1,0:T(8,128)S(1)} %get-tuple-element.158.refs_0_, f32[19,256,128]{2,1,0:T(8,128)S(1)} %get-tuple-element.159.refs_1_, ...), custom_call_target="tpu_custom_call", output_to_operand_aliasing={{0}: (4, {}), {1}: (5, {})} | custom-call | flops 10000000 | bytes 10000000 | tf_op jit(solution)/shard_map/pallas_call | solution.py:81
  98.4 0.2 collective-permute-done.24.refs_6_.refs_10_
  98.6 1.0 shard_map.87
  99.6 1.3 collective-permute-start.26
  100.9 1.9 %collective-permute-start.27 = (f32[336,128]{1,0:T(8,128)S(1)}, f32[336,128]{1,0:T(8,128)S(1)}, u32[]{:S(2)}, u32[]{:S(2)}) collective-permute-start(f32[336,128]{1,0:T(8,128)S(1)} %get-tuple-element.175), channel_id=1, source_target_pairs={{0,7},{1,0},{2,1},{3,2},{4,3},{5,4},{6,5},{7,6},{8,15},{9,8},{10,9... | collective-permute-start | bytes 516104 | tf_op jit(solution)/shard_map/ppermute | solution.py:940
  102.8 4.4 %collective-permute-done.26.refs_1_ = f32[336,128]{1,0:T(8,128)S(1)} collective-permute-done((f32[336,128]{1,0:T(8,128)S(1)}, f32[336,128]{1,0:T(8,128)S(1)}, u32[]{:S(2)}, u32[]{:S(2)}) %collective-permute-start.26) | collective-permute-done | bytes 172064 | tf_op jit(solution)/shard_map/ppermute | solution.py:940
  107.2 0.6 collective-permute-start.30
  107.8 4.0 %collective-permute-start.31 = (f32[336,128]{1,0:T(8,128)S(1)}, f32[336,128]{1,0:T(8,128)S(1)}, u32[]{:S(2)}, u32[]{:S(2)}) collective-permute-start(f32[336,128]{1,0:T(8,128)S(1)} %pad_maximum_fusion.3), channel_id=1, source_target_pairs={{0,5},{1,6},{2,7},{3,0},{4,1},{5,2},{6,3},{7,4},{8,13},{9,14},{10,... | collective-permute-start | bytes 516104 | tf_op jit(solution)/shard_map/ppermute | solution.py:940
  111.9 3.6 %collective-permute-start.29 = (f32[224,128]{1,0:T(8,128)S(1)}, f32[224,128]{1,0:T(8,128)S(1)}, u32[]{:S(2)}, u32[]{:S(2)}) collective-permute-start(f32[224,128]{1,0:T(8,128)S(1)} %get-tuple-element.177), channel_id=1, source_target_pairs={{0,6},{1,7},{2,0},{3,1},{4,2},{5,3},{6,4},{7,5},{8,14},{9,15},{10,... | collective-permute-start | bytes 344072 | tf_op jit(solution)/shard_map/ppermute | solution.py:940
  115.5 3.1 %shard_map.88 = (f32[19,256,128]{2,1,0:T(8,128)}, f32[19,1152,128]{2,1,0:T(8,128)S(1)}) custom-call(f32[19,256,128]{2,1,0:T(8,128)S(1)} %get-tuple-element.158.refs_0_, f32[19,256,128]{2,1,0:T(8,128)S(1)} %get-tuple-element.159.refs_1_, f32[7,512,128]{2,1,0:T(8,128)S(1)} %get-tuple-element.160.refs_2_, ...), custom_call_target="tpu_custom_call", output_to_operand_aliasing={{1}: (4, {})} | custom-call | flops 10000000 | bytes 10000000 | tf_op jit(solution)/shard_map/pallas_call | solution.py:81
  118.5 6.2 %collective-permute-done.28.refs_3_ = f32[224,128]{1,0:T(8,128)S(1)} collective-permute-done((f32[224,128]{1,0:T(8,128)S(1)}, f32[224,128]{1,0:T(8,128)S(1)}, u32[]{:S(2)}, u32[]{:S(2)}) %collective-permute-start.28) | collective-permute-done | bytes 114720 | tf_op jit(solution)/shard_map/ppermute | solution.py:940
  124.7 3.5 %collective-permute-done.29.refs_4_ = f32[224,128]{1,0:T(8,128)S(1)} collective-permute-done((f32[224,128]{1,0:T(8,128)S(1)}, f32[224,128]{1,0:T(8,128)S(1)}, u32[]{:S(2)}, u32[]{:S(2)}) %collective-permute-start.29) | collective-permute-done | bytes 114720 | tf_op jit(solution)/shard_map/ppermute | solution.py:940
  128.2 1.8 %shard_map.89 = f32[1792,128]{1,0:T(8,128)} custom-call(s32[1]{0:T(128)} %bitcast.8.me_ref, s32[8]{0:T(128)S(1)} %copy-done.3, f32[224,128]{1,0:T(8,128)S(1)} %get-tuple-element.173.refs_0_, f32[336,128]{1,0:T(8,128)S(1)} %collective-permute-done.26.refs_1_, f32[336,128]{1,0:T(8,128)S(1)} %collective-permute-done.27.refs_2_, ...), custom_call_target="tpu_custom_call" | custom-call | flops 1 | bytes 2000000 | tf_op jit(solution)/shard_map/pallas_call | solution.py:81
  (70 shorter events, 1.3 us)
Async XLA Ops:
  0.6 25.4 %copy-start = (s32[16,16,128]{2,1,0:T(8,128)S(1)}, s32[16,16,128]{2,1,0:T(8,128)}, u32[]{:S(2)}) copy-start(s32[16,16,128]{2,1,0:T(8,128)} %param.7) | copy-start | bytes 393220
  0.6 0.7 copy-start.2
  3.3 12.3 %collective-permute-start.2 = (f32[336,128]{1,0:T(8,128)S(1)}, f32[336,128]{1,0:T(8,128)S(1)}, u32[]{:S(2)}, u32[]{:S(2)}) collective-permute-start(f32[336,128]{1,0:T(8,128)S(1)} %get-tuple-element.96), channel_id=1, source_target_pairs={{0,1},{1,2},{2,3},{3,4},{4,5},{5,6},{6,7},{7,0},{8,9},{9,10},{10,1... | collective-permute-start | bytes 516104 | tf_op jit(solution)/shard_map/ppermute | solution.py:940
  5.0 12.3 %collective-permute-start.3 = (f32[336,128]{1,0:T(8,128)S(1)}, f32[336,128]{1,0:T(8,128)S(1)}, u32[]{:S(2)}, u32[]{:S(2)}) collective-permute-start(f32[336,128]{1,0:T(8,128)S(1)} %get-tuple-element.97), channel_id=1, source_target_pairs={{0,7},{1,0},{2,1},{3,2},{4,3},{5,4},{6,5},{7,6},{8,15},{9,8},{10,9... | collective-permute-start | bytes 516104 | tf_op jit(solution)/shard_map/ppermute | solution.py:940
  12.8 20.3 %copy-start.1 = (s32[1,1,8]{2,1,0:T(1,128)S(1)}, s32[1,1,8]{2,1,0:T(1,128)}, u32[]{:S(2)}) copy-start(s32[1,1,8]{2,1,0:T(1,128)} %slot_ref.8) | copy-start | bytes 100
  12.8 7.5 %collective-permute-start = (f32[320,128]{1,0:T(8,128)S(1)}, f32[320,128]{1,0:T(8,128)S(1)}, u32[]{:S(2)}, u32[]{:S(2)}) collective-permute-start(f32[320,128]{1,0:T(8,128)S(1)} %get-tuple-element.91), channel_id=1, source_target_pairs={{0,192},{64,0},{128,64},{192,128},{1,193},{65,1},{129,65},{193,129... | collective-permute-start | bytes 491528 | tf_op jit(solution)/shard_map/ppermute | solution.py:935
  15.7 17.5 %collective-permute-start.6 = (f32[336,128]{1,0:T(8,128)S(1)}, f32[336,128]{1,0:T(8,128)S(1)}, u32[]{:S(2)}, u32[]{:S(2)}) collective-permute-start(f32[336,128]{1,0:T(8,128)S(1)} %pad_maximum_fusion), channel_id=1, source_target_pairs={{0,3},{1,4},{2,5},{3,6},{4,7},{5,0},{6,1},{7,2},{8,11},{9,12},{10,... | collective-permute-start | bytes 516104 | tf_op jit(solution)/shard_map/ppermute | solution.py:940
  17.3 15.8 %collective-permute-start.7 = (f32[336,128]{1,0:T(8,128)S(1)}, f32[336,128]{1,0:T(8,128)S(1)}, u32[]{:S(2)}, u32[]{:S(2)}) collective-permute-start(f32[336,128]{1,0:T(8,128)S(1)} %pad_maximum_fusion.1), channel_id=1, source_target_pairs={{0,5},{1,6},{2,7},{3,0},{4,1},{5,2},{6,3},{7,4},{8,13},{9,14},{10,... | collective-permute-start | bytes 516104 | tf_op jit(solution)/shard_map/ppermute | solution.py:940
  20.3 5.7 %collective-permute-start.1 = (f32[320,128]{1,0:T(8,128)S(1)}, f32[320,128]{1,0:T(8,128)S(1)}, u32[]{:S(2)}, u32[]{:S(2)}) collective-permute-start(f32[320,128]{1,0:T(8,128)S(1)} %get-tuple-element.92), channel_id=1, source_target_pairs={{0,64},{64,128},{128,192},{192,0},{1,65},{65,129},{129,193},{193,1... | collective-permute-start | bytes 491528 | tf_op jit(solution)/shard_map/ppermute | solution.py:935
  20.4 10.8 %collective-permute-start.4 = (f32[224,128]{1,0:T(8,128)S(1)}, f32[224,128]{1,0:T(8,128)S(1)}, u32[]{:S(2)}, u32[]{:S(2)}) collective-permute-start(f32[224,128]{1,0:T(8,128)S(1)} %get-tuple-element.98), channel_id=1, source_target_pairs={{0,2},{1,3},{2,4},{3,5},{4,6},{5,7},{6,0},{7,1},{8,10},{9,11},{10,... | collective-permute-start | bytes 344072 | tf_op jit(solution)/shard_map/ppermute | solution.py:940
  20.4 12.8 %collective-permute-start.5 = (f32[224,128]{1,0:T(8,128)S(1)}, f32[224,128]{1,0:T(8,128)S(1)}, u32[]{:S(2)}, u32[]{:S(2)}) collective-permute-start(f32[224,128]{1,0:T(8,128)S(1)} %get-tuple-element.99), channel_id=1, source_target_pairs={{0,6},{1,7},{2,0},{3,1},{4,2},{5,3},{6,4},{7,5},{8,14},{9,15},{10,... | collective-permute-start | bytes 344072 | tf_op jit(solution)/shard_map/ppermute | solution.py:940
  34.0 4.8 %collective-permute-start.8 = (f32[112,128]{1,0:T(8,128)S(1)}, f32[112,128]{1,0:T(8,128)S(1)}, u32[]{:S(2)}, u32[]{:S(2)}) collective-permute-start(f32[112,128]{1,0:T(8,128)S(1)} %get-tuple-element.103), channel_id=1, source_target_pairs={{0,192},{64,0},{128,64},{192,128},{1,193},{65,1},{129,65},{193,129... | collective-permute-start | bytes 172040 | tf_op jit(solution)/shard_map/ppermute | solution.py:935
  36.6 4.2 %collective-permute-start.9 = (f32[112,128]{1,0:T(8,128)S(1)}, f32[112,128]{1,0:T(8,128)S(1)}, u32[]{:S(2)}, u32[]{:S(2)}) collective-permute-start(f32[112,128]{1,0:T(8,128)S(1)} %get-tuple-element.104), channel_id=1, source_target_pairs={{0,64},{64,128},{128,192},{192,0},{1,65},{65,129},{129,193},{193,1... | collective-permute-start | bytes 172040 | tf_op jit(solution)/shard_map/ppermute | solution.py:935
  42.9 5.4 %collective-permute-start.11 = (f32[224,128]{1,0:T(8,128)S(1)}, f32[224,128]{1,0:T(8,128)S(1)}, u32[]{:S(2)}, u32[]{:S(2)}) collective-permute-start(f32[224,128]{1,0:T(8,128)S(1)} %get-tuple-element.111), channel_id=1, source_target_pairs={{0,56},{8,0},{16,8},{24,16},{32,24},{40,32},{48,40},{56,48},{1,57}... | collective-permute-start | bytes 344072 | tf_op jit(solution)/shard_map/ppermute | solution.py:935
  45.8 2.5 %collective-permute-start.10 = (f32[224,128]{1,0:T(8,128)S(1)}, f32[224,128]{1,0:T(8,128)S(1)}, u32[]{:S(2)}, u32[]{:S(2)}) collective-permute-start(f32[224,128]{1,0:T(8,128)S(1)} %get-tuple-element.110), channel_id=1, source_target_pairs={{0,8},{8,16},{16,24},{24,32},{32,40},{40,48},{48,56},{56,0},{1,9},... | collective-permute-start | bytes 344072 | tf_op jit(solution)/shard_map/ppermute | solution.py:935
  48.5 8.1 %collective-permute-start.12 = (f32[256,128]{1,0:T(8,128)S(1)}, f32[256,128]{1,0:T(8,128)S(1)}, u32[]{:S(2)}, u32[]{:S(2)}) collective-permute-start(f32[256,128]{1,0:T(8,128)S(1)} %get-tuple-element.203), channel_id=1, source_target_pairs={{0,1},{1,2},{2,3},{3,4},{4,5},{5,6},{6,7},{7,0},{8,9},{9,10},{10,1... | collective-permute-start | bytes 393224 | tf_op jit(solution)/shard_map/ppermute | solution.py:935
  52.9 4.3 %collective-permute-start.13 = (f32[256,128]{1,0:T(8,128)S(1)}, f32[256,128]{1,0:T(8,128)S(1)}, u32[]{:S(2)}, u32[]{:S(2)}) collective-permute-start(f32[256,128]{1,0:T(8,128)S(1)} %get-tuple-element.202), channel_id=1, source_target_pairs={{0,7},{1,0},{2,1},{3,2},{4,3},{5,4},{6,5},{7,6},{8,15},{9,8},{10,9... | collective-permute-start | bytes 393224 | tf_op jit(solution)/shard_map/ppermute | solution.py:935
  59.2 6.4 %collective-permute-start.15 = (f32[208,128]{1,0:T(8,128)S(1)}, f32[208,128]{1,0:T(8,128)S(1)}, u32[]{:S(2)}, u32[]{:S(2)}) collective-permute-start(f32[208,128]{1,0:T(8,128)S(1)} %get-tuple-element.133), channel_id=1, source_target_pairs={{0,56},{8,0},{16,8},{24,16},{32,24},{40,32},{48,40},{56,48},{1,57}... | collective-permute-start | bytes 319496 | tf_op jit(solution)/shard_map/ppermute | solution.py:935
  62.0 3.6 %collective-permute-start.14 = (f32[208,128]{1,0:T(8,128)S(1)}, f32[208,128]{1,0:T(8,128)S(1)}, u32[]{:S(2)}, u32[]{:S(2)}) collective-permute-start(f32[208,128]{1,0:T(8,128)S(1)} %get-tuple-element.132), channel_id=1, source_target_pairs={{0,8},{8,16},{16,24},{24,32},{32,40},{40,48},{48,56},{56,0},{1,9},... | collective-permute-start | bytes 319496 | tf_op jit(solution)/shard_map/ppermute | solution.py:935
  65.8 5.7 %collective-permute-start.16 = (f32[240,128]{1,0:T(8,128)S(1)}, f32[240,128]{1,0:T(8,128)S(1)}, u32[]{:S(2)}, u32[]{:S(2)}) collective-permute-start(f32[240,128]{1,0:T(8,128)S(1)} %get-tuple-element.201), channel_id=1, source_target_pairs={{0,1},{1,2},{2,3},{3,4},{4,5},{5,6},{6,7},{7,0},{8,9},{9,10},{10,1... | collective-permute-start | bytes 368648 | tf_op jit(solution)/shard_map/ppermute | solution.py:935
  67.6 4.1 %collective-permute-start.17 = (f32[240,128]{1,0:T(8,128)S(1)}, f32[240,128]{1,0:T(8,128)S(1)}, u32[]{:S(2)}, u32[]{:S(2)}) collective-permute-start(f32[240,128]{1,0:T(8,128)S(1)} %get-tuple-element.200), channel_id=1, source_target_pairs={{0,7},{1,0},{2,1},{3,2},{4,3},{5,4},{6,5},{7,6},{8,15},{9,8},{10,9... | collective-permute-start | bytes 368648 | tf_op jit(solution)/shard_map/ppermute | solution.py:935
  72.8 6.5 %collective-permute-start.19 = (f32[208,128]{1,0:T(8,128)S(1)}, f32[208,128]{1,0:T(8,128)S(1)}, u32[]{:S(2)}, u32[]{:S(2)}) collective-permute-start(f32[208,128]{1,0:T(8,128)S(1)} %get-tuple-element.149), channel_id=1, source_target_pairs={{0,56},{8,0},{16,8},{24,16},{32,24},{40,32},{48,40},{56,48},{1,57}... | collective-permute-start | bytes 319496 | tf_op jit(solution)/shard_map/ppermute | solution.py:935
  74.5 4.8 %collective-permute-start.18 = (f32[208,128]{1,0:T(8,128)S(1)}, f32[208,128]{1,0:T(8,128)S(1)}, u32[]{:S(2)}, u32[]{:S(2)}) collective-permute-start(f32[208,128]{1,0:T(8,128)S(1)} %get-tuple-element.148), channel_id=1, source_target_pairs={{0,8},{8,16},{16,24},{24,32},{32,40},{40,48},{48,56},{56,0},{1,9},... | collective-permute-start | bytes 319496 | tf_op jit(solution)/shard_map/ppermute | solution.py:935
  79.6 6.1 %collective-permute-start.20 = (f32[240,128]{1,0:T(8,128)S(1)}, f32[240,128]{1,0:T(8,128)S(1)}, u32[]{:S(2)}, u32[]{:S(2)}) collective-permute-start(f32[240,128]{1,0:T(8,128)S(1)} %get-tuple-element.199), channel_id=1, source_target_pairs={{0,1},{1,2},{2,3},{3,4},{4,5},{5,6},{6,7},{7,0},{8,9},{9,10},{10,1... | collective-permute-start | bytes 368648 | tf_op jit(solution)/shard_map/ppermute | solution.py:935
  79.9 5.8 %collective-permute-start.21 = (f32[240,128]{1,0:T(8,128)S(1)}, f32[240,128]{1,0:T(8,128)S(1)}, u32[]{:S(2)}, u32[]{:S(2)}) collective-permute-start(f32[240,128]{1,0:T(8,128)S(1)} %get-tuple-element.198), channel_id=1, source_target_pairs={{0,7},{1,0},{2,1},{3,2},{4,3},{5,4},{6,5},{7,6},{8,15},{9,8},{10,9... | collective-permute-start | bytes 368648 | tf_op jit(solution)/shard_map/ppermute | solution.py:935
  86.9 5.4 %collective-permute-start.23 = (f32[208,128]{1,0:T(8,128)S(1)}, f32[208,128]{1,0:T(8,128)S(1)}, u32[]{:S(2)}, u32[]{:S(2)}) collective-permute-start(f32[208,128]{1,0:T(8,128)S(1)} %get-tuple-element.165), channel_id=1, source_target_pairs={{0,56},{8,0},{16,8},{24,16},{32,24},{40,32},{48,40},{56,48},{1,57}... | collective-permute-start | bytes 319496 | tf_op jit(solution)/shard_map/ppermute | solution.py:935
  87.3 5.0 %collective-permute-start.22 = (f32[208,128]{1,0:T(8,128)S(1)}, f32[208,128]{1,0:T(8,128)S(1)}, u32[]{:S(2)}, u32[]{:S(2)}) collective-permute-start(f32[208,128]{1,0:T(8,128)S(1)} %get-tuple-element.164), channel_id=1, source_target_pairs={{0,8},{8,16},{16,24},{24,32},{32,40},{40,48},{48,56},{56,0},{1,9},... | collective-permute-start | bytes 319496 | tf_op jit(solution)/shard_map/ppermute | solution.py:935
  92.5 6.2 %collective-permute-start.24 = (f32[240,128]{1,0:T(8,128)S(1)}, f32[240,128]{1,0:T(8,128)S(1)}, u32[]{:S(2)}, u32[]{:S(2)}) collective-permute-start(f32[240,128]{1,0:T(8,128)S(1)} %get-tuple-element.197), channel_id=1, source_target_pairs={{0,1},{1,2},{2,3},{3,4},{4,5},{5,6},{6,7},{7,0},{8,9},{9,10},{10,1... | collective-permute-start | bytes 368648 | tf_op jit(solution)/shard_map/ppermute | solution.py:935
  93.2 5.5 %collective-permute-start.25 = (f32[240,128]{1,0:T(8,128)S(1)}, f32[240,128]{1,0:T(8,128)S(1)}, u32[]{:S(2)}, u32[]{:S(2)}) collective-permute-start(f32[240,128]{1,0:T(8,128)S(1)} %get-tuple-element.196), channel_id=1, source_target_pairs={{0,7},{1,0},{2,1},{3,2},{4,3},{5,4},{6,5},{7,6},{8,15},{9,8},{10,9... | collective-permute-start | bytes 368648 | tf_op jit(solution)/shard_map/ppermute | solution.py:935
  99.6 7.6 %collective-permute-start.26 = (f32[336,128]{1,0:T(8,128)S(1)}, f32[336,128]{1,0:T(8,128)S(1)}, u32[]{:S(2)}, u32[]{:S(2)}) collective-permute-start(f32[336,128]{1,0:T(8,128)S(1)} %get-tuple-element.174), channel_id=1, source_target_pairs={{0,1},{1,2},{2,3},{3,4},{4,5},{5,6},{6,7},{7,0},{8,9},{9,10},{10,1... | collective-permute-start | bytes 516104 | tf_op jit(solution)/shard_map/ppermute | solution.py:940
  100.9 6.9 %collective-permute-start.27 = (f32[336,128]{1,0:T(8,128)S(1)}, f32[336,128]{1,0:T(8,128)S(1)}, u32[]{:S(2)}, u32[]{:S(2)}) collective-permute-start(f32[336,128]{1,0:T(8,128)S(1)} %get-tuple-element.175), channel_id=1, source_target_pairs={{0,7},{1,0},{2,1},{3,2},{4,3},{5,4},{6,5},{7,6},{8,15},{9,8},{10,9... | collective-permute-start | bytes 516104 | tf_op jit(solution)/shard_map/ppermute | solution.py:940
  107.2 21.0 %collective-permute-start.30 = (f32[336,128]{1,0:T(8,128)S(1)}, f32[336,128]{1,0:T(8,128)S(1)}, u32[]{:S(2)}, u32[]{:S(2)}) collective-permute-start(f32[336,128]{1,0:T(8,128)S(1)} %pad_maximum_fusion.2), channel_id=1, source_target_pairs={{0,3},{1,4},{2,5},{3,6},{4,7},{5,0},{6,1},{7,2},{8,11},{9,12},{10,... | collective-permute-start | bytes 516104 | tf_op jit(solution)/shard_map/ppermute | solution.py:940
  107.8 20.3 %collective-permute-start.31 = (f32[336,128]{1,0:T(8,128)S(1)}, f32[336,128]{1,0:T(8,128)S(1)}, u32[]{:S(2)}, u32[]{:S(2)}) collective-permute-start(f32[336,128]{1,0:T(8,128)S(1)} %pad_maximum_fusion.3), channel_id=1, source_target_pairs={{0,5},{1,6},{2,7},{3,0},{4,1},{5,2},{6,3},{7,4},{8,13},{9,14},{10,... | collective-permute-start | bytes 516104 | tf_op jit(solution)/shard_map/ppermute | solution.py:940
  111.9 12.8 %collective-permute-start.28 = (f32[224,128]{1,0:T(8,128)S(1)}, f32[224,128]{1,0:T(8,128)S(1)}, u32[]{:S(2)}, u32[]{:S(2)}) collective-permute-start(f32[224,128]{1,0:T(8,128)S(1)} %get-tuple-element.176), channel_id=1, source_target_pairs={{0,2},{1,3},{2,4},{3,5},{4,6},{5,7},{6,0},{7,1},{8,10},{9,11},{10,... | collective-permute-start | bytes 344072 | tf_op jit(solution)/shard_map/ppermute | solution.py:940
  111.9 16.3 %collective-permute-start.29 = (f32[224,128]{1,0:T(8,128)S(1)}, f32[224,128]{1,0:T(8,128)S(1)}, u32[]{:S(2)}, u32[]{:S(2)}) collective-permute-start(f32[224,128]{1,0:T(8,128)S(1)} %get-tuple-element.177), channel_id=1, source_target_pairs={{0,6},{1,7},{2,0},{3,1},{4,2},{5,3},{6,4},{7,5},{8,14},{9,15},{10,... | collective-permute-start | bytes 344072 | tf_op jit(solution)/shard_map/ppermute | solution.py:940
  115.5 12.7 %copy-start.3 = (s32[8]{0:T(128)S(1)}, s32[8]{0:T(128)}, u32[]{:S(2)}) copy-start(s32[8]{0:T(128)} %slot_ref.9) | copy-start | bytes 100

commit v5 on v4

--- a/solution.py
+++ b/solution.py
@@ -192,14 +192,17 @@
     return found
 
 
-def fill_messages(me, slots, blocks_ref, outs):
+def fill_messages(me, slots, blocks_ref, outs, ready=lambda comp: None):
     own, up1, down1, up2, down2, up3, down3 = outs
-    for off, ref in ((0, own), (1, up1), (7, down1), (2, up2), (6, down2), (3, up3), (5, down3)):
-        at = jnp.maximum(find(slots, (me + off) & 7), 0)
-        ref[pl.ds(0, ROW), :] = blocks_ref[pl.ds(at, ROW, stride=8), :]
-    at = jnp.maximum(find(slots, (me + 4) & 7), 0)
-    up1[pl.ds(ROW, HALF), :] = blocks_ref[pl.ds(at, HALF, stride=8), :]
-    down1[pl.ds(ROW, HALF), :] = blocks_ref[pl.ds(HALF * 8 + at, HALF, stride=8), :]
+    places = ((0, own), (1, up1), (7, down1), (2, up2), (6, down2), (3, up3), (5, down3))
+    slot_of = [jnp.maximum(find(slots, (me + off) & 7), 0) for off in range(8)]
+    for comp in range(7):
+        ready(comp)
+        for off, ref in places:
+            at = comp * 256 + slot_of[off]
+            ref[pl.ds(comp * 32, 32), :] = blocks_ref[pl.ds(at, 32, stride=8), :]
+    up1[pl.ds(ROW, HALF), :] = blocks_ref[pl.ds(slot_of[4], HALF, stride=8), :]
+    down1[pl.ds(ROW, HALF), :] = blocks_ref[pl.ds(HALF * 8 + slot_of[4], HALF, stride=8), :]
 
 
 def receive(me, slots, refs, out_ref):
@@ -218,11 +221,16 @@
 
 
 def gather_kernel(me_ref, slot_ref, state_ref, *refs):
-    *outs, blocks_ref, sem = refs
-    load = pltpu.make_async_copy(state_ref, blocks_ref, sem)
-    load.start()
-    load.wait()
-    fill_messages(me_ref[0], [slot_ref[s] for s in range(8)], blocks_ref, outs)
+    *outs, blocks_ref, sems = refs
+
+    def load(comp):
+        rows = pl.ds(comp * 256, 256)
+        return pltpu.make_async_copy(state_ref.at[rows], blocks_ref.at[rows], sems.at[comp])
+
+    for comp in range(7):
+        load(comp).start()
+    slots = [slot_ref[s] for s in range(8)]
+    fill_messages(me_ref[0], slots, blocks_ref, outs, lambda comp: load(comp).wait())
 
 
 def pick_kernel(me_ref, slot_ref, *refs):
@@ -756,7 +764,7 @@
             post_ref[i, pl.ds(pl.multiple_of(z * PLANE, PLANE), PLANE), :] = post[i]
         return carry
 
-    lax.fori_loop(0, B, body, 0, unroll=UNROLL)
+    lax.fori_loop(0, B, body, 0, unroll=2 * UNROLL)
     pops_refs = pops_ref, side_ref
     write_y_messages(pops_refs, post_ref, aux_ref, (ydn_ref, yup_ref), ring_ref=ring_ref)
 
@@ -972,7 +980,7 @@
     sent = tuple(held(n, L) for n in (ROW, ROW + HALF, ROW + HALF, ROW, ROW, ROW, ROW))
     state = solute_state.reshape(7, 8, 32, L).transpose(0, 2, 1, 3).reshape(BLOCKROWS, L)
     send = call(
-        gather_kernel, sent, [SMEM, SMEM, HBM], [turn, pltpu.SemaphoreType.DMA], 1, 2 * 10**6
+        gather_kernel, sent, [SMEM, SMEM, HBM], [turn, pltpu.SemaphoreType.DMA((7,))], 1, 2 * 10**6
     )(me, slot_block, state)
     recv = exchange_blocks(*send)
 

time: 130 us -> 130 us (level)
  no operation moved by 1% of the time
where the time goes in v5:
time: 130 us; the launch traced here: 129 us
  starting transfers between devices  58.3 us (45%)
  Pallas kernels  45.5 us (35%)
  waiting for transfers between devices  22.9 us (18%)
    pallas_call x22, Pallas kernels, placed(): return run(*map(place, args, in_specs))  45.5 us
    ppermute x20, starting transfers between devices, neighbours(): return (lax.ppermute(high, axis, up), lax.ppermute(low, axis, down))  33 us
    ppermute x12, starting transfers between devices, shifted(): return lax.ppermute(x, 'gz', [(i, (i + step) % 8) for i in range(8)])  25.4 us
    ppermute x12, waiting for transfers between devices, shifted(): return lax.ppermute(x, 'gz', [(i, (i + step) % 8) for i in range(8)])  16.4 us
    ppermute x20, waiting for transfers between devices, neighbours(): return (lax.ppermute(high, axis, up), lax.ppermute(low, axis, down))  6.52 us
  transfers between devices with their start and end apart: 32, of which 16 were waited for; matrix products, arithmetic and copies ran while one was open for 0% of the time, Pallas kernels for 26%

profile of v5, /device:TPU:7, one launch (start us, length us, event | category | flops | bytes accessed | tf_op | source)
XLA Modules:
  0.0 129.4 jit_solution(2567551074328545112)
XLA Ops:
  0.7 0.7 copy-done.2
  1.3 1.9 %shard_map.70 = (f32[224,128]{1,0:T(8,128)S(1)}, f32[336,128]{1,0:T(8,128)S(1)}, f32[336,128]{1,0:T(8,128)S(1)}, f32[224,128]{1,0:T(8,128)S(1)}, f32[224,128]{1,...) custom-call(s32[1]{0:T(128)} %bitcast.8.me_ref, s32[8]{0:T(128)S(1)} %copy-done.2, f32[1792,128]{1,0:T(8,128)} %bitcast.85), custom_call_target="tpu_custom_call" | custom-call | flops 1 | bytes 2000000 | tf_op jit(solution)/shard_map/pallas_call | solution.py:81
  3.2 1.7 %collective-permute-start.2 = (f32[336,128]{1,0:T(8,128)S(1)}, f32[336,128]{1,0:T(8,128)S(1)}, u32[]{:S(2)}, u32[]{:S(2)}) collective-permute-start(f32[336,128]{1,0:T(8,128)S(1)} %get-tuple-element.96), channel_id=1, source_target_pairs={{0,1},{1,2},{2,3},{3,4},{4,5},{5,6},{6,7},{7,0},{8,9},{9,10},{10,1... | collective-permute-start | bytes 516104 | tf_op jit(solution)/shard_map/ppermute | solution.py:948
  5.0 4.0 %collective-permute-start.3 = (f32[336,128]{1,0:T(8,128)S(1)}, f32[336,128]{1,0:T(8,128)S(1)}, u32[]{:S(2)}, u32[]{:S(2)}) collective-permute-start(f32[336,128]{1,0:T(8,128)S(1)} %get-tuple-element.97), channel_id=1, source_target_pairs={{0,7},{1,0},{2,1},{3,2},{4,3},{5,4},{6,5},{7,6},{8,15},{9,8},{10,9... | collective-permute-start | bytes 516104 | tf_op jit(solution)/shard_map/ppermute | solution.py:948
  9.0 3.8 %shard_map.68 = (f32[320,128]{1,0:T(8,128)S(1)}, f32[320,128]{1,0:T(8,128)S(1)}) custom-call(f32[19,256,128]{2,1,0:T(8,128)} %bitcast.82, s32[256,128]{1,0:T(8,128)} %bitcast.76), custom_call_target="tpu_custom_call" | custom-call | flops 1000000 | bytes 13000000 | tf_op jit(solution)/shard_map/pallas_call | solution.py:81
  12.8 2.8 %collective-permute-start = (f32[320,128]{1,0:T(8,128)S(1)}, f32[320,128]{1,0:T(8,128)S(1)}, u32[]{:S(2)}, u32[]{:S(2)}) collective-permute-start(f32[320,128]{1,0:T(8,128)S(1)} %get-tuple-element.91), channel_id=1, source_target_pairs={{0,192},{64,0},{128,64},{192,128},{1,193},{65,1},{129,65},{193,129... | collective-permute-start | bytes 491528 | tf_op jit(solution)/shard_map/ppermute | solution.py:943
  15.6 1.6 %collective-permute-start.6 = (f32[336,128]{1,0:T(8,128)S(1)}, f32[336,128]{1,0:T(8,128)S(1)}, u32[]{:S(2)}, u32[]{:S(2)}) collective-permute-start(f32[336,128]{1,0:T(8,128)S(1)} %pad_maximum_fusion), channel_id=1, source_target_pairs={{0,3},{1,4},{2,5},{3,6},{4,7},{5,0},{6,1},{7,2},{8,11},{9,12},{10,... | collective-permute-start | bytes 516104 | tf_op jit(solution)/shard_map/ppermute | solution.py:948
  17.3 3.0 %collective-permute-start.7 = (f32[336,128]{1,0:T(8,128)S(1)}, f32[336,128]{1,0:T(8,128)S(1)}, u32[]{:S(2)}, u32[]{:S(2)}) collective-permute-start(f32[336,128]{1,0:T(8,128)S(1)} %pad_maximum_fusion.1), channel_id=1, source_target_pairs={{0,5},{1,6},{2,7},{3,0},{4,1},{5,2},{6,3},{7,4},{8,13},{9,14},{10,... | collective-permute-start | bytes 516104 | tf_op jit(solution)/shard_map/ppermute | solution.py:948
  20.3 3.6 %collective-permute-start.5 = (f32[224,128]{1,0:T(8,128)S(1)}, f32[224,128]{1,0:T(8,128)S(1)}, u32[]{:S(2)}, u32[]{:S(2)}) collective-permute-start(f32[224,128]{1,0:T(8,128)S(1)} %get-tuple-element.99), channel_id=1, source_target_pairs={{0,6},{1,7},{2,0},{3,1},{4,2},{5,3},{6,4},{7,5},{8,14},{9,15},{10,... | collective-permute-start | bytes 344072 | tf_op jit(solution)/shard_map/ppermute | solution.py:948
  24.0 2.0 %collective-permute-done.1.left_ref = f32[320,128]{1,0:T(8,128)S(1)} collective-permute-done((f32[320,128]{1,0:T(8,128)S(1)}, f32[320,128]{1,0:T(8,128)S(1)}, u32[]{:S(2)}, u32[]{:S(2)}) %collective-permute-start.1) | collective-permute-done | bytes 163872 | tf_op jit(solution)/shard_map/ppermute | solution.py:943
  26.0 4.8 %shard_map.69 = (f32[19,256,128]{2,1,0:T(8,128)S(1)}, f32[19,256,128]{2,1,0:T(8,128)S(1)}, f32[512,128]{1,0:T(8,128)S(1)}, f32[4,512,128]{2,1,0:T(8,128)S(1)}, f...) custom-call(f32[6]{0:T(128)S(1)} %convert_element_type.3.flag_ref, f32[19,256,128]{2,1,0:T(8,128)} %bitcast.83, ...), custom_call_target="tpu_custom_call" | custom-call | flops 1000000 | bytes 20000000 | tf_op jit(solution)/shard_map/pallas_call | solution.py:81
  30.7 0.4 collective-permute-done.4.refs_3_
  31.1 2.0 %collective-permute-done.5.refs_4_ = f32[224,128]{1,0:T(8,128)S(1)} collective-permute-done((f32[224,128]{1,0:T(8,128)S(1)}, f32[224,128]{1,0:T(8,128)S(1)}, u32[]{:S(2)}, u32[]{:S(2)}) %collective-permute-start.5) | collective-permute-done | bytes 114720 | tf_op jit(solution)/shard_map/ppermute | solution.py:948
  33.1 0.9 shard_map.72
  34.0 2.5 %collective-permute-start.8 = (f32[112,128]{1,0:T(8,128)S(1)}, f32[112,128]{1,0:T(8,128)S(1)}, u32[]{:S(2)}, u32[]{:S(2)}) collective-permute-start(f32[112,128]{1,0:T(8,128)S(1)} %get-tuple-element.103), channel_id=1, source_target_pairs={{0,192},{64,0},{128,64},{192,128},{1,193},{65,1},{129,65},{193,129... | collective-permute-start | bytes 172040 | tf_op jit(solution)/shard_map/ppermute | solution.py:943
  36.5 2.2 %shard_map.71.dense_ref = f32[1792,128]{1,0:T(8,128)S(1)} custom-call(s32[1]{0:T(128)} %bitcast.8.me_ref, s32[1,1,8]{2,1,0:T(1,128)S(1)} %copy-done.1, f32[224,128]{1,0:T(8,128)S(1)} %get-tuple-element.95.refs_0_, f32[336,128]{1,0:T(8,128)S(1)} %collective-permute-done.2.refs_1_, f32[336,128]{1,0:T(8,128)S(1)} %collective-permute-done.3.refs_2_, ...), custom_call_target="tpu_custom_call" | custom-call | flops 1000000 | bytes 10000000 | tf_op jit(solution)/shard_map/pallas_call | solution.py:81
  38.7 2.0 %collective-permute-done.9.left_ref = f32[112,128]{1,0:T(8,128)S(1)} collective-permute-done((f32[112,128]{1,0:T(8,128)S(1)}, f32[112,128]{1,0:T(8,128)S(1)}, u32[]{:S(2)}, u32[]{:S(2)}) %collective-permute-start.9) | collective-permute-done | bytes 57376 | tf_op jit(solution)/shard_map/ppermute | solution.py:943
  40.8 1.5 %shard_map.73 = (f32[7,512,128]{2,1,0:T(8,128)S(1)}, f32[224,128]{1,0:T(8,128)S(1)}, f32[224,128]{1,0:T(8,128)S(1)}) custom-call(f32[1792,128]{1,0:T(8,128)S(1)} %shard_map.71.dense_ref, f32[112,128]{1,0:T(8,128)S(1)} %collective-permute-done.8.right_ref, f32[112,128]{1,0:T(8,128)S(1)} %collective-permute-done.9.left_ref, ...), custom_call_target="tpu_custom_call" | custom-call | flops 10000000 | bytes 10000000 | tf_op jit(solution)/shard_map/pallas_call | solution.py:81
  42.3 2.9 %collective-permute-start.11 = (f32[224,128]{1,0:T(8,128)S(1)}, f32[224,128]{1,0:T(8,128)S(1)}, u32[]{:S(2)}, u32[]{:S(2)}) collective-permute-start(f32[224,128]{1,0:T(8,128)S(1)} %get-tuple-element.111), channel_id=1, source_target_pairs={{0,56},{8,0},{16,8},{24,16},{32,24},{40,32},{48,40},{56,48},{1,57}... | collective-permute-start | bytes 344072 | tf_op jit(solution)/shard_map/ppermute | solution.py:943
  45.3 2.2 %shard_map.74 = (f32[224,128]{1,0:T(8,128)S(1)}, f32[224,128]{1,0:T(8,128)S(1)}, f32[19,1152,128]{2,1,0:T(8,128)S(1)}, f32[7,512,128]{2,1,0:T(8,128)S(1)}) custom-call(f32[19,256,128]{2,1,0:T(8,128)S(1)} %get-tuple-element.93.pops_ref.refs_0_, f32[19,256,128]{2,1,0:T(8,128)S(1)} %get-tuple-element.94.side_ref.refs_1_, ...), custom_call_target="tpu_custom_call" | custom-call | flops 10000000 | bytes 10000000 | tf_op jit(solution)/shard_map/pallas_call | solution.py:81
  47.6 0.2 collective-permute-done.11.yhi_ref.refs_9_
  47.9 4.4 %collective-permute-start.12 = (f32[256,128]{1,0:T(8,128)S(1)}, f32[256,128]{1,0:T(8,128)S(1)}, u32[]{:S(2)}, u32[]{:S(2)}) collective-permute-start(f32[256,128]{1,0:T(8,128)S(1)} %get-tuple-element.203), channel_id=1, source_target_pairs={{0,1},{1,2},{2,3},{3,4},{4,5},{5,6},{6,7},{7,0},{8,9},{9,10},{10,1... | collective-permute-start | bytes 393224 | tf_op jit(solution)/shard_map/ppermute | solution.py:943
  52.3 0.3 collective-permute-start.13
  52.6 0.7 shard_map.75
  53.3 2.7 %shard_map.76 = (f32[19,256,128]{2,1,0:T(8,128)S(1)}, f32[19,256,128]{2,1,0:T(8,128)S(1)}, f32[7,512,128]{2,1,0:T(8,128)S(1)}, f32[4,512,128]{2,1,0:T(8,128)S(1)...) custom-call(f32[19,256,128]{2,1,0:T(8,128)S(1)} %get-tuple-element.9, ...), custom_call_target="tpu_custom_call", output_to_operand_aliasing={{0}: (0, {}), {1}: (1, {}), {2}: (2, {}), {3}: (3, {}), {4}... | custom-call | flops 10000000 | bytes 10000000 | tf_op jit(solution)/shard_map/pallas_call | solution.py:81
  56.0 0.5 collective-permute-done.13.zhi_ref.refs_11_
  56.5 0.9 shard_map.77
  57.4 1.2 shard_map.78
  58.6 2.7 %collective-permute-start.15 = (f32[208,128]{1,0:T(8,128)S(1)}, f32[208,128]{1,0:T(8,128)S(1)}, u32[]{:S(2)}, u32[]{:S(2)}) collective-permute-start(f32[208,128]{1,0:T(8,128)S(1)} %get-tuple-element.133), channel_id=1, source_target_pairs={{0,56},{8,0},{16,8},{24,16},{32,24},{40,32},{48,40},{56,48},{1,57}... | collective-permute-start | bytes 319496 | tf_op jit(solution)/shard_map/ppermute | solution.py:943
  61.4 1.3 %collective-permute-start.14 = (f32[208,128]{1,0:T(8,128)S(1)}, f32[208,128]{1,0:T(8,128)S(1)}, u32[]{:S(2)}, u32[]{:S(2)}) collective-permute-start(f32[208,128]{1,0:T(8,128)S(1)} %get-tuple-element.132), channel_id=1, source_target_pairs={{0,8},{8,16},{16,24},{24,32},{32,40},{40,48},{48,56},{56,0},{1,9},... | collective-permute-start | bytes 319496 | tf_op jit(solution)/shard_map/ppermute | solution.py:943
  62.8 2.2 %shard_map.79 = (f32[208,128]{1,0:T(8,128)S(1)}, f32[208,128]{1,0:T(8,128)S(1)}, f32[19,1152,128]{2,1,0:T(8,128)S(1)}, f32[7,512,128]{2,1,0:T(8,128)S(1)}) custom-call(f32[19,256,128]{2,1,0:T(8,128)S(1)} %get-tuple-element.126.refs_0_, f32[19,256,128]{2,1,0:T(8,128)S(1)} %get-tuple-element.127.refs_1_, f32[7,512,128]{2,1,0:T(8,128)S(1)} %get-tuple-element.128.refs_2_, ...), custom_call_target="tpu_custom_call" | custom-call | flops 10000000 | bytes 10000000 | tf_op jit(solution)/shard_map/pallas_call | solution.py:81
  65.2 1.7 %collective-permute-start.16 = (f32[240,128]{1,0:T(8,128)S(1)}, f32[240,128]{1,0:T(8,128)S(1)}, u32[]{:S(2)}, u32[]{:S(2)}) collective-permute-start(f32[240,128]{1,0:T(8,128)S(1)} %get-tuple-element.201), channel_id=1, source_target_pairs={{0,1},{1,2},{2,3},{3,4},{4,5},{5,6},{6,7},{7,0},{8,9},{9,10},{10,1... | collective-permute-start | bytes 368648 | tf_op jit(solution)/shard_map/ppermute | solution.py:943
  67.0 1.0 collective-permute-start.17
  68.0 2.7 %shard_map.80 = (f32[19,256,128]{2,1,0:T(8,128)S(1)}, f32[19,256,128]{2,1,0:T(8,128)S(1)}, f32[7,512,128]{2,1,0:T(8,128)S(1)}, f32[4,512,128]{2,1,0:T(8,128)S(1)...) custom-call(f32[19,256,128]{2,1,0:T(8,128)S(1)} %get-tuple-element.1, ...), custom_call_target="tpu_custom_call", output_to_operand_aliasing={{0}: (0, {}), {1}: (1, {}), {2}: (2, {}), {3}: (3, {}), {4}... | custom-call | flops 10000000 | bytes 10000000 | tf_op jit(solution)/shard_map/pallas_call | solution.py:81
  70.7 0.2 collective-permute-done.16.refs_10_
  71.0 1.2 shard_map.81
  72.3 1.7 %collective-permute-start.19 = (f32[208,128]{1,0:T(8,128)S(1)}, f32[208,128]{1,0:T(8,128)S(1)}, u32[]{:S(2)}, u32[]{:S(2)}) collective-permute-start(f32[208,128]{1,0:T(8,128)S(1)} %get-tuple-element.149), channel_id=1, source_target_pairs={{0,56},{8,0},{16,8},{24,16},{32,24},{40,32},{48,40},{56,48},{1,57}... | collective-permute-start | bytes 319496 | tf_op jit(solution)/shard_map/ppermute | solution.py:943
  74.0 2.5 %collective-permute-start.18 = (f32[208,128]{1,0:T(8,128)S(1)}, f32[208,128]{1,0:T(8,128)S(1)}, u32[]{:S(2)}, u32[]{:S(2)}) collective-permute-start(f32[208,128]{1,0:T(8,128)S(1)} %get-tuple-element.148), channel_id=1, source_target_pairs={{0,8},{8,16},{16,24},{24,32},{32,40},{40,48},{48,56},{56,0},{1,9},... | collective-permute-start | bytes 319496 | tf_op jit(solution)/shard_map/ppermute | solution.py:943
  76.4 2.2 %shard_map.82 = (f32[208,128]{1,0:T(8,128)S(1)}, f32[208,128]{1,0:T(8,128)S(1)}, f32[19,1152,128]{2,1,0:T(8,128)S(1)}, f32[7,512,128]{2,1,0:T(8,128)S(1)}) custom-call(f32[19,256,128]{2,1,0:T(8,128)S(1)} %get-tuple-element.142.refs_0_, f32[19,256,128]{2,1,0:T(8,128)S(1)} %get-tuple-element.143.refs_1_, f32[7,512,128]{2,1,0:T(8,128)S(1)} %get-tuple-element.144.refs_2_, ...), custom_call_target="tpu_custom_call" | custom-call | flops 10000000 | bytes 10000000 | tf_op jit(solution)/shard_map/pallas_call | solution.py:81
  78.6 0.2 collective-permute-done.19.refs_9_
  79.0 0.3 collective-permute-start.20
  79.3 2.5 %collective-permute-start.21 = (f32[240,128]{1,0:T(8,128)S(1)}, f32[240,128]{1,0:T(8,128)S(1)}, u32[]{:S(2)}, u32[]{:S(2)}) collective-permute-start(f32[240,128]{1,0:T(8,128)S(1)} %get-tuple-element.198), channel_id=1, source_target_pairs={{0,7},{1,0},{2,1},{3,2},{4,3},{5,4},{6,5},{7,6},{8,15},{9,8},{10,9... | collective-permute-start | bytes 368648 | tf_op jit(solution)/shard_map/ppermute | solution.py:943
  81.7 2.7 %shard_map.83 = (f32[19,256,128]{2,1,0:T(8,128)S(1)}, f32[19,256,128]{2,1,0:T(8,128)S(1)}, f32[7,512,128]{2,1,0:T(8,128)S(1)}, f32[4,512,128]{2,1,0:T(8,128)S(1)...) custom-call(f32[19,256,128]{2,1,0:T(8,128)S(1)} %get-tuple-element.1, ...), custom_call_target="tpu_custom_call", output_to_operand_aliasing={{0}: (0, {}), {1}: (1, {}), {2}: (2, {}), {3}: (3, {}), {4}... | custom-call | flops 10000000 | bytes 10000000 | tf_op jit(solution)/shard_map/pallas_call | solution.py:81
  84.4 0.7 collective-permute-done.20.refs_10_
  85.1 1.2 shard_map.84
  86.3 0.4 collective-permute-start.23
  86.7 2.6 %collective-permute-start.22 = (f32[208,128]{1,0:T(8,128)S(1)}, f32[208,128]{1,0:T(8,128)S(1)}, u32[]{:S(2)}, u32[]{:S(2)}) collective-permute-start(f32[208,128]{1,0:T(8,128)S(1)} %get-tuple-element.164), channel_id=1, source_target_pairs={{0,8},{8,16},{16,24},{24,32},{32,40},{40,48},{48,56},{56,0},{1,9},... | collective-permute-start | bytes 319496 | tf_op jit(solution)/shard_map/ppermute | solution.py:943
  89.3 2.1 %shard_map.85 = (f32[208,128]{1,0:T(8,128)S(1)}, f32[208,128]{1,0:T(8,128)S(1)}, f32[19,1152,128]{2,1,0:T(8,128)S(1)}, f32[7,512,128]{2,1,0:T(8,128)S(1)}) custom-call(f32[19,256,128]{2,1,0:T(8,128)S(1)} %get-tuple-element.158.refs_0_, f32[19,256,128]{2,1,0:T(8,128)S(1)} %get-tuple-element.159.refs_1_, f32[7,512,128]{2,1,0:T(8,128)S(1)} %get-tuple-element.160.refs_2_, ...), custom_call_target="tpu_custom_call" | custom-call | flops 10000000 | bytes 10000000 | tf_op jit(solution)/shard_map/pallas_call | solution.py:81
  91.5 0.2 collective-permute-done.23.refs_9_.refs_5_
  91.9 0.7 collective-permute-start.24
  92.6 2.6 %collective-permute-start.25 = (f32[240,128]{1,0:T(8,128)S(1)}, f32[240,128]{1,0:T(8,128)S(1)}, u32[]{:S(2)}, u32[]{:S(2)}) collective-permute-start(f32[240,128]{1,0:T(8,128)S(1)} %get-tuple-element.196), channel_id=1, source_target_pairs={{0,7},{1,0},{2,1},{3,2},{4,3},{5,4},{6,5},{7,6},{8,15},{9,8},{10,9... | collective-permute-start | bytes 368648 | tf_op jit(solution)/shard_map/ppermute | solution.py:943
  95.2 2.6 %shard_map.86 = (f32[19,1152,128]{2,1,0:T(8,128)S(1)}, f32[7,512,128]{2,1,0:T(8,128)S(1)}, f32[1792,128]{1,0:T(8,128)S(1)}) custom-call(f32[19,256,128]{2,1,0:T(8,128)S(1)} %get-tuple-element.158.refs_0_, f32[19,256,128]{2,1,0:T(8,128)S(1)} %get-tuple-element.159.refs_1_, ...), custom_call_target="tpu_custom_call", output_to_operand_aliasing={{0}: (4, {}), {1}: (5, {})} | custom-call | flops 10000000 | bytes 10000000 | tf_op jit(solution)/shard_map/pallas_call | solution.py:81
  97.8 0.2 collective-permute-done.24.refs_6_.refs_10_
  98.1 1.0 shard_map.87
  99.1 1.3 collective-permute-start.26
  100.3 1.9 %collective-permute-start.27 = (f32[336,128]{1,0:T(8,128)S(1)}, f32[336,128]{1,0:T(8,128)S(1)}, u32[]{:S(2)}, u32[]{:S(2)}) collective-permute-start(f32[336,128]{1,0:T(8,128)S(1)} %get-tuple-element.175), channel_id=1, source_target_pairs={{0,7},{1,0},{2,1},{3,2},{4,3},{5,4},{6,5},{7,6},{8,15},{9,8},{10,9... | collective-permute-start | bytes 516104 | tf_op jit(solution)/shard_map/ppermute | solution.py:948
  102.3 4.4 %collective-permute-done.26.refs_1_ = f32[336,128]{1,0:T(8,128)S(1)} collective-permute-done((f32[336,128]{1,0:T(8,128)S(1)}, f32[336,128]{1,0:T(8,128)S(1)}, u32[]{:S(2)}, u32[]{:S(2)}) %collective-permute-start.26) | collective-permute-done | bytes 172064 | tf_op jit(solution)/shard_map/ppermute | solution.py:948
  106.7 0.6 collective-permute-start.30
  107.3 4.0 %collective-permute-start.31 = (f32[336,128]{1,0:T(8,128)S(1)}, f32[336,128]{1,0:T(8,128)S(1)}, u32[]{:S(2)}, u32[]{:S(2)}) collective-permute-start(f32[336,128]{1,0:T(8,128)S(1)} %pad_maximum_fusion.3), channel_id=1, source_target_pairs={{0,5},{1,6},{2,7},{3,0},{4,1},{5,2},{6,3},{7,4},{8,13},{9,14},{10,... | collective-permute-start | bytes 516104 | tf_op jit(solution)/shard_map/ppermute | solution.py:948
  111.3 3.6 %collective-permute-start.29 = (f32[224,128]{1,0:T(8,128)S(1)}, f32[224,128]{1,0:T(8,128)S(1)}, u32[]{:S(2)}, u32[]{:S(2)}) collective-permute-start(f32[224,128]{1,0:T(8,128)S(1)} %get-tuple-element.177), channel_id=1, source_target_pairs={{0,6},{1,7},{2,0},{3,1},{4,2},{5,3},{6,4},{7,5},{8,14},{9,15},{10,... | collective-permute-start | bytes 344072 | tf_op jit(solution)/shard_map/ppermute | solution.py:948
  114.9 3.1 %shard_map.88 = (f32[19,256,128]{2,1,0:T(8,128)}, f32[19,1152,128]{2,1,0:T(8,128)S(1)}) custom-call(f32[19,256,128]{2,1,0:T(8,128)S(1)} %get-tuple-element.158.refs_0_, f32[19,256,128]{2,1,0:T(8,128)S(1)} %get-tuple-element.159.refs_1_, f32[7,512,128]{2,1,0:T(8,128)S(1)} %get-tuple-element.160.refs_2_, ...), custom_call_target="tpu_custom_call", output_to_operand_aliasing={{1}: (4, {})} | custom-call | flops 10000000 | bytes 10000000 | tf_op jit(solution)/shard_map/pallas_call | solution.py:81
  118.0 6.2 %collective-permute-done.28.refs_3_ = f32[224,128]{1,0:T(8,128)S(1)} collective-permute-done((f32[224,128]{1,0:T(8,128)S(1)}, f32[224,128]{1,0:T(8,128)S(1)}, u32[]{:S(2)}, u32[]{:S(2)}) %collective-permute-start.28) | collective-permute-done | bytes 114720 | tf_op jit(solution)/shard_map/ppermute | solution.py:948
  124.1 3.5 %collective-permute-done.29.refs_4_ = f32[224,128]{1,0:T(8,128)S(1)} collective-permute-done((f32[224,128]{1,0:T(8,128)S(1)}, f32[224,128]{1,0:T(8,128)S(1)}, u32[]{:S(2)}, u32[]{:S(2)}) %collective-permute-start.29) | collective-permute-done | bytes 114720 | tf_op jit(solution)/shard_map/ppermute | solution.py:948
  127.6 1.8 %shard_map.89 = f32[1792,128]{1,0:T(8,128)} custom-call(s32[1]{0:T(128)} %bitcast.8.me_ref, s32[8]{0:T(128)S(1)} %copy-done.3, f32[224,128]{1,0:T(8,128)S(1)} %get-tuple-element.173.refs_0_, f32[336,128]{1,0:T(8,128)S(1)} %collective-permute-done.26.refs_1_, f32[336,128]{1,0:T(8,128)S(1)} %collective-permute-done.27.refs_2_, ...), custom_call_target="tpu_custom_call" | custom-call | flops 1 | bytes 2000000 | tf_op jit(solution)/shard_map/pallas_call | solution.py:81
  (70 shorter events, 1.3 us)
Async XLA Ops:
  0.6 25.3 %copy-start = (s32[16,16,128]{2,1,0:T(8,128)S(1)}, s32[16,16,128]{2,1,0:T(8,128)}, u32[]{:S(2)}) copy-start(s32[16,16,128]{2,1,0:T(8,128)} %param.7) | copy-start | bytes 393220
  0.6 0.7 copy-start.2
  3.2 12.3 %collective-permute-start.2 = (f32[336,128]{1,0:T(8,128)S(1)}, f32[336,128]{1,0:T(8,128)S(1)}, u32[]{:S(2)}, u32[]{:S(2)}) collective-permute-start(f32[336,128]{1,0:T(8,128)S(1)} %get-tuple-element.96), channel_id=1, source_target_pairs={{0,1},{1,2},{2,3},{3,4},{4,5},{5,6},{6,7},{7,0},{8,9},{9,10},{10,1... | collective-permute-start | bytes 516104 | tf_op jit(solution)/shard_map/ppermute | solution.py:948
  5.0 12.3 %collective-permute-start.3 = (f32[336,128]{1,0:T(8,128)S(1)}, f32[336,128]{1,0:T(8,128)S(1)}, u32[]{:S(2)}, u32[]{:S(2)}) collective-permute-start(f32[336,128]{1,0:T(8,128)S(1)} %get-tuple-element.97), channel_id=1, source_target_pairs={{0,7},{1,0},{2,1},{3,2},{4,3},{5,4},{6,5},{7,6},{8,15},{9,8},{10,9... | collective-permute-start | bytes 516104 | tf_op jit(solution)/shard_map/ppermute | solution.py:948
  12.8 20.3 %copy-start.1 = (s32[1,1,8]{2,1,0:T(1,128)S(1)}, s32[1,1,8]{2,1,0:T(1,128)}, u32[]{:S(2)}) copy-start(s32[1,1,8]{2,1,0:T(1,128)} %slot_ref.8) | copy-start | bytes 100
  12.8 7.5 %collective-permute-start = (f32[320,128]{1,0:T(8,128)S(1)}, f32[320,128]{1,0:T(8,128)S(1)}, u32[]{:S(2)}, u32[]{:S(2)}) collective-permute-start(f32[320,128]{1,0:T(8,128)S(1)} %get-tuple-element.91), channel_id=1, source_target_pairs={{0,192},{64,0},{128,64},{192,128},{1,193},{65,1},{129,65},{193,129... | collective-permute-start | bytes 491528 | tf_op jit(solution)/shard_map/ppermute | solution.py:943
  15.6 17.5 %collective-permute-start.6 = (f32[336,128]{1,0:T(8,128)S(1)}, f32[336,128]{1,0:T(8,128)S(1)}, u32[]{:S(2)}, u32[]{:S(2)}) collective-permute-start(f32[336,128]{1,0:T(8,128)S(1)} %pad_maximum_fusion), channel_id=1, source_target_pairs={{0,3},{1,4},{2,5},{3,6},{4,7},{5,0},{6,1},{7,2},{8,11},{9,12},{10,... | collective-permute-start | bytes 516104 | tf_op jit(solution)/shard_map/ppermute | solution.py:948
  17.3 15.8 %collective-permute-start.7 = (f32[336,128]{1,0:T(8,128)S(1)}, f32[336,128]{1,0:T(8,128)S(1)}, u32[]{:S(2)}, u32[]{:S(2)}) collective-permute-start(f32[336,128]{1,0:T(8,128)S(1)} %pad_maximum_fusion.1), channel_id=1, source_target_pairs={{0,5},{1,6},{2,7},{3,0},{4,1},{5,2},{6,3},{7,4},{8,13},{9,14},{10,... | collective-permute-start | bytes 516104 | tf_op jit(solution)/shard_map/ppermute | solution.py:948
  20.3 5.7 %collective-permute-start.1 = (f32[320,128]{1,0:T(8,128)S(1)}, f32[320,128]{1,0:T(8,128)S(1)}, u32[]{:S(2)}, u32[]{:S(2)}) collective-permute-start(f32[320,128]{1,0:T(8,128)S(1)} %get-tuple-element.92), channel_id=1, source_target_pairs={{0,64},{64,128},{128,192},{192,0},{1,65},{65,129},{129,193},{193,1... | collective-permute-start | bytes 491528 | tf_op jit(solution)/shard_map/ppermute | solution.py:943
  20.3 10.8 %collective-permute-start.4 = (f32[224,128]{1,0:T(8,128)S(1)}, f32[224,128]{1,0:T(8,128)S(1)}, u32[]{:S(2)}, u32[]{:S(2)}) collective-permute-start(f32[224,128]{1,0:T(8,128)S(1)} %get-tuple-element.98), channel_id=1, source_target_pairs={{0,2},{1,3},{2,4},{3,5},{4,6},{5,7},{6,0},{7,1},{8,10},{9,11},{10,... | collective-permute-start | bytes 344072 | tf_op jit(solution)/shard_map/ppermute | solution.py:948
  20.3 12.8 %collective-permute-start.5 = (f32[224,128]{1,0:T(8,128)S(1)}, f32[224,128]{1,0:T(8,128)S(1)}, u32[]{:S(2)}, u32[]{:S(2)}) collective-permute-start(f32[224,128]{1,0:T(8,128)S(1)} %get-tuple-element.99), channel_id=1, source_target_pairs={{0,6},{1,7},{2,0},{3,1},{4,2},{5,3},{6,4},{7,5},{8,14},{9,15},{10,... | collective-permute-start | bytes 344072 | tf_op jit(solution)/shard_map/ppermute | solution.py:948
  34.0 4.8 %collective-permute-start.8 = (f32[112,128]{1,0:T(8,128)S(1)}, f32[112,128]{1,0:T(8,128)S(1)}, u32[]{:S(2)}, u32[]{:S(2)}) collective-permute-start(f32[112,128]{1,0:T(8,128)S(1)} %get-tuple-element.103), channel_id=1, source_target_pairs={{0,192},{64,0},{128,64},{192,128},{1,193},{65,1},{129,65},{193,129... | collective-permute-start | bytes 172040 | tf_op jit(solution)/shard_map/ppermute | solution.py:943
  36.5 4.2 %collective-permute-start.9 = (f32[112,128]{1,0:T(8,128)S(1)}, f32[112,128]{1,0:T(8,128)S(1)}, u32[]{:S(2)}, u32[]{:S(2)}) collective-permute-start(f32[112,128]{1,0:T(8,128)S(1)} %get-tuple-element.104), channel_id=1, source_target_pairs={{0,64},{64,128},{128,192},{192,0},{1,65},{65,129},{129,193},{193,1... | collective-permute-start | bytes 172040 | tf_op jit(solution)/shard_map/ppermute | solution.py:943
  42.3 5.4 %collective-permute-start.11 = (f32[224,128]{1,0:T(8,128)S(1)}, f32[224,128]{1,0:T(8,128)S(1)}, u32[]{:S(2)}, u32[]{:S(2)}) collective-permute-start(f32[224,128]{1,0:T(8,128)S(1)} %get-tuple-element.111), channel_id=1, source_target_pairs={{0,56},{8,0},{16,8},{24,16},{32,24},{40,32},{48,40},{56,48},{1,57}... | collective-permute-start | bytes 344072 | tf_op jit(solution)/shard_map/ppermute | solution.py:943
  45.2 2.5 %collective-permute-start.10 = (f32[224,128]{1,0:T(8,128)S(1)}, f32[224,128]{1,0:T(8,128)S(1)}, u32[]{:S(2)}, u32[]{:S(2)}) collective-permute-start(f32[224,128]{1,0:T(8,128)S(1)} %get-tuple-element.110), channel_id=1, source_target_pairs={{0,8},{8,16},{16,24},{24,32},{32,40},{40,48},{48,56},{56,0},{1,9},... | collective-permute-start | bytes 344072 | tf_op jit(solution)/shard_map/ppermute | solution.py:943
  47.9 8.1 %collective-permute-start.12 = (f32[256,128]{1,0:T(8,128)S(1)}, f32[256,128]{1,0:T(8,128)S(1)}, u32[]{:S(2)}, u32[]{:S(2)}) collective-permute-start(f32[256,128]{1,0:T(8,128)S(1)} %get-tuple-element.203), channel_id=1, source_target_pairs={{0,1},{1,2},{2,3},{3,4},{4,5},{5,6},{6,7},{7,0},{8,9},{9,10},{10,1... | collective-permute-start | bytes 393224 | tf_op jit(solution)/shard_map/ppermute | solution.py:943
  52.3 4.3 %collective-permute-start.13 = (f32[256,128]{1,0:T(8,128)S(1)}, f32[256,128]{1,0:T(8,128)S(1)}, u32[]{:S(2)}, u32[]{:S(2)}) collective-permute-start(f32[256,128]{1,0:T(8,128)S(1)} %get-tuple-element.202), channel_id=1, source_target_pairs={{0,7},{1,0},{2,1},{3,2},{4,3},{5,4},{6,5},{7,6},{8,15},{9,8},{10,9... | collective-permute-start | bytes 393224 | tf_op jit(solution)/shard_map/ppermute | solution.py:943
  58.6 6.4 %collective-permute-start.15 = (f32[208,128]{1,0:T(8,128)S(1)}, f32[208,128]{1,0:T(8,128)S(1)}, u32[]{:S(2)}, u32[]{:S(2)}) collective-permute-start(f32[208,128]{1,0:T(8,128)S(1)} %get-tuple-element.133), channel_id=1, source_target_pairs={{0,56},{8,0},{16,8},{24,16},{32,24},{40,32},{48,40},{56,48},{1,57}... | collective-permute-start | bytes 319496 | tf_op jit(solution)/shard_map/ppermute | solution.py:943
  61.4 3.6 %collective-permute-start.14 = (f32[208,128]{1,0:T(8,128)S(1)}, f32[208,128]{1,0:T(8,128)S(1)}, u32[]{:S(2)}, u32[]{:S(2)}) collective-permute-start(f32[208,128]{1,0:T(8,128)S(1)} %get-tuple-element.132), channel_id=1, source_target_pairs={{0,8},{8,16},{16,24},{24,32},{32,40},{40,48},{48,56},{56,0},{1,9},... | collective-permute-start | bytes 319496 | tf_op jit(solution)/shard_map/ppermute | solution.py:943
  65.2 5.7 %collective-permute-start.16 = (f32[240,128]{1,0:T(8,128)S(1)}, f32[240,128]{1,0:T(8,128)S(1)}, u32[]{:S(2)}, u32[]{:S(2)}) collective-permute-start(f32[240,128]{1,0:T(8,128)S(1)} %get-tuple-element.201), channel_id=1, source_target_pairs={{0,1},{1,2},{2,3},{3,4},{4,5},{5,6},{6,7},{7,0},{8,9},{9,10},{10,1... | collective-permute-start | bytes 368648 | tf_op jit(solution)/shard_map/ppermute | solution.py:943
  67.0 4.1 %collective-permute-start.17 = (f32[240,128]{1,0:T(8,128)S(1)}, f32[240,128]{1,0:T(8,128)S(1)}, u32[]{:S(2)}, u32[]{:S(2)}) collective-permute-start(f32[240,128]{1,0:T(8,128)S(1)} %get-tuple-element.200), channel_id=1, source_target_pairs={{0,7},{1,0},{2,1},{3,2},{4,3},{5,4},{6,5},{7,6},{8,15},{9,8},{10,9... | collective-permute-start | bytes 368648 | tf_op jit(solution)/shard_map/ppermute | solution.py:943
  72.3 6.5 %collective-permute-start.19 = (f32[208,128]{1,0:T(8,128)S(1)}, f32[208,128]{1,0:T(8,128)S(1)}, u32[]{:S(2)}, u32[]{:S(2)}) collective-permute-start(f32[208,128]{1,0:T(8,128)S(1)} %get-tuple-element.149), channel_id=1, source_target_pairs={{0,56},{8,0},{16,8},{24,16},{32,24},{40,32},{48,40},{56,48},{1,57}... | collective-permute-start | bytes 319496 | tf_op jit(solution)/shard_map/ppermute | solution.py:943
  74.0 4.8 %collective-permute-start.18 = (f32[208,128]{1,0:T(8,128)S(1)}, f32[208,128]{1,0:T(8,128)S(1)}, u32[]{:S(2)}, u32[]{:S(2)}) collective-permute-start(f32[208,128]{1,0:T(8,128)S(1)} %get-tuple-element.148), channel_id=1, source_target_pairs={{0,8},{8,16},{16,24},{24,32},{32,40},{40,48},{48,56},{56,0},{1,9},... | collective-permute-start | bytes 319496 | tf_op jit(solution)/shard_map/ppermute | solution.py:943
  79.0 6.1 %collective-permute-start.20 = (f32[240,128]{1,0:T(8,128)S(1)}, f32[240,128]{1,0:T(8,128)S(1)}, u32[]{:S(2)}, u32[]{:S(2)}) collective-permute-start(f32[240,128]{1,0:T(8,128)S(1)} %get-tuple-element.199), channel_id=1, source_target_pairs={{0,1},{1,2},{2,3},{3,4},{4,5},{5,6},{6,7},{7,0},{8,9},{9,10},{10,1... | collective-permute-start | bytes 368648 | tf_op jit(solution)/shard_map/ppermute | solution.py:943
  79.3 5.8 %collective-permute-start.21 = (f32[240,128]{1,0:T(8,128)S(1)}, f32[240,128]{1,0:T(8,128)S(1)}, u32[]{:S(2)}, u32[]{:S(2)}) collective-permute-start(f32[240,128]{1,0:T(8,128)S(1)} %get-tuple-element.198), channel_id=1, source_target_pairs={{0,7},{1,0},{2,1},{3,2},{4,3},{5,4},{6,5},{7,6},{8,15},{9,8},{10,9... | collective-permute-start | bytes 368648 | tf_op jit(solution)/shard_map/ppermute | solution.py:943
  86.3 5.4 %collective-permute-start.23 = (f32[208,128]{1,0:T(8,128)S(1)}, f32[208,128]{1,0:T(8,128)S(1)}, u32[]{:S(2)}, u32[]{:S(2)}) collective-permute-start(f32[208,128]{1,0:T(8,128)S(1)} %get-tuple-element.165), channel_id=1, source_target_pairs={{0,56},{8,0},{16,8},{24,16},{32,24},{40,32},{48,40},{56,48},{1,57}... | collective-permute-start | bytes 319496 | tf_op jit(solution)/shard_map/ppermute | solution.py:943
  86.7 5.0 %collective-permute-start.22 = (f32[208,128]{1,0:T(8,128)S(1)}, f32[208,128]{1,0:T(8,128)S(1)}, u32[]{:S(2)}, u32[]{:S(2)}) collective-permute-start(f32[208,128]{1,0:T(8,128)S(1)} %get-tuple-element.164), channel_id=1, source_target_pairs={{0,8},{8,16},{16,24},{24,32},{32,40},{40,48},{48,56},{56,0},{1,9},... | collective-permute-start | bytes 319496 | tf_op jit(solution)/shard_map/ppermute | solution.py:943
  91.9 6.2 %collective-permute-start.24 = (f32[240,128]{1,0:T(8,128)S(1)}, f32[240,128]{1,0:T(8,128)S(1)}, u32[]{:S(2)}, u32[]{:S(2)}) collective-permute-start(f32[240,128]{1,0:T(8,128)S(1)} %get-tuple-element.197), channel_id=1, source_target_pairs={{0,1},{1,2},{2,3},{3,4},{4,5},{5,6},{6,7},{7,0},{8,9},{9,10},{10,1... | collective-permute-start | bytes 368648 | tf_op jit(solution)/shard_map/ppermute | solution.py:943
  92.6 5.5 %collective-permute-start.25 = (f32[240,128]{1,0:T(8,128)S(1)}, f32[240,128]{1,0:T(8,128)S(1)}, u32[]{:S(2)}, u32[]{:S(2)}) collective-permute-start(f32[240,128]{1,0:T(8,128)S(1)} %get-tuple-element.196), channel_id=1, source_target_pairs={{0,7},{1,0},{2,1},{3,2},{4,3},{5,4},{6,5},{7,6},{8,15},{9,8},{10,9... | collective-permute-start | bytes 368648 | tf_op jit(solution)/shard_map/ppermute | solution.py:943
  99.1 7.6 %collective-permute-start.26 = (f32[336,128]{1,0:T(8,128)S(1)}, f32[336,128]{1,0:T(8,128)S(1)}, u32[]{:S(2)}, u32[]{:S(2)}) collective-permute-start(f32[336,128]{1,0:T(8,128)S(1)} %get-tuple-element.174), channel_id=1, source_target_pairs={{0,1},{1,2},{2,3},{3,4},{4,5},{5,6},{6,7},{7,0},{8,9},{9,10},{10,1... | collective-permute-start | bytes 516104 | tf_op jit(solution)/shard_map/ppermute | solution.py:948
  100.3 6.9 %collective-permute-start.27 = (f32[336,128]{1,0:T(8,128)S(1)}, f32[336,128]{1,0:T(8,128)S(1)}, u32[]{:S(2)}, u32[]{:S(2)}) collective-permute-start(f32[336,128]{1,0:T(8,128)S(1)} %get-tuple-element.175), channel_id=1, source_target_pairs={{0,7},{1,0},{2,1},{3,2},{4,3},{5,4},{6,5},{7,6},{8,15},{9,8},{10,9... | collective-permute-start | bytes 516104 | tf_op jit(solution)/shard_map/ppermute | solution.py:948
  106.7 21.0 %collective-permute-start.30 = (f32[336,128]{1,0:T(8,128)S(1)}, f32[336,128]{1,0:T(8,128)S(1)}, u32[]{:S(2)}, u32[]{:S(2)}) collective-permute-start(f32[336,128]{1,0:T(8,128)S(1)} %pad_maximum_fusion.2), channel_id=1, source_target_pairs={{0,3},{1,4},{2,5},{3,6},{4,7},{5,0},{6,1},{7,2},{8,11},{9,12},{10,... | collective-permute-start | bytes 516104 | tf_op jit(solution)/shard_map/ppermute | solution.py:948
  107.3 20.3 %collective-permute-start.31 = (f32[336,128]{1,0:T(8,128)S(1)}, f32[336,128]{1,0:T(8,128)S(1)}, u32[]{:S(2)}, u32[]{:S(2)}) collective-permute-start(f32[336,128]{1,0:T(8,128)S(1)} %pad_maximum_fusion.3), channel_id=1, source_target_pairs={{0,5},{1,6},{2,7},{3,0},{4,1},{5,2},{6,3},{7,4},{8,13},{9,14},{10,... | collective-permute-start | bytes 516104 | tf_op jit(solution)/shard_map/ppermute | solution.py:948
  111.3 12.8 %collective-permute-start.28 = (f32[224,128]{1,0:T(8,128)S(1)}, f32[224,128]{1,0:T(8,128)S(1)}, u32[]{:S(2)}, u32[]{:S(2)}) collective-permute-start(f32[224,128]{1,0:T(8,128)S(1)} %get-tuple-element.176), channel_id=1, source_target_pairs={{0,2},{1,3},{2,4},{3,5},{4,6},{5,7},{6,0},{7,1},{8,10},{9,11},{10,... | collective-permute-start | bytes 344072 | tf_op jit(solution)/shard_map/ppermute | solution.py:948
  111.3 16.3 %collective-permute-start.29 = (f32[224,128]{1,0:T(8,128)S(1)}, f32[224,128]{1,0:T(8,128)S(1)}, u32[]{:S(2)}, u32[]{:S(2)}) collective-permute-start(f32[224,128]{1,0:T(8,128)S(1)} %get-tuple-element.177), channel_id=1, source_target_pairs={{0,6},{1,7},{2,0},{3,1},{4,2},{5,3},{6,4},{7,5},{8,14},{9,15},{10,... | collective-permute-start | bytes 344072 | tf_op jit(solution)/shard_map/ppermute | solution.py:948
  114.9 12.7 %copy-start.3 = (s32[8]{0:T(128)S(1)}, s32[8]{0:T(128)}, u32[]{:S(2)}) copy-start(s32[8]{0:T(128)} %slot_ref.9) | copy-start | bytes 100
